TPU v7x, 32 devices: a whole 2x2x4 slice. The times are simulated.
32 devices in a mesh: groups: 2 (over x), pts: 16 (over z, y, core).
Axes of the slice: x: 2, y: 2, z: 4, core: 2. Of those that a mesh axis runs over, the one named last changes fastest.
Arguments:
- occupied_at_nodes: bfloat16 [12288, 4096], P(('groups', 'pts')), parts along dimension 0, may hold values from -0.75 to 0.75
- within_group_screening: bfloat16 [12288, 384], P(('groups', 'pts')), parts along dimension 0, may hold values from -1.1953125 to 1.1953125
- adjacent_group_screening: bfloat16 [12288, 2, 384], P(('groups', 'pts')), parts along dimension 0, may hold values from -1.1953125 to 1.1953125
- close_couple_indicator: int32 [32, 2], P(('groups', 'pts')), parts along dimension 0, may hold values 0 or 1
- group_node_tally: int32 [32], P(('groups', 'pts')), parts along dimension 0, may hold values from 192 to 384, as said below
Outputs:
- exchange_rows: bfloat16 [12288, 4096], P(('groups', 'pts')), parts along dimension 0
There are 2 independent parts, one for each index of `groups`. A program takes and returns all parts, laid end to end along the dimension named above; each array names one. Nothing has to cross between parts.
Inputs may be any that keep to these rules, and one draw needn't show every extreme that they name: `group_node_tally`: some block has all 384 points valid.
All inputs are finite; a program needn't handle non-finite values. No bound on the sum of `close_couple_indicator` on one device may be relied on, other than what follows from the above.
Results may differ from a plain program's by a relative error of at most 0.0051.
Values may be sent and summed in bfloat16 or wider, within the bound.
No kernel may reach another device: no remote copies, remote signals or barrier semaphores. Data moves between devices by JAX's collectives and lax.ppermute only.
A program may use at most 128 MiB of HBM per device.

v0:
```python
import jax
import jax.numpy as jnp
from jax import lax
from jax.sharding import PartitionSpec as P


def shifted(array, axis, by):
    peers = lax.axis_size(axis)
    pairs = [(i, i + by) for i in range(peers) if 0 <= i + by < peers]
    return lax.ppermute(array, axis, pairs)


def pair_weights(kernel, left, right, pair_flag):
    gram = lax.dot_general(
        left, right, (((1,), (1,)), ((), ())), preferred_element_type=jnp.float32
    )
    return (kernel.astype(jnp.float32) * gram * pair_flag).astype(jnp.bfloat16)


def transposed_product(weights, rows):
    return lax.dot_general(
        weights, rows, (((0,), (0,)), ((), ())), preferred_element_type=jnp.float32
    )


def on_device(
    occupied_at_nodes,
    within_group_screening,
    adjacent_group_screening,
    close_couple_indicator,
    group_node_tally,
):
    group_exchange_lines = occupied_at_nodes.shape[0]
    node_locations = lax.iota(jnp.int32, group_exchange_lines)
    usable_line_indicator = (node_locations < group_node_tally[0]).astype(occupied_at_nodes.dtype)
    within_group_lines = occupied_at_nodes * usable_line_indicator[:, None]
    unit_flag = jnp.float32(1.0)
    accumulated = jnp.dot(
        pair_weights(within_group_screening, within_group_lines, within_group_lines, unit_flag),
        within_group_lines,
        preferred_element_type=jnp.float32,
    )
    neighbours = adjacent_group_screening.shape[1]
    for offset in range(1, neighbours + 1):
        above_rows = shifted(within_group_lines, "pts", -offset)
        kernel = adjacent_group_screening[:, offset - 1, :]
        pair_flag = close_couple_indicator[0, offset - 1].astype(jnp.float32)
        weights = pair_weights(kernel, within_group_lines, above_rows, pair_flag)
        forward = jnp.dot(weights, above_rows, preferred_element_type=jnp.float32)
        forward, behind = (forward, transposed_product(weights, within_group_lines))
        arrived = shifted(behind, "pts", offset)
        accumulated = accumulated + forward + arrived
    return (-accumulated).astype(jnp.bfloat16)


def solution(mesh):
    placed = (
        P(("groups", "pts"), None),
        P(("groups", "pts"), None),
        P(("groups", "pts"), None, None),
        P(("groups", "pts"), None),
        P(("groups", "pts")),
    )
    return jax.shard_map(
        on_device, mesh=mesh, in_specs=placed, out_specs=P(("groups", "pts"), None), check_vma=False
    )
```

profile of v0, /device:TPU:24, one launch (start us, length us, event | category | flops | bytes accessed | tf_op | source)
XLA Modules:
  0.0 333.0 jit_solution(9806630445282042122)
XLA Ops:
  0.7 0.0 copy-start.6
  0.7 0.0 copy-start.4
  0.7 2.2 broadcast_multiply_fusion
  2.9 2.8 collective-permute-start
  5.7 2.5 collective-permute-start.2
  8.2 0.0 copy-done.6
  8.2 0.6 fusion.9
  10.1 0.0 copy-done.4
  10.1 0.8 fusion.8
  10.9 61.2 %collective-permute-done = bf16[384,4096]{1,0:T(8,128)(2,1)S(1)} collective-permute-done((bf16[384,4096]{1,0:T(8,128)(2,1)S(1)}, bf16[384,4096]{1,0:T(8,128)(2,1)S(1)}, u32[]{:S(2)}, u32[]{:S(2)}) %collective-permute-start) | collective-permute-done | bytes 3145760 | tf_op jit(solution)/shard_map/ppermute | solution.py:10
  72.1 0.0 copy-start.3
  72.1 1.8 fusion.3
  73.9 0.0 copy-start.5
  73.9 4.4 %fusion.11 = f32[384,4096]{1,0:T(8,128)} fusion(bf16[384,384]{1,0:T(8,128)(2,1)S(1)} %fusion.3, bf16[384,4096]{1,0:T(8,128)(2,1)S(1)} %broadcast_multiply_fusion), kind=kOutput, calls=%fused_computation.19 | convolution fusion | flops 1207959552 | bytes 9732096 | tf_op jit(solution)/shard_map/dot_general | solution.py:21
  78.3 2.9 collective-permute-start.1
  81.2 162.6 %collective-permute-done.2 = bf16[384,4096]{1,0:T(8,128)(2,1)S(1)} collective-permute-done((bf16[384,4096]{1,0:T(8,128)(2,1)S(1)}, bf16[384,4096]{1,0:T(8,128)(2,1)S(1)}, u32[]{:S(2)}, u32[]{:S(2)}) %collective-permute-start.2) | collective-permute-done | bytes 3145760 | tf_op jit(solution)/shard_map/ppermute | solution.py:10
  243.8 0.0 copy-start.1
  243.8 1.8 fusion.4
  245.6 0.0 copy-done.3
  245.6 0.0 copy-done.1
  245.7 4.4 %fusion.12 = f32[384,4096]{1,0:T(8,128)} fusion(bf16[384,384]{1,0:T(8,128)(2,1)S(1)} %fusion.4, bf16[384,4096]{1,0:T(8,128)(2,1)S(1)} %broadcast_multiply_fusion), kind=kOutput, calls=%fused_computation.20 | convolution fusion | flops 1207959552 | bytes 9732096 | tf_op jit(solution)/shard_map/dot_general | solution.py:21
  250.1 0.0 copy-done.5
  250.1 2.1 collective-permute-start.3
  252.2 7.2 %fusion.5 = f32[384,4096]{1,0:T(8,128)} fusion(bf16[384,4096]{1,0:T(8,128)(2,1)S(1)} %broadcast_multiply_fusion, bf16[384,384]{1,0:T(8,128)(2,1)} %param.6), kind=kOutput, calls=%fused_computation.10 | convolution fusion | flops 2416361472 | bytes 9732096 | tf_op jit(solution)/shard_map/dot_general | solution.py:38
  259.3 0.0 copy-start
  259.3 0.0 copy-start.2
  259.3 3.9 %fusion.10 = f32[384,4096]{1,0:T(8,128)S(1)} fusion(bf16[384,384]{1,0:T(8,128)(2,1)} %copy-done.5, bf16[384,4096]{1,0:T(8,128)(2,1)} %copy-done.3), kind=kOutput, calls=%fused_computation.18 | convolution fusion | flops 1207959552 | bytes 9732096 | tf_op jit(solution)/shard_map/dot_general | solution.py:49
  263.3 0.0 collective-permute-done.1
  263.3 60.9 %collective-permute-done.3 = f32[384,4096]{1,0:T(8,128)} collective-permute-done((f32[384,4096]{1,0:T(8,128)}, f32[384,4096]{1,0:T(8,128)}, u32[]{:S(2)}, u32[]{:S(2)}) %collective-permute-start.3) | collective-permute-done | bytes 6291488 | tf_op jit(solution)/shard_map/ppermute | solution.py:10
  324.2 0.0 copy-done
  324.2 0.0 copy-done.2
  324.2 8.9 %negate_convert_fusion = bf16[384,4096]{1,0:T(8,128)(2,1)} fusion(f32[384,4096]{1,0:T(8,128)} %collective-permute-done.3, f32[384,4096]{1,0:T(8,128)} %collective-permute-done.1, f32[384,4096]{1,0:T(8,128)S(1)} %copy-done, f32[384,4096]{1,0:T(8,128)S(1)} %fusion.10, bf16[384,384]{1,0:T(8,128)(2,1)S(1)} %fusion.4, bf16[384,4096]{1,0:T(8,128)(2,1)S(1)} %copy-done.2), kind=kOutput, calls=%fused_computation | convolution fusion | flops 1217396736 | bytes 31752192 | tf_op jit(solution)/shard_map/dot_general | solution.py:49
  (1 shorter events, 0.0 us)
Async XLA Ops:
  0.7 7.5 %copy-start.6 = (s32[1,2]{1,0:T(1,128)S(1)}, s32[1,2]{1,0:T(1,128)}, u32[]{:S(2)}) copy-start(s32[1,2]{1,0:T(1,128)} %param.8) | copy-start | bytes 28
  0.7 9.4 %copy-start.4 = (bf16[384,2,384]{2,1,0:T(2,128)(2,1)S(1)}, bf16[384,2,384]{2,1,0:T(2,128)(2,1)}, u32[]{:S(2)}) copy-start(bf16[384,2,384]{2,1,0:T(2,128)(2,1)} %param.7) | copy-start | bytes 1769476
  2.9 69.1 %collective-permute-start = (bf16[384,4096]{1,0:T(8,128)(2,1)S(1)}, bf16[384,4096]{1,0:T(8,128)(2,1)S(1)}, u32[]{:S(2)}, u32[]{:S(2)}) collective-permute-start(bf16[384,4096]{1,0:T(8,128)(2,1)S(1)} %broadcast_multiply_fusion), channel_id=1, source_target_pairs={{1,0},{2,1},{3,2},{4,3},{5,4},{6,5},{7,6},{8,7},{9,8},{10,9},{11,1... | collective-permute-start | bytes 9437192 | tf_op jit(solution)/shard_map/ppermute | solution.py:10
  5.7 238.1 %collective-permute-start.2 = (bf16[384,4096]{1,0:T(8,128)(2,1)S(1)}, bf16[384,4096]{1,0:T(8,128)(2,1)S(1)}, u32[]{:S(2)}, u32[]{:S(2)}) collective-permute-start(bf16[384,4096]{1,0:T(8,128)(2,1)S(1)} %broadcast_multiply_fusion), channel_id=1, source_target_pairs={{2,0},{3,1},{4,2},{5,3},{6,4},{7,5},{8,6},{9,7},{10,8},{11,9},{12,... | collective-permute-start | bytes 9437192 | tf_op jit(solution)/shard_map/ppermute | solution.py:10
  72.1 173.6 %copy-start.3 = (bf16[384,4096]{1,0:T(8,128)(2,1)}, bf16[384,4096]{1,0:T(8,128)(2,1)S(1)}, u32[]{:S(2)}) copy-start(bf16[384,4096]{1,0:T(8,128)(2,1)S(1)} %collective-permute-done) | copy-start | bytes 9437188
  73.9 176.2 %copy-start.5 = (bf16[384,384]{1,0:T(8,128)(2,1)}, bf16[384,384]{1,0:T(8,128)(2,1)S(1)}, u32[]{:S(2)}) copy-start(bf16[384,384]{1,0:T(8,128)(2,1)S(1)} %fusion.3) | copy-start | bytes 884740
  78.3 185.0 %collective-permute-start.1 = (f32[384,4096]{1,0:T(8,128)}, f32[384,4096]{1,0:T(8,128)}, u32[]{:S(2)}, u32[]{:S(2)}) collective-permute-start(f32[384,4096]{1,0:T(8,128)} %fusion.11), channel_id=1, source_target_pairs={{0,1},{1,2},{2,3},{3,4},{4,5},{5,6},{6,7},{7,8},{8,9},{9,10},{10,1... | collective-permute-start | bytes 18874376 | tf_op jit(solution)/shard_map/ppermute | solution.py:10
  243.8 1.8 copy-start.1
  250.1 74.1 %collective-permute-start.3 = (f32[384,4096]{1,0:T(8,128)}, f32[384,4096]{1,0:T(8,128)}, u32[]{:S(2)}, u32[]{:S(2)}) collective-permute-start(f32[384,4096]{1,0:T(8,128)} %fusion.12), channel_id=1, source_target_pairs={{0,2},{1,3},{2,4},{3,5},{4,6},{5,7},{6,8},{7,9},{8,10},{9,11},{10,... | collective-permute-start | bytes 18874376 | tf_op jit(solution)/shard_map/ppermute | solution.py:10
  259.3 64.8 %copy-start = (f32[384,4096]{1,0:T(8,128)S(1)}, f32[384,4096]{1,0:T(8,128)}, u32[]{:S(2)}) copy-start(f32[384,4096]{1,0:T(8,128)} %fusion.5) | copy-start | bytes 18874372
  259.3 64.8 %copy-start.2 = (bf16[384,4096]{1,0:T(8,128)(2,1)S(1)}, bf16[384,4096]{1,0:T(8,128)(2,1)}, u32[]{:S(2)}) copy-start(bf16[384,4096]{1,0:T(8,128)(2,1)} %copy-done.1) | copy-start | bytes 9437188
where the time goes:
time: 333 us
  waiting for transfers between devices  285 us (86%)
  matrix products  32.4 us (10%)
  starting transfers between devices  10.2 us (3%)
    ppermute x4, waiting for transfers between devices, shifted(): return lax.ppermute(array, axis, pairs)  285 us
    dot_general x2, matrix products, on_device(): forward = jnp.dot(weights, above_rows, preferred_element_type=jnp.float32)  12.8 us
    ppermute x4, starting transfers between devices, shifted(): return lax.ppermute(array, axis, pairs)  10.2 us
    dot_general x2, matrix products, transposed_product(): lax.dot_general(weights, rows, (((0,), (0,)), ((), ())), preferred_elemen...  8.84 us
    dot_general x1, matrix products, on_device(): jnp.dot(pair_weights(within_group_screening, within_group_lines, within_g...  7.16 us
  transfers between devices with their start and end apart: 4, of which 3 were waited for; matrix products, arithmetic and copies ran while one was open for 7% of the time, Pallas kernels for 0%

commit v1 on v0

v1 whole, which is shorter than its diff:
```python
import jax
import jax.numpy as jnp
from jax import lax
from jax.sharding import PartitionSpec as P

CUTS = (96, 96, 96, 96)


def routes(peers):
    def pairs(f):
        return [(i, f(i)) for i in range(peers) if 0 <= f(i) < peers]

    across = pairs(lambda i: i ^ 2)
    onward = pairs(lambda i: i + 4 if (i // 2) % 2 == 0 else i - 4)
    sibling = pairs(lambda i: i ^ 1)
    return across, onward, sibling


def send(array, pairs):
    return lax.ppermute(array, "pts", pairs)


def stage(total, own, rows, kernel):
    gram = lax.dot_general(rows, own, (((1,), (1,)), ((), ())), preferred_element_type=jnp.float32)
    weights = (kernel.astype(jnp.float32) * gram).astype(jnp.bfloat16)
    part = lax.dot_general(weights, rows, (((0,), (0,)), ((), ())), preferred_element_type=jnp.float32)
    return part if total is None else total + part


def on_device(orbitals, kern_diag, kern_near, couple, tally):
    peers = lax.axis_size("pts")
    me = lax.axis_index("pts")
    odd_core = me % 2 == 1
    odd_chip = (me // 2) % 2 == 1
    across, onward, sibling = routes(peers)

    row = lax.iota(jnp.int32, orbitals.shape[0])
    valid = (row < tally[0]).astype(orbitals.dtype)
    own = orbitals * valid[:, None]

    flags = couple[0].astype(kern_near.dtype)
    near = [kern_near[:, o, :] * flags[o] for o in range(2)]
    below = [send(near[o], [(i, i + o + 1) for i in range(peers - o - 1)]) for o in range(2)]
    above = [n.T for n in near]
    k_sib = jnp.where(odd_core, below[0], above[0])
    k_swap = jnp.where(odd_core, above[0], below[0])
    k_across = jnp.where(odd_chip, below[1], above[1])
    k_onward = jnp.where(odd_chip, above[1], below[1])

    beside = send(own, sibling)
    total = stage(None, own, own, kern_diag.T)
    total = stage(total, own, beside, k_sib)
    at = 0
    for count in CUTS:
        rows = slice(at, at + count)
        from_across = send(own[rows], across)
        from_onward = send(from_across, onward)
        swapped = send(jnp.where(odd_core == odd_chip, from_across, from_onward), sibling)
        arrived = jnp.concatenate([from_across, from_onward, swapped])
        kernel = jnp.concatenate([k_across[rows], k_onward[rows], k_swap[rows]])
        total = stage(total, own, arrived, kernel)
        at += count
    return (-total).astype(jnp.bfloat16)


def solution(mesh):
    placed = (
        P(("groups", "pts"), None),
        P(("groups", "pts"), None),
        P(("groups", "pts"), None, None),
        P(("groups", "pts"), None),
        P(("groups", "pts")),
    )
    return jax.shard_map(
        on_device, mesh=mesh, in_specs=placed, out_specs=P(("groups", "pts"), None), check_vma=False
    )
```

time: 333 us -> 171 us (0.51)
  the two profiles are of different devices: /device:TPU:24 before, /device:TPU:11 now
where the time goes in v1:
time: 171 us; the launch traced here: 170 us
  matrix products  60.1 us (35%)
  waiting for transfers between devices  58.6 us (34%)
  starting transfers between devices  27.6 us (16%)
  local copies, waits for them, and re-layouts  13.1 us (8%)
  other arithmetic  9.48 us (6%)
    dot_general x6, matrix products, stage(): lax.dot_general(weights, rows, (((0,), (0,)), ((), ())), preferred_elemen...  60.1 us
    ppermute x15, waiting for transfers between devices, send(): return lax.ppermute(array, 'pts', pairs)  58.6 us
    ppermute x15, starting transfers between devices, send(): return lax.ppermute(array, 'pts', pairs)  27.6 us
  transfers between devices with their start and end apart: 15, of which 6 were waited for; matrix products, arithmetic and copies ran while one was open for 30% of the time, Pallas kernels for 0%

profile of v1, /device:TPU:11, one launch (start us, length us, event | category | flops | bytes accessed | tf_op | source)
XLA Modules:
  0.0 169.7 jit_solution(12880779829644893902)
XLA Ops:
  0.0 0.7 convert_element_type.57
  0.7 0.6 fusion.40
  1.2 2.3 %fusion.36 = (bf16[384,1,384]{2,1,0:T(2,128)(2,1)S(1)}, bf16[384,1,384]{2,1,0:T(2,128)(2,1)S(1)}) fusion(bf16[384,2,384]{2,1,0:T(2,128)(2,1)} %param.7), kind=kLoop, calls=%fused_computation.67 | loop fusion | bytes 1179648 | tf_op jit(solution)/shard_map/slice | solution.py:42
  3.5 0.8 fusion.70
  4.3 0.9 copy.10
  5.2 3.7 %collective-permute-start = (bf16[384,384]{0,1:T(8,128)(2,1)}, bf16[384,384]{0,1:T(8,128)(2,1)S(1)}, u32[]{:S(2)}, u32[]{:S(2)}) collective-permute-start(bf16[384,384]{0,1:T(8,128)(2,1)} %copy.10), channel_id=1, source_target_pairs={{0,1},{1,2},{2,3},{3,4},{4,5},{5,6},{6,7},{7,8},{8,9},{9,10},{10,1... | collective-permute-start | bytes 884744 | tf_op jit(solution)/shard_map/ppermute | solution.py:20
  8.9 0.6 fusion.69
  9.5 0.9 copy.12
  10.4 3.1 %collective-permute-start.2 = (bf16[384,384]{0,1:T(8,128)(2,1)}, bf16[384,384]{0,1:T(8,128)(2,1)}, u32[]{:S(2)}, u32[]{:S(2)}) collective-permute-start(bf16[384,384]{0,1:T(8,128)(2,1)} %copy.12), channel_id=1, source_target_pairs={{0,2},{1,3},{2,4},{3,5},{4,6},{5,7},{6,8},{7,9},{8,10},{9,11},{10,... | collective-permute-start | bytes 884744 | tf_op jit(solution)/shard_map/ppermute | solution.py:20
  14.2 0.0 copy-done
  14.2 0.0 copy-done.1
  14.2 2.2 %broadcast_multiply_fusion = bf16[384,4096]{1,0:T(8,128)(2,1)S(1)} fusion(bf16[384,4096]{1,0:T(8,128)(2,1)} %param.5, bf16[384]{0:T(512)(128)(2,1)S(1)} %fusion.30), kind=kLoop, calls=%fused_computation.1 | loop fusion | flops 1572864 | bytes 6292224 | tf_op jit(solution)/shard_map/mul | solution.py:39
  16.4 0.1 collective-permute-start.1
  16.5 1.7 %fusion.35 = (bf16[96,4096]{1,0:T(8,128)(2,1)}, bf16[96,4096]{1,0:T(8,128)(2,1)}, bf16[96,4096]{1,0:T(8,128)(2,1)}, bf16[96,4096]{1,0:T(8,128)(2,1)}) fusion(bf16[384,4096]{1,0:T(8,128)(2,1)S(1)} %broadcast_multiply_fusion), kind=kLoop, calls=%fused_computation.66 | loop fusion | bytes 6291456 | tf_op jit(solution)/shard_map/slice | solution.py:56
  18.2 1.2 collective-permute-start.12
  19.5 0.2 collective-permute-start.6
  19.7 7.1 %fusion.1 = f32[384,4096]{1,0:T(8,128)} fusion(bf16[384,4096]{1,0:T(8,128)(2,1)S(1)} %broadcast_multiply_fusion, bf16[384,384]{1,0:T(8,128)(2,1)} %param.6), kind=kOutput, calls=%fused_computation.4 | convolution fusion | flops 2416361472 | bytes 9732096 | tf_op jit(solution)/shard_map/dot_general | solution.py:26
  26.8 0.0 collective-permute-done
  26.8 1.2 collective-permute-start.3
  28.0 1.8 %bitcast_select_fusion = bf16[384,384]{0,1:T(8,128)(2,1)S(1)} fusion(bf16[384,384]{0,1:T(8,128)(2,1)S(1)} %collective-permute-done, pred[]{:T(512)S(6)} %eq.15, bf16[]{:T(256)} %bitcast.2, bf16[384,1,384]{2,1,0:T(2,128)(2,1)} %copy-done), kind=kLoop, calls=%fused_computation.43 | loop fusion | flops 294912 | bytes 884739 | tf_op jit(solution)/shard_map/jit(_where)/select_n | solution.py:46
  29.8 0.9 fusion.39
  30.7 0.0 collective-permute-done.2
  30.7 0.2 collective-permute-start.9
  30.9 1.8 %bitcast_select_fusion.4 = (bf16[384,384]{0,1:T(8,128)(2,1)S(1)}, bf16[384,384]{0,1:T(8,128)(2,1)S(1)}) fusion(bf16[384,384]{0,1:T(8,128)(2,1)} %collective-permute-done.2, pred[]{:T(512)S(6)} %eq.16, bf16[]{:T(256)} %bitcast.5, bf16[384,1,384]{2,1,0:T(2,128)(2,1)} %copy-done.1), kind=kLoop, calls=%fused_computation.46 | loop fusion | flops 442368 | bytes 1179651 | tf_op jit(solution)/shard_map/jit(_where)/select_n | solution.py:47
  32.8 1.1 fusion.37
  33.8 4.6 %collective-permute-done.12 = bf16[96,4096]{1,0:T(8,128)(2,1)} collective-permute-done((bf16[96,4096]{1,0:T(8,128)(2,1)}, bf16[96,4096]{1,0:T(8,128)(2,1)}, u32[]{:S(2)}, u32[]{:S(2)}) %collective-permute-start.12) | collective-permute-done | bytes 786464 | tf_op jit(solution)/shard_map/ppermute | solution.py:20
  38.4 3.2 %collective-permute-start.13 = (bf16[96,4096]{1,0:T(8,128)(2,1)}, bf16[96,4096]{1,0:T(8,128)(2,1)S(1)}, u32[]{:S(2)}, u32[]{:S(2)}) collective-permute-start(bf16[96,4096]{1,0:T(8,128)(2,1)} %collective-permute-done.12), channel_id=1, source_target_pairs={{0,4},{1,5},{4,8},{5,9},{6,2},{7,3},{8,12},{9,13},{10,6},{11,7},{1... | collective-permute-start | bytes 2359304 | tf_op jit(solution)/shard_map/ppermute | solution.py:20
  41.6 13.7 %collective-permute-done.6 = bf16[96,4096]{1,0:T(8,128)(2,1)} collective-permute-done((bf16[96,4096]{1,0:T(8,128)(2,1)}, bf16[96,4096]{1,0:T(8,128)(2,1)}, u32[]{:S(2)}, u32[]{:S(2)}) %collective-permute-start.6) | collective-permute-done | bytes 786464 | tf_op jit(solution)/shard_map/ppermute | solution.py:20
  55.3 3.2 %collective-permute-start.7 = (bf16[96,4096]{1,0:T(8,128)(2,1)}, bf16[96,4096]{1,0:T(8,128)(2,1)S(1)}, u32[]{:S(2)}, u32[]{:S(2)}) collective-permute-start(bf16[96,4096]{1,0:T(8,128)(2,1)} %collective-permute-done.6), channel_id=1, source_target_pairs={{0,4},{1,5},{4,8},{5,9},{6,2},{7,3},{8,12},{9,13},{10,6},{11,7},{1... | collective-permute-start | bytes 2359304 | tf_op jit(solution)/shard_map/ppermute | solution.py:20
  58.5 13.5 %collective-permute-done.3 = bf16[96,4096]{1,0:T(8,128)(2,1)S(1)} collective-permute-done((bf16[96,4096]{1,0:T(8,128)(2,1)}, bf16[96,4096]{1,0:T(8,128)(2,1)S(1)}, u32[]{:S(2)}, u32[]{:S(2)}) %collective-permute-start.3) | collective-permute-done | bytes 786464 | tf_op jit(solution)/shard_map/ppermute | solution.py:20
  72.0 3.2 %collective-permute-start.4 = (bf16[96,4096]{1,0:T(8,128)(2,1)S(1)}, bf16[96,4096]{1,0:T(8,128)(2,1)S(1)}, u32[]{:S(2)}, u32[]{:S(2)}) collective-permute-start(bf16[96,4096]{1,0:T(8,128)(2,1)S(1)} %collective-permute-done.3), channel_id=1, source_target_pairs={{0,4},{1,5},{4,8},{5,9},{6,2},{7,3},{8,12},{9,13},{10,6},{11,7},{1... | collective-permute-start | bytes 2359304 | tf_op jit(solution)/shard_map/ppermute | solution.py:20
  75.2 0.1 constant_dynamic-update-slice_fusion.2
  75.3 1.2 constant_dynamic-update-slice_fusion.5
  76.5 12.4 %collective-permute-done.9 = bf16[96,4096]{1,0:T(8,128)(2,1)S(1)} collective-permute-done((bf16[96,4096]{1,0:T(8,128)(2,1)}, bf16[96,4096]{1,0:T(8,128)(2,1)S(1)}, u32[]{:S(2)}, u32[]{:S(2)}) %collective-permute-start.9) | collective-permute-done | bytes 786464 | tf_op jit(solution)/shard_map/ppermute | solution.py:20
  88.9 3.4 %collective-permute-start.10 = (bf16[96,4096]{1,0:T(8,128)(2,1)S(1)}, bf16[96,4096]{1,0:T(8,128)(2,1)S(1)}, u32[]{:S(2)}, u32[]{:S(2)}) collective-permute-start(bf16[96,4096]{1,0:T(8,128)(2,1)S(1)} %collective-permute-done.9), channel_id=1, source_target_pairs={{0,4},{1,5},{4,8},{5,9},{6,2},{7,3},{8,12},{9,13},{10,6},{11,7},{1... | collective-permute-start | bytes 2359304 | tf_op jit(solution)/shard_map/ppermute | solution.py:20
  92.3 0.1 constant_dynamic-update-slice_fusion.8
  92.3 2.1 %constant_dynamic-update-slice_fusion.11 = bf16[288,4096]{1,0:T(8,128)(2,1)} fusion(bf16[96,4096]{1,0:T(8,128)(2,1)} %collective-permute-done.12), kind=kLoop, calls=%fused_computation.59 | loop fusion | bytes 1572864
  94.4 0.0 collective-permute-done.4
  94.4 0.2 broadcast_select_fusion.3
  94.6 1.1 collective-permute-start.5
  95.7 0.0 collective-permute-done.7
  95.7 0.2 broadcast_select_fusion.2
  95.9 1.2 collective-permute-start.8
  97.1 12.7 %collective-permute-done.10 = bf16[96,4096]{1,0:T(8,128)(2,1)S(1)} collective-permute-done((bf16[96,4096]{1,0:T(8,128)(2,1)S(1)}, bf16[96,4096]{1,0:T(8,128)(2,1)S(1)}, u32[]{:S(2)}, u32[]{:S(2)}) %collective-permute-start.10) | collective-permute-done | bytes 786464 | tf_op jit(solution)/shard_map/ppermute | solution.py:20
  109.8 0.2 broadcast_select_fusion.1
  110.0 1.3 collective-permute-start.11
  111.3 0.0 collective-permute-done.13
  111.3 1.1 broadcast_select_fusion
  112.4 1.2 collective-permute-start.14
  113.5 0.0 collective-permute-done.5
  113.5 0.1 constant_dynamic-update-slice_fusion
  113.6 0.0 collective-permute-done.8
  113.6 0.1 constant_dynamic-update-slice_fusion.3
  113.7 0.0 collective-permute-done.11
  113.7 0.1 constant_dynamic-update-slice_fusion.6
  113.8 0.0 copy-start.2
  113.8 1.7 collective-permute-done.14
  115.4 1.2 constant_dynamic-update-slice_fusion.9
  116.7 8.7 %fusion.7 = f32[384,4096]{1,0:T(8,128)} fusion(bf16[288,4096]{1,0:T(8,128)(2,1)} %copy-done.2, bf16[96,384]{0,1:T(8,128)(2,1)} %get-tuple-element.30, bf16[96,384]{0,1:T(8,128)(2,1)} %get-tuple-element.37, bf16[96,384]{0,1:T(8,128)(2,1)} %get-tuple-element.22, bf16[384,4096]{1,0:T(8,128)(2,1)S(1)} %broadcast_multiply_fusion), kind=kOutput, calls=%fused_computation.19 | convolution fusion | flops 1812824064 | bytes 12017664 | tf_op jit(solution)/shard_map/dot_general | solution.py:26
  125.4 8.7 %fusion.6 = f32[384,4096]{1,0:T(8,128)} fusion(bf16[288,4096]{1,0:T(8,128)(2,1)} %copy-done.3, bf16[96,384]{0,1:T(8,128)(2,1)} %get-tuple-element.31, bf16[96,384]{0,1:T(8,128)(2,1)} %get-tuple-element.36, bf16[96,384]{0,1:T(8,128)(2,1)} %get-tuple-element.23, bf16[384,4096]{1,0:T(8,128)(2,1)S(1)} %broadcast_multiply_fusion), kind=kOutput, calls=%fused_computation.18 | convolution fusion | flops 1812824064 | bytes 12017664 | tf_op jit(solution)/shard_map/dot_general | solution.py:26
  134.0 8.7 %fusion.5 = f32[384,4096]{1,0:T(8,128)} fusion(bf16[288,4096]{1,0:T(8,128)(2,1)} %copy-done.4, bf16[96,384]{0,1:T(8,128)(2,1)} %get-tuple-element.32, bf16[96,384]{0,1:T(8,128)(2,1)} %get-tuple-element.35, bf16[96,384]{0,1:T(8,128)(2,1)} %get-tuple-element.24, bf16[384,4096]{1,0:T(8,128)(2,1)S(1)} %broadcast_multiply_fusion), kind=kOutput, calls=%fused_computation.17 | convolution fusion | flops 1812824064 | bytes 12017664 | tf_op jit(solution)/shard_map/dot_general | solution.py:26
  142.7 0.0 collective-permute-done.1
  142.7 9.9 %fusion.4 = f32[384,4096]{1,0:T(8,128)} fusion(bf16[384,4096]{1,0:T(8,128)(2,1)} %collective-permute-done.1, bf16[384,384]{0,1:T(8,128)(2,1)S(1)} %collective-permute-done, pred[]{:T(512)S(6)} %eq.15, bf16[384,4096]{1,0:T(8,128)(2,1)S(1)} %broadcast_multiply_fusion, bf16[384,1,384]{2,1,0:T(2,128)(2,1)} %copy-done, bf16[]{:T(256)} %bitcast.2), kind=kOutput, calls=%fused_computation.16 | convolution fusion | flops 2416656384 | bytes 13172739 | tf_op jit(solution)/shard_map/dot_general | solution.py:26
  152.6 17.1 %negate_convert_fusion = bf16[384,4096]{1,0:T(8,128)(2,1)} fusion(f32[384,4096]{1,0:T(8,128)} %fusion.7, f32[384,4096]{1,0:T(8,128)} %fusion.6, f32[384,4096]{1,0:T(8,128)} %fusion.5, f32[384,4096]{1,0:T(8,128)} %fusion.1, f32[384,4096]{1,0:T(8,128)} %fusion.4, bf16[288,4096]{1,0:T(8,128)(2,1)} %constant_dynamic-update-slice_fusion.9, ...), kind=kOutput, calls=%fused_computation | convolution fusion | flops 1823834112 | bytes 40329216 | tf_op jit(solution)/shard_map/dot_general | solution.py:26
  (8 shorter events, 0.0 us)
Async XLA Ops:
  3.5 10.7 %copy-start = (bf16[384,1,384]{2,1,0:T(2,128)(2,1)}, bf16[384,1,384]{2,1,0:T(2,128)(2,1)S(1)}, u32[]{:S(2)}) copy-start(bf16[384,1,384]{2,1,0:T(2,128)(2,1)S(1)} %get-tuple-element.20) | copy-start | bytes 884740
  3.5 10.7 %copy-start.1 = (bf16[384,1,384]{2,1,0:T(2,128)(2,1)}, bf16[384,1,384]{2,1,0:T(2,128)(2,1)S(1)}, u32[]{:S(2)}) copy-start(bf16[384,1,384]{2,1,0:T(2,128)(2,1)S(1)} %get-tuple-element.19) | copy-start | bytes 884740
  5.2 21.6 %collective-permute-start = (bf16[384,384]{0,1:T(8,128)(2,1)}, bf16[384,384]{0,1:T(8,128)(2,1)S(1)}, u32[]{:S(2)}, u32[]{:S(2)}) collective-permute-start(bf16[384,384]{0,1:T(8,128)(2,1)} %copy.10), channel_id=1, source_target_pairs={{0,1},{1,2},{2,3},{3,4},{4,5},{5,6},{6,7},{7,8},{8,9},{9,10},{10,1... | collective-permute-start | bytes 884744 | tf_op jit(solution)/shard_map/ppermute | solution.py:20
  10.4 20.3 %collective-permute-start.2 = (bf16[384,384]{0,1:T(8,128)(2,1)}, bf16[384,384]{0,1:T(8,128)(2,1)}, u32[]{:S(2)}, u32[]{:S(2)}) collective-permute-start(bf16[384,384]{0,1:T(8,128)(2,1)} %copy.12), channel_id=1, source_target_pairs={{0,2},{1,3},{2,4},{3,5},{4,6},{5,7},{6,8},{7,9},{8,10},{9,11},{10,... | collective-permute-start | bytes 884744 | tf_op jit(solution)/shard_map/ppermute | solution.py:20
  16.4 126.3 %collective-permute-start.1 = (bf16[384,4096]{1,0:T(8,128)(2,1)S(1)}, bf16[384,4096]{1,0:T(8,128)(2,1)}, u32[]{:S(2)}, u32[]{:S(2)}) collective-permute-start(bf16[384,4096]{1,0:T(8,128)(2,1)S(1)} %broadcast_multiply_fusion), channel_id=1, source_target_pairs={{0,1},{1,0},{2,3},{3,2},{4,5},{5,4},{6,7},{7,6},{8,9},{9,8},{10,11... | collective-permute-start | bytes 9437192 | tf_op jit(solution)/shard_map/ppermute | solution.py:20
  18.2 20.2 %collective-permute-start.12 = (bf16[96,4096]{1,0:T(8,128)(2,1)}, bf16[96,4096]{1,0:T(8,128)(2,1)}, u32[]{:S(2)}, u32[]{:S(2)}) collective-permute-start(bf16[96,4096]{1,0:T(8,128)(2,1)} %get-tuple-element.5), channel_id=1, source_target_pairs={{0,2},{1,3},{2,0},{3,1},{4,6},{5,7},{6,4},{7,5},{8,10},{9,11},{10,... | collective-permute-start | bytes 2359304 | tf_op jit(solution)/shard_map/ppermute | solution.py:20
  19.5 35.8 %collective-permute-start.6 = (bf16[96,4096]{1,0:T(8,128)(2,1)}, bf16[96,4096]{1,0:T(8,128)(2,1)}, u32[]{:S(2)}, u32[]{:S(2)}) collective-permute-start(bf16[96,4096]{1,0:T(8,128)(2,1)} %get-tuple-element.7), channel_id=1, source_target_pairs={{0,2},{1,3},{2,0},{3,1},{4,6},{5,7},{6,4},{7,5},{8,10},{9,11},{10,... | collective-permute-start | bytes 2359304 | tf_op jit(solution)/shard_map/ppermute | solution.py:20
  26.8 45.2 %collective-permute-start.3 = (bf16[96,4096]{1,0:T(8,128)(2,1)}, bf16[96,4096]{1,0:T(8,128)(2,1)S(1)}, u32[]{:S(2)}, u32[]{:S(2)}) collective-permute-start(bf16[96,4096]{1,0:T(8,128)(2,1)} %get-tuple-element.8), channel_id=1, source_target_pairs={{0,2},{1,3},{2,0},{3,1},{4,6},{5,7},{6,4},{7,5},{8,10},{9,11},{10,... | collective-permute-start | bytes 2359304 | tf_op jit(solution)/shard_map/ppermute | solution.py:20
  30.7 58.2 %collective-permute-start.9 = (bf16[96,4096]{1,0:T(8,128)(2,1)}, bf16[96,4096]{1,0:T(8,128)(2,1)S(1)}, u32[]{:S(2)}, u32[]{:S(2)}) collective-permute-start(bf16[96,4096]{1,0:T(8,128)(2,1)} %get-tuple-element.6), channel_id=1, source_target_pairs={{0,2},{1,3},{2,0},{3,1},{4,6},{5,7},{6,4},{7,5},{8,10},{9,11},{10,... | collective-permute-start | bytes 2359304 | tf_op jit(solution)/shard_map/ppermute | solution.py:20
  38.4 72.9 %collective-permute-start.13 = (bf16[96,4096]{1,0:T(8,128)(2,1)}, bf16[96,4096]{1,0:T(8,128)(2,1)S(1)}, u32[]{:S(2)}, u32[]{:S(2)}) collective-permute-start(bf16[96,4096]{1,0:T(8,128)(2,1)} %collective-permute-done.12), channel_id=1, source_target_pairs={{0,4},{1,5},{4,8},{5,9},{6,2},{7,3},{8,12},{9,13},{10,6},{11,7},{1... | collective-permute-start | bytes 2359304 | tf_op jit(solution)/shard_map/ppermute | solution.py:20
  55.3 40.4 %collective-permute-start.7 = (bf16[96,4096]{1,0:T(8,128)(2,1)}, bf16[96,4096]{1,0:T(8,128)(2,1)S(1)}, u32[]{:S(2)}, u32[]{:S(2)}) collective-permute-start(bf16[96,4096]{1,0:T(8,128)(2,1)} %collective-permute-done.6), channel_id=1, source_target_pairs={{0,4},{1,5},{4,8},{5,9},{6,2},{7,3},{8,12},{9,13},{10,6},{11,7},{1... | collective-permute-start | bytes 2359304 | tf_op jit(solution)/shard_map/ppermute | solution.py:20
  72.0 22.4 %collective-permute-start.4 = (bf16[96,4096]{1,0:T(8,128)(2,1)S(1)}, bf16[96,4096]{1,0:T(8,128)(2,1)S(1)}, u32[]{:S(2)}, u32[]{:S(2)}) collective-permute-start(bf16[96,4096]{1,0:T(8,128)(2,1)S(1)} %collective-permute-done.3), channel_id=1, source_target_pairs={{0,4},{1,5},{4,8},{5,9},{6,2},{7,3},{8,12},{9,13},{10,6},{11,7},{1... | collective-permute-start | bytes 2359304 | tf_op jit(solution)/shard_map/ppermute | solution.py:20
  88.9 20.9 %collective-permute-start.10 = (bf16[96,4096]{1,0:T(8,128)(2,1)S(1)}, bf16[96,4096]{1,0:T(8,128)(2,1)S(1)}, u32[]{:S(2)}, u32[]{:S(2)}) collective-permute-start(bf16[96,4096]{1,0:T(8,128)(2,1)S(1)} %collective-permute-done.9), channel_id=1, source_target_pairs={{0,4},{1,5},{4,8},{5,9},{6,2},{7,3},{8,12},{9,13},{10,6},{11,7},{1... | collective-permute-start | bytes 2359304 | tf_op jit(solution)/shard_map/ppermute | solution.py:20
  94.6 18.9 %collective-permute-start.5 = (bf16[96,4096]{1,0:T(8,128)(2,1)S(1)}, bf16[96,4096]{1,0:T(8,128)(2,1)S(1)}, u32[]{:S(2)}, u32[]{:S(2)}) collective-permute-start(bf16[96,4096]{1,0:T(8,128)(2,1)S(1)} %get-tuple-element.11), channel_id=1, source_target_pairs={{0,1},{1,0},{2,3},{3,2},{4,5},{5,4},{6,7},{7,6},{8,9},{9,8},{10,11... | collective-permute-start | bytes 2359304 | tf_op jit(solution)/shard_map/ppermute | solution.py:20
  95.9 17.7 %collective-permute-start.8 = (bf16[96,4096]{1,0:T(8,128)(2,1)S(1)}, bf16[96,4096]{1,0:T(8,128)(2,1)S(1)}, u32[]{:S(2)}, u32[]{:S(2)}) collective-permute-start(bf16[96,4096]{1,0:T(8,128)(2,1)S(1)} %get-tuple-element.13), channel_id=1, source_target_pairs={{0,1},{1,0},{2,3},{3,2},{4,5},{5,4},{6,7},{7,6},{8,9},{9,8},{10,11... | collective-permute-start | bytes 2359304 | tf_op jit(solution)/shard_map/ppermute | solution.py:20
  110.0 3.7 %collective-permute-start.11 = (bf16[96,4096]{1,0:T(8,128)(2,1)S(1)}, bf16[96,4096]{1,0:T(8,128)(2,1)S(1)}, u32[]{:S(2)}, u32[]{:S(2)}) collective-permute-start(bf16[96,4096]{1,0:T(8,128)(2,1)S(1)} %get-tuple-element.15), channel_id=1, source_target_pairs={{0,1},{1,0},{2,3},{3,2},{4,5},{5,4},{6,7},{7,6},{8,9},{9,8},{10,11... | collective-permute-start | bytes 2359304 | tf_op jit(solution)/shard_map/ppermute | solution.py:20
  112.4 3.1 %collective-permute-start.14 = (bf16[96,4096]{1,0:T(8,128)(2,1)S(1)}, bf16[96,4096]{1,0:T(8,128)(2,1)S(1)}, u32[]{:S(2)}, u32[]{:S(2)}) collective-permute-start(bf16[96,4096]{1,0:T(8,128)(2,1)S(1)} %get-tuple-element.9), channel_id=1, source_target_pairs={{0,1},{1,0},{2,3},{3,2},{4,5},{5,4},{6,7},{7,6},{8,9},{9,8},{10,11... | collective-permute-start | bytes 2359304 | tf_op jit(solution)/shard_map/ppermute | solution.py:20
  113.6 3.1 %copy-start.4 = (bf16[288,4096]{1,0:T(8,128)(2,1)}, bf16[288,4096]{1,0:T(8,128)(2,1)S(1)}, u32[]{:S(2)}) copy-start(bf16[288,4096]{1,0:T(8,128)(2,1)S(1)} %constant_dynamic-update-slice_fusion) | copy-start | bytes 7077892
  113.7 3.0 %copy-start.3 = (bf16[288,4096]{1,0:T(8,128)(2,1)}, bf16[288,4096]{1,0:T(8,128)(2,1)S(1)}, u32[]{:S(2)}) copy-start(bf16[288,4096]{1,0:T(8,128)(2,1)S(1)} %constant_dynamic-update-slice_fusion.3) | copy-start | bytes 7077892
  113.8 2.9 %copy-start.2 = (bf16[288,4096]{1,0:T(8,128)(2,1)}, bf16[288,4096]{1,0:T(8,128)(2,1)S(1)}, u32[]{:S(2)}) copy-start(bf16[288,4096]{1,0:T(8,128)(2,1)S(1)} %constant_dynamic-update-slice_fusion.6) | copy-start | bytes 7077892

commit v2 on v1

v2 whole, which is shorter than its diff:
```python
import functools

import jax
import jax.numpy as jnp
from jax import lax
from jax.experimental import pallas as pl
from jax.experimental.pallas import tpu as pltpu
from jax.sharding import PartitionSpec as P

CUTS = (64,) * 6
KAT = 5
LAG = 3
TILE = 512
MIB = 2**20


def routes(peers):
    def pairs(f):
        return [(i, f(i)) for i in range(peers) if 0 <= f(i) < peers]

    across = pairs(lambda i: i ^ 2)
    onward = pairs(lambda i: i + 4 if (i // 2) % 2 == 0 else i - 4)
    sibling = pairs(lambda i: i ^ 1)
    return across, onward, sibling


def send(array, pairs):
    return lax.ppermute(array, "pts", pairs)


def after(array, *gates):
    return lax.optimization_barrier((array, *gates))[0]


def grams(rows, own):
    return lax.dot_general(rows, own, (((1,), (1,)), ((), ())), preferred_element_type=jnp.float32)


def weigh(kern, gram):
    return kern.astype(jnp.float32) * gram


def tiles(width, body):
    def step(i, carry):
        body(pl.ds(pl.multiple_of(i * TILE, TILE), TILE))
        return carry

    lax.fori_loop(0, width // TILE, step, 0)


def call(body, out, args, scratch=(), smem=0, aliases=None, limit=16, flops=0):
    held = [pltpu.with_memory_space_constraint(a, pltpu.VMEM) for a in args[: len(args) - smem]]
    vector, scalar = pl.BlockSpec(memory_space=pltpu.VMEM), pl.BlockSpec(memory_space=pltpu.SMEM)
    return pl.pallas_call(
        body,
        out_shape=out,
        in_specs=[vector] * len(held) + [scalar] * smem,
        out_specs=jax.tree.map(lambda _: vector, out),
        input_output_aliases=aliases or {},
        scratch_shapes=list(scratch),
        compiler_params=pltpu.CompilerParams(vmem_limit_bytes=limit * MIB),
        cost_estimate=pl.CostEstimate(flops=flops, bytes_accessed=flops // 100, transcendentals=0),
    )(*held, *args[len(args) - smem :])


def prepare_body(near0, near1, couple, down0, down1, up0, up1):
    for o, (near, down, up) in enumerate(((near0, down0, up0), (near1, down1, up1))):
        kept = near[...].astype(jnp.float32) * couple[0, o].astype(jnp.float32)
        down[...] = kept.astype(down.dtype)
        up[...] = kept.T.astype(up.dtype)


def diagonal_body(own, kern, total, weights):
    weights[...] = weigh(kern[...], grams(own[...], own[...])).astype(weights.dtype)

    def tile(cols):
        total[:, cols] = jnp.dot(weights[...], own[:, cols], preferred_element_type=jnp.float32)

    tiles(own.shape[1], tile)


def collect_body(n, base, own, *refs):
    pieces, (rows, gram) = refs[:n], refs[-2:]
    at = base
    for piece in pieces:
        rows[at : at + piece.shape[0], :] = piece[...]
        at += piece.shape[0]
    gram[base:at, :] = grams(rows[base:at, :], own[...])


def pick(odd, down, up, rows):
    return jnp.where(odd, down[rows, :], up[rows, :])


def chosen(place, downs, ups, span):
    odd_core, odd_chip = (place & 1) == 1, (place & 2) == 2
    (down0, down1), (up0, up1) = downs, ups
    return [pick(odd_chip, down1, up1, span), pick(odd_chip, up1, down1, span), pick(odd_core, up0, down0, span)]


def product_body(spans, gram, rows, down0, down1, up0, up1, before, place, total, weights):
    odd_core = (place[0] & 1) == 1
    height = total.shape[0]
    kerns = [pick(odd_core, down0, up0, slice(0, height))]
    for span in spans:
        kerns += chosen(place[0], (down0, down1), (up0, up1), span)
    at = 0
    for kern in kerns:
        to = at + kern.shape[0]
        weights[at:to, :] = weigh(kern, gram[at:to, :]).astype(weights.dtype)
        at = to

    def tile(cols):
        part = lax.dot_general(
            weights[...], rows[:at, cols], (((0,), (0,)), ((), ())), preferred_element_type=jnp.float32
        )
        total[:, cols] = before[:, cols] + part

    tiles(total.shape[1], tile)


def last_body(span, own, across, onward, swap, down0, down1, up0, up1, before, place, out, rows, weights):
    at = 0
    for piece in (across, onward, swap):
        rows[at : at + piece.shape[0], :] = piece[...]
        at += piece.shape[0]
    kern = jnp.concatenate(chosen(place[0], (down0, down1), (up0, up1), span))
    weights[...] = weigh(kern, grams(rows[...], own[...])).T.astype(weights.dtype)

    def tile(cols):
        part = jnp.dot(weights[...], rows[:, cols], preferred_element_type=jnp.float32)
        out[:, cols] = (-(before[:, cols] + part)).astype(out.dtype)

    tiles(out.shape[1], tile)


def on_device(orbitals, kern_diag, kern_near, couple, tally):
    peers = lax.axis_size("pts")
    me = lax.axis_index("pts")
    mixed = ((me & 1) == 1) == ((me & 2) == 2)
    place = me.astype(jnp.int32)[None]
    across, onward, sibling = routes(peers)
    height, width = orbitals.shape
    kind = orbitals.dtype

    valid = (lax.iota(jnp.int32, height) < tally[0]).astype(kind)[:, None]
    spans, at = [], 0
    for count in CUTS:
        spans.append(slice(at, at + count))
        at += count
    last = len(spans) - 1

    held = {}

    def join(*names):
        names = [n for n in names if n in held]
        for n, value in zip(names, lax.optimization_barrier(tuple(held[n] for n in names))):
            held[n] = value

    def part(j, *gates):
        return after(orbitals, *gates)[spans[j]] * valid[spans[j]]

    def pieces(i):
        return [held["across", i], held["onward", i], held["swap", i]]

    first = part(0)
    held["across", 0] = send(first, across)
    second = part(1, first)
    held["across", 1] = send(second, across)
    own = after(orbitals, second) * valid
    beside = send(own, sibling)
    near = after(kern_near, own)
    square = jax.ShapeDtypeStruct((height, height), kind)
    down0, down1, up0, up1 = call(
        prepare_body, (square,) * 4, [near[:, 0, :], near[:, 1, :], couple], smem=1
    )
    held["total"] = call(
        diagonal_body, pltpu.VMEM((height, width), jnp.float32), [own, after(kern_diag, up0)],
        scratch=[pltpu.VMEM((height, height), kind)], flops=4 * height * height * width,
    )

    depth = height + 3 * (height - CUTS[-1])

    def collect(base, pieces):
        state = [held[n] for n in ("rows", "gram") if n in held]
        args = [own, *pieces] + state
        out = (pltpu.VMEM((depth, width), kind), pltpu.VMEM((depth, height), jnp.float32))
        aliases = {len(args) - 2: 0, len(args) - 1: 1} if state else {}
        count = sum(p.shape[0] for p in pieces)
        held["rows"], held["gram"] = call(
            functools.partial(collect_body, len(pieces), base), out, args, aliases=aliases,
            flops=2 * count * height * width,
        )

    collect(0, [after(beside, held["total"])])
    join(("across", 0), "rows", "gram")
    for w in range(1, last + 5):
        now = held["rows"]
        if w + 1 <= last:
            held["across", w + 1] = send(part(w + 1, now), across)
        if w - 1 <= last:
            held["onward", w - 1] = send(held["across", w - 1], onward)
        if w == KAT:
            for o, down in enumerate((down0, down1)):
                pairs = [(i, i + o + 1) for i in range(peers - o - 1)]
                held["down", o] = send(after(down, now), pairs)
        i = w - LAG
        if 0 <= i <= last:
            held["swap", i] = send(jnp.where(mixed, held["across", i], held["onward", i]), sibling)
        i -= 1
        if 0 <= i < last:
            collect(height + 3 * spans[i].start, pieces(i))
        if w <= last:
            join(("across", w), ("onward", w - LAG + 1), ("swap", w - LAG), "rows", "gram")
    downs = [held["down", o] for o in range(2)]
    state = held["rows"], held["gram"]
    total = held["total"]
    from_across, from_onward, swapped = ({last: piece} for piece in pieces(last))
    rows, gram = state
    kerns = [*downs, up0, up1]
    total = call(
        functools.partial(product_body, spans[:last]), pltpu.VMEM((height, width), jnp.float32),
        [gram, rows, *kerns, total, place], smem=1, aliases={6: 0},
        scratch=[pltpu.VMEM((depth, height), kind)], flops=2 * depth * height * width,
    )
    count = 3 * CUTS[-1]
    return call(
        functools.partial(last_body, spans[last]), jax.ShapeDtypeStruct((height, width), kind),
        [own, from_across[last], from_onward[last], swapped[last], *kerns, total, place], smem=1,
        scratch=[pltpu.VMEM((count, width), kind), pltpu.VMEM((height, count), kind)],
        flops=4 * count * height * width,
    )


def solution(mesh):
    placed = (
        P(("groups", "pts"), None),
        P(("groups", "pts"), None),
        P(("groups", "pts"), None, None),
        P(("groups", "pts"), None),
        P(("groups", "pts")),
    )
    return jax.shard_map(
        on_device, mesh=mesh, in_specs=placed, out_specs=P(("groups", "pts"), None), check_vma=False
    )
```

time: 171 us -> 118 us (0.69)
  matrix products: 60.1 us -> 0 us
  Pallas kernels: 0 us -> 29.2 us
  waiting for transfers between devices: 58.6 us -> 37.8 us
  local copies, waits for them, and re-layouts: 13.1 us -> 3.37 us
  starting transfers between devices: 27.6 us -> 37.1 us
  other arithmetic: 9.48 us -> 6.94 us
    dot_general x6 -> x0, matrix products: 60.1 us -> none  [stage(): lax.dot_general(weights, rows, (((0,), (0,)), ((), ())), preferred_elemen...]
    pallas_call x0 -> x10, Pallas kernels: none -> 29.2 us  [call(): pl.pallas_call(body, out_shape=out, in_specs=[vector] * len(held) + [scal...]
    ppermute x15 -> x21, waiting for transfers between devices: 58.6 us -> 37.8 us  [send(): return lax.ppermute(array, 'pts', pairs)]
    ppermute x15 -> x21, starting transfers between devices: 27.6 us -> 37.1 us  [send(): return lax.ppermute(array, 'pts', pairs)]
    slice x5 -> x1, local copies, waits for them, and re-layouts: 6.49 us -> 0.08 us  [part(): return after(orbitals, *gates)[spans[j]] * valid[spans[j]]]
    select_n x6, other arithmetic: 5.27 us -> 0.42 us  [on_device(): jnp.where(mixed, held['across', i], held['onward', i])]
    mul x3 -> x7, other arithmetic: 3.54 us -> 6.52 us  [the longest x6 4.3 us: part(): return after(orbitals, *gates)[spans[j]] * valid[spans[j]]]
    mul x2 -> x0, local copies, waits for them, and re-layouts: 1.79 us -> none  [on_device(): near = [kern_near[:, o, :] * flags[o] for o in range(2)]]
  transfers between devices with their start and end apart: 15 -> 21, of which waited for: 6 -> 6; matrix products, arithmetic and copies ran while one was open for 30% -> 1% of each run, Pallas kernels for 0% -> 21%
where the time goes in v2:
time: 118 us; the launch traced here: 115 us
  waiting for transfers between devices  37.8 us (32%)
  starting transfers between devices  37.1 us (31%)
  Pallas kernels  29.2 us (25%)
  other arithmetic  6.94 us (6%)
  local copies, waits for them, and re-layouts  3.37 us (3%)
    ppermute x21, waiting for transfers between devices, send(): return lax.ppermute(array, 'pts', pairs)  37.8 us
    ppermute x21, starting transfers between devices, send(): return lax.ppermute(array, 'pts', pairs)  37.1 us
    pallas_call x10, Pallas kernels, call(): pl.pallas_call(body, out_shape=out, in_specs=[vector] * len(held) + [scal...  29.2 us
    mul x6, other arithmetic, part(): return after(orbitals, *gates)[spans[j]] * valid[spans[j]]  4.3 us
    unnamed x20, local copies, waits for them, and re-layouts  3.16 us
  transfers between devices with their start and end apart: 21, of which 6 were waited for; matrix products, arithmetic and copies ran while one was open for 1% of the time, Pallas kernels for 21%

profile of v2, /device:TPU:11, one launch (start us, length us, event | category | flops | bytes accessed | tf_op | source)
XLA Modules:
  0.0 115.5 jit_solution(18239891350005434165)
XLA Ops:
  0.7 0.1 fusion.1
  0.7 1.9 %slice_multiply_fusion = bf16[64,4096]{1,0:T(8,128)(2,1)} fusion(bf16[384,4096]{1,0:T(8,128)(2,1)} %param.5, bf16[64]{0:T(256)(128)(2,1)S(1)} %get-tuple-element.116), kind=kLoop, calls=%fused_computation.1 | loop fusion | flops 262144 | bytes 1048704 | tf_op jit(solution)/shard_map/mul | solution.py:161
  2.7 1.9 %slice_multiply_fusion.5 = bf16[64,4096]{1,0:T(8,128)(2,1)} fusion(bf16[384,4096]{1,0:T(8,128)(2,1)} %param.5, bf16[64]{0:T(256)(128)(2,1)S(1)} %get-tuple-element.115), kind=kLoop, calls=%fused_computation.6 | loop fusion | flops 262144 | bytes 1048704 | tf_op jit(solution)/shard_map/mul | solution.py:161
  4.6 2.2 %broadcast_multiply_fusion.own = bf16[384,4096]{1,0:T(8,128)(2,1)S(1)} fusion(bf16[384,4096]{1,0:T(8,128)(2,1)} %param.5, bf16[384]{0:T(512)(128)(2,1)S(1)} %fusion), kind=kLoop, calls=%fused_computation | loop fusion | flops 1572864 | bytes 6292224 | tf_op jit(solution)/shard_map/mul | solution.py:170
  6.9 0.7 collective-permute-start.2
  7.6 1.3 %collective-permute-start.1 = (bf16[64,4096]{1,0:T(8,128)(2,1)}, bf16[64,4096]{1,0:T(8,128)(2,1)}, u32[]{:S(2)}, u32[]{:S(2)}) collective-permute-start(bf16[64,4096]{1,0:T(8,128)(2,1)} %slice_multiply_fusion), channel_id=1, source_target_pairs={{0,2},{1,3},{2,0},{3,1},{4,6},{5,7},{6,4},{7,5},{8,10},{9,11},{10,... | collective-permute-start | bytes 1572872 | tf_op jit(solution)/shard_map/ppermute | solution.py:28
  8.9 0.2 collective-permute-start
  9.1 0.1 copy.17
  9.2 0.1 slice_bitcast_fusion
  9.2 0.8 shard_map.55
  10.0 0.7 copy-done
  10.8 0.7 copy-done.4
  11.5 0.7 copy-done.6
  12.2 1.0 copy-done.2
  13.2 4.7 %shard_map.56.before = f32[384,4096]{1,0:T(8,128)S(1)} custom-call(bf16[384,4096]{1,0:T(8,128)(2,1)S(1)} %broadcast_multiply_fusion.own, bf16[384,384]{1,0:T(8,128)(2,1)S(1)} %copy-done.2), custom_call_target="tpu_custom_call" | custom-call | flops 2415919104 | bytes 24159192 | tf_op jit(solution)/shard_map/pallas_call | solution.py:54
  17.9 0.0 copy-start.8
  18.0 3.8 %shard_map.57 = (bf16[1344,4096]{1,0:T(8,128)(2,1)S(1)}, f32[1344,384]{1,0:T(8,128)S(1)}) custom-call(bf16[384,4096]{1,0:T(8,128)(2,1)S(1)} %broadcast_multiply_fusion.own, bf16[384,4096]{1,0:T(8,128)(2,1)} %collective-permute-done.2.refs_0_), custom_call_target="tpu_custom_call" | custom-call | flops 1207959552 | bytes 12079595 | tf_op jit(solution)/shard_map/pallas_call | solution.py:54
  21.8 0.0 collective-permute-done.1.refs_0_
  21.8 0.1 slice_multiply_fusion.3
  21.9 1.3 %collective-permute-start.5 = (bf16[64,4096]{1,0:T(8,128)(2,1)S(1)}, bf16[64,4096]{1,0:T(8,128)(2,1)S(1)}, u32[]{:S(2)}, u32[]{:S(2)}) collective-permute-start(bf16[64,4096]{1,0:T(8,128)(2,1)S(1)} %slice_multiply_fusion.3), channel_id=1, source_target_pairs={{0,2},{1,3},{2,0},{3,1},{4,6},{5,7},{6,4},{7,5},{8,10},{9,11},{10,... | collective-permute-start | bytes 1572872 | tf_op jit(solution)/shard_map/ppermute | solution.py:28
  23.2 3.2 %collective-permute-start.6 = (bf16[64,4096]{1,0:T(8,128)(2,1)}, bf16[64,4096]{1,0:T(8,128)(2,1)S(1)}, u32[]{:S(2)}, u32[]{:S(2)}) collective-permute-start(bf16[64,4096]{1,0:T(8,128)(2,1)} %collective-permute-done.1.refs_0_), channel_id=1, source_target_pairs={{0,4},{1,5},{4,8},{5,9},{6,2},{7,3},{8,12},{9,13},{10,6},{11,7},{1... | collective-permute-start | bytes 1572872 | tf_op jit(solution)/shard_map/ppermute | solution.py:28
  26.4 6.2 %collective-permute-done.refs_0_ = bf16[64,4096]{1,0:T(8,128)(2,1)} collective-permute-done((bf16[64,4096]{1,0:T(8,128)(2,1)}, bf16[64,4096]{1,0:T(8,128)(2,1)}, u32[]{:S(2)}, u32[]{:S(2)}) %collective-permute-start) | collective-permute-done | bytes 524320 | tf_op jit(solution)/shard_map/ppermute | solution.py:28
  32.7 0.1 slice_multiply_fusion.4
  32.8 1.3 %collective-permute-start.3 = (bf16[64,4096]{1,0:T(8,128)(2,1)S(1)}, bf16[64,4096]{1,0:T(8,128)(2,1)S(1)}, u32[]{:S(2)}, u32[]{:S(2)}) collective-permute-start(bf16[64,4096]{1,0:T(8,128)(2,1)S(1)} %slice_multiply_fusion.4), channel_id=1, source_target_pairs={{0,2},{1,3},{2,0},{3,1},{4,6},{5,7},{6,4},{7,5},{8,10},{9,11},{10,... | collective-permute-start | bytes 1572872 | tf_op jit(solution)/shard_map/ppermute | solution.py:28
  34.1 3.2 %collective-permute-start.4 = (bf16[64,4096]{1,0:T(8,128)(2,1)}, bf16[64,4096]{1,0:T(8,128)(2,1)S(1)}, u32[]{:S(2)}, u32[]{:S(2)}) collective-permute-start(bf16[64,4096]{1,0:T(8,128)(2,1)} %collective-permute-done.refs_0_), channel_id=1, source_target_pairs={{0,4},{1,5},{4,8},{5,9},{6,2},{7,3},{8,12},{9,13},{10,6},{11,7},{1... | collective-permute-start | bytes 1572872 | tf_op jit(solution)/shard_map/ppermute | solution.py:28
  37.3 6.5 %collective-permute-done.5.refs_0_ = bf16[64,4096]{1,0:T(8,128)(2,1)S(1)} collective-permute-done((bf16[64,4096]{1,0:T(8,128)(2,1)S(1)}, bf16[64,4096]{1,0:T(8,128)(2,1)S(1)}, u32[]{:S(2)}, u32[]{:S(2)}) %collective-permute-start.5) | collective-permute-done | bytes 524320 | tf_op jit(solution)/shard_map/ppermute | solution.py:28
  43.8 0.1 broadcast_select_fusion.5
  43.9 2.4 %collective-permute-start.7 = (bf16[64,4096]{1,0:T(8,128)(2,1)S(1)}, bf16[64,4096]{1,0:T(8,128)(2,1)S(1)}, u32[]{:S(2)}, u32[]{:S(2)}) collective-permute-start(bf16[64,4096]{1,0:T(8,128)(2,1)S(1)} %broadcast_select_fusion.5), channel_id=1, source_target_pairs={{0,1},{1,0},{2,3},{3,2},{4,5},{5,4},{6,7},{7,6},{8,9},{9,8},{10,11... | collective-permute-start | bytes 1572872 | tf_op jit(solution)/shard_map/ppermute | solution.py:28
  46.3 0.1 slice_multiply_fusion.1
  46.4 0.3 collective-permute-start.10
  46.6 3.2 %collective-permute-start.11 = (bf16[64,4096]{1,0:T(8,128)(2,1)S(1)}, bf16[64,4096]{1,0:T(8,128)(2,1)S(1)}, u32[]{:S(2)}, u32[]{:S(2)}) collective-permute-start(bf16[64,4096]{1,0:T(8,128)(2,1)S(1)} %collective-permute-done.5.refs_0_), channel_id=1, source_target_pairs={{0,4},{1,5},{4,8},{5,9},{6,2},{7,3},{8,12},{9,13},{10,6},{11,7},{1... | collective-permute-start | bytes 1572872 | tf_op jit(solution)/shard_map/ppermute | solution.py:28
  49.9 5.2 %collective-permute-done.3.refs_0_ = bf16[64,4096]{1,0:T(8,128)(2,1)S(1)} collective-permute-done((bf16[64,4096]{1,0:T(8,128)(2,1)S(1)}, bf16[64,4096]{1,0:T(8,128)(2,1)S(1)}, u32[]{:S(2)}, u32[]{:S(2)}) %collective-permute-start.3) | collective-permute-done | bytes 524320 | tf_op jit(solution)/shard_map/ppermute | solution.py:28
  55.0 0.1 broadcast_select_fusion.4
  55.1 2.4 %collective-permute-start.12 = (bf16[64,4096]{1,0:T(8,128)(2,1)S(1)}, bf16[64,4096]{1,0:T(8,128)(2,1)S(1)}, u32[]{:S(2)}, u32[]{:S(2)}) collective-permute-start(bf16[64,4096]{1,0:T(8,128)(2,1)S(1)} %broadcast_select_fusion.4), channel_id=1, source_target_pairs={{0,1},{1,0},{2,3},{3,2},{4,5},{5,4},{6,7},{7,6},{8,9},{9,8},{10,11... | collective-permute-start | bytes 1572872 | tf_op jit(solution)/shard_map/ppermute | solution.py:28
  57.5 0.1 slice_multiply_fusion.2
  57.6 0.3 collective-permute-start.8
  57.9 3.2 %collective-permute-start.9 = (bf16[64,4096]{1,0:T(8,128)(2,1)S(1)}, bf16[64,4096]{1,0:T(8,128)(2,1)S(1)}, u32[]{:S(2)}, u32[]{:S(2)}) collective-permute-start(bf16[64,4096]{1,0:T(8,128)(2,1)S(1)} %collective-permute-done.3.refs_0_), channel_id=1, source_target_pairs={{0,4},{1,5},{4,8},{5,9},{6,2},{7,3},{8,12},{9,13},{10,6},{11,7},{1... | collective-permute-start | bytes 1572872 | tf_op jit(solution)/shard_map/ppermute | solution.py:28
  61.1 2.2 %shard_map.58 = (bf16[1344,4096]{1,0:T(8,128)(2,1)S(1)}, f32[1344,384]{1,0:T(8,128)S(1)}) custom-call(bf16[384,4096]{1,0:T(8,128)(2,1)S(1)} %broadcast_multiply_fusion.own, bf16[64,4096]{1,0:T(8,128)(2,1)} %collective-permute-done.1.refs_0_, bf16[64,4096]{1,0:T(8,128)(2,1)S(1)} %collective-permute-done.6.refs_1_, ...), custom_call_target="tpu_custom_call", output_to_operand_aliasing={{0}: (4, {}), {1}: (5, {})} | custom-call | flops 603979776 | bytes 6039797 | tf_op jit(solution)/shard_map/pallas_call | solution.py:54
  63.3 2.9 %collective-permute-done.10.refs_0_ = bf16[64,4096]{1,0:T(8,128)(2,1)S(1)} collective-permute-done((bf16[64,4096]{1,0:T(8,128)(2,1)S(1)}, bf16[64,4096]{1,0:T(8,128)(2,1)S(1)}, u32[]{:S(2)}, u32[]{:S(2)}) %collective-permute-start.10) | collective-permute-done | bytes 524320 | tf_op jit(solution)/shard_map/ppermute | solution.py:28
  66.3 0.0 collective-permute-done.11.refs_1_
  66.3 0.0 collective-permute-done.12.refs_2_
  66.3 0.1 broadcast_select_fusion.3
  66.3 1.4 %collective-permute-start.13 = (bf16[64,4096]{1,0:T(8,128)(2,1)S(1)}, bf16[64,4096]{1,0:T(8,128)(2,1)S(1)}, u32[]{:S(2)}, u32[]{:S(2)}) collective-permute-start(bf16[64,4096]{1,0:T(8,128)(2,1)S(1)} %broadcast_select_fusion.3), channel_id=1, source_target_pairs={{0,1},{1,0},{2,3},{3,2},{4,5},{5,4},{6,7},{7,6},{8,9},{9,8},{10,11... | collective-permute-start | bytes 1572872 | tf_op jit(solution)/shard_map/ppermute | solution.py:28
  67.7 3.3 %collective-permute-start.18 = (bf16[64,4096]{1,0:T(8,128)(2,1)S(1)}, bf16[64,4096]{1,0:T(8,128)(2,1)S(1)}, u32[]{:S(2)}, u32[]{:S(2)}) collective-permute-start(bf16[64,4096]{1,0:T(8,128)(2,1)S(1)} %collective-permute-done.10.refs_0_), channel_id=1, source_target_pairs={{0,4},{1,5},{4,8},{5,9},{6,2},{7,3},{8,12},{9,13},{10,6},{11,7},{1... | collective-permute-start | bytes 1572872 | tf_op jit(solution)/shard_map/ppermute | solution.py:28
  71.0 2.2 %collective-permute-start.16 = (bf16[384,384]{1,0:T(8,128)(2,1)S(1)}, bf16[384,384]{1,0:T(8,128)(2,1)S(1)}, u32[]{:S(2)}, u32[]{:S(2)}) collective-permute-start(bf16[384,384]{1,0:T(8,128)(2,1)S(1)} %copy-done.7), channel_id=1, source_target_pairs={{0,1},{1,2},{2,3},{3,4},{4,5},{5,6},{6,7},{7,8},{8,9},{9,10},{10,1... | collective-permute-start | bytes 884744 | tf_op jit(solution)/shard_map/ppermute | solution.py:28
  73.3 2.2 %shard_map.59 = (bf16[1344,4096]{1,0:T(8,128)(2,1)S(1)}, f32[1344,384]{1,0:T(8,128)S(1)}) custom-call(bf16[384,4096]{1,0:T(8,128)(2,1)S(1)} %broadcast_multiply_fusion.own, bf16[64,4096]{1,0:T(8,128)(2,1)} %collective-permute-done.refs_0_, bf16[64,4096]{1,0:T(8,128)(2,1)S(1)} %collective-permute-done.4.refs_1_, ...), custom_call_target="tpu_custom_call", output_to_operand_aliasing={{0}: (4, {}), {1}: (5, {})} | custom-call | flops 603979776 | bytes 6039797 | tf_op jit(solution)/shard_map/pallas_call | solution.py:54
  75.5 5.2 %collective-permute-done.8.across = bf16[64,4096]{1,0:T(8,128)(2,1)S(1)} collective-permute-done((bf16[64,4096]{1,0:T(8,128)(2,1)S(1)}, bf16[64,4096]{1,0:T(8,128)(2,1)S(1)}, u32[]{:S(2)}, u32[]{:S(2)}) %collective-permute-start.8) | collective-permute-done | bytes 524320 | tf_op jit(solution)/shard_map/ppermute | solution.py:28
  80.7 1.9 %collective-permute-start.17 = (bf16[384,384]{1,0:T(8,128)(2,1)S(1)}, bf16[384,384]{1,0:T(8,128)(2,1)S(1)}, u32[]{:S(2)}, u32[]{:S(2)}) collective-permute-start(bf16[384,384]{1,0:T(8,128)(2,1)S(1)} %copy-done.5), channel_id=1, source_target_pairs={{0,2},{1,3},{2,4},{3,5},{4,6},{5,7},{6,8},{7,9},{8,10},{9,11},{10,... | collective-permute-start | bytes 884744 | tf_op jit(solution)/shard_map/ppermute | solution.py:28
  82.6 0.0 collective-permute-done.9.refs_1_
  82.6 0.1 broadcast_select_fusion
  82.7 0.9 collective-permute-start.20
  83.6 3.2 %collective-permute-start.14 = (bf16[64,4096]{1,0:T(8,128)(2,1)S(1)}, bf16[64,4096]{1,0:T(8,128)(2,1)S(1)}, u32[]{:S(2)}, u32[]{:S(2)}) collective-permute-start(bf16[64,4096]{1,0:T(8,128)(2,1)S(1)} %collective-permute-done.8.across), channel_id=1, source_target_pairs={{0,4},{1,5},{4,8},{5,9},{6,2},{7,3},{8,12},{9,13},{10,6},{11,7},{1... | collective-permute-start | bytes 1572872 | tf_op jit(solution)/shard_map/ppermute | solution.py:28
  86.8 0.1 broadcast_select_fusion.1
  86.9 0.4 collective-permute-start.19
  87.2 11.8 %collective-permute-done.14.onward = bf16[64,4096]{1,0:T(8,128)(2,1)S(1)} collective-permute-done((bf16[64,4096]{1,0:T(8,128)(2,1)S(1)}, bf16[64,4096]{1,0:T(8,128)(2,1)S(1)}, u32[]{:S(2)}, u32[]{:S(2)}) %collective-permute-start.14) | collective-permute-done | bytes 524320 | tf_op jit(solution)/shard_map/ppermute | solution.py:28
  99.0 0.1 broadcast_select_fusion.2
  99.1 0.9 collective-permute-start.15
  99.9 1.2 %shard_map.60 = (bf16[1344,4096]{1,0:T(8,128)(2,1)S(1)}, f32[1344,384]{1,0:T(8,128)S(1)}) custom-call(bf16[384,4096]{1,0:T(8,128)(2,1)S(1)} %broadcast_multiply_fusion.own, bf16[64,4096]{1,0:T(8,128)(2,1)S(1)} %collective-permute-done.5.refs_0_, bf16[64,4096]{1,0:T(8,128)(2,1)S(1)} %collective-permute-done.11.refs_1_, ...), custom_call_target="tpu_custom_call", output_to_operand_aliasing={{0}: (4, {}), {1}: (5, {})} | custom-call | flops 603979776 | bytes 6039797 | tf_op jit(solution)/shard_map/pallas_call | solution.py:54
  101.1 0.0 collective-permute-done.20.refs_2_
  101.1 1.2 %shard_map.61 = (bf16[1344,4096]{1,0:T(8,128)(2,1)S(1)}, f32[1344,384]{1,0:T(8,128)S(1)}) custom-call(bf16[384,4096]{1,0:T(8,128)(2,1)S(1)} %broadcast_multiply_fusion.own, bf16[64,4096]{1,0:T(8,128)(2,1)S(1)} %collective-permute-done.3.refs_0_, bf16[64,4096]{1,0:T(8,128)(2,1)S(1)} %collective-permute-done.9.refs_1_, ...), custom_call_target="tpu_custom_call", output_to_operand_aliasing={{0}: (4, {}), {1}: (5, {})} | custom-call | flops 603979776 | bytes 6039797 | tf_op jit(solution)/shard_map/pallas_call | solution.py:54
  102.3 0.0 collective-permute-done.19.refs_2_
  102.3 1.2 %shard_map.62 = (bf16[1344,4096]{1,0:T(8,128)(2,1)S(1)}, f32[1344,384]{1,0:T(8,128)S(1)}) custom-call(bf16[384,4096]{1,0:T(8,128)(2,1)S(1)} %broadcast_multiply_fusion.own, bf16[64,4096]{1,0:T(8,128)(2,1)S(1)} %collective-permute-done.10.refs_0_, bf16[64,4096]{1,0:T(8,128)(2,1)S(1)} %collective-permute-done.18.refs_1_, ...), custom_call_target="tpu_custom_call", output_to_operand_aliasing={{0}: (4, {}), {1}: (5, {})} | custom-call | flops 603979776 | bytes 6039797 | tf_op jit(solution)/shard_map/pallas_call | solution.py:54
  103.6 6.8 %shard_map.63.before = f32[384,4096]{1,0:T(8,128)S(1)} custom-call(f32[1344,384]{1,0:T(8,128)S(1)} %get-tuple-element.107.gram, bf16[1344,4096]{1,0:T(8,128)(2,1)S(1)} %get-tuple-element.108.rows, bf16[384,384]{1,0:T(8,128)(2,1)S(1)} %collective-permute-done.16.down0, ...), custom_call_target="tpu_custom_call", output_to_operand_aliasing={{}: (6, {})} | custom-call | flops 4227858432 | bytes 42278584 | tf_op jit(solution)/shard_map/pallas_call | solution.py:54
  110.4 5.0 %shard_map.64 = bf16[384,4096]{1,0:T(8,128)(2,1)} custom-call(bf16[384,4096]{1,0:T(8,128)(2,1)S(1)} %broadcast_multiply_fusion.own, bf16[64,4096]{1,0:T(8,128)(2,1)S(1)} %collective-permute-done.8.across, bf16[64,4096]{1,0:T(8,128)(2,1)S(1)} %collective-permute-done.14.onward, bf16[64,4096]{1,0:T(8,128)(2,1)S(1)} %collective-permute-done.15.swap, ...), custom_call_target="tpu_custom_call" | custom-call | flops 1207959552 | bytes 12079595 | tf_op jit(solution)/shard_map/pallas_call | solution.py:54
  (25 shorter events, 0.1 us)
Async XLA Ops:
  4.6 4.5 %copy-start.9 = (bf16[384,2,384]{2,1,0:T(2,128)(2,1)S(1)}, bf16[384,2,384]{2,1,0:T(2,128)(2,1)}, u32[]{:S(2)}) copy-start(bf16[384,2,384]{2,1,0:T(2,128)(2,1)} %param.7) | copy-start | bytes 1769476
  4.6 4.6 %copy-start.3 = (s32[1,2]{1,0:T(1,128)S(1)}, s32[1,2]{1,0:T(1,128)}, u32[]{:S(2)}) copy-start(s32[1,2]{1,0:T(1,128)} %couple.1) | copy-start | bytes 28
  6.9 11.1 %collective-permute-start.2 = (bf16[384,4096]{1,0:T(8,128)(2,1)S(1)}, bf16[384,4096]{1,0:T(8,128)(2,1)}, u32[]{:S(2)}, u32[]{:S(2)}) collective-permute-start(bf16[384,4096]{1,0:T(8,128)(2,1)S(1)} %broadcast_multiply_fusion.own), channel_id=1, source_target_pairs={{0,1},{1,0},{2,3},{3,2},{4,5},{5,4},{6,7},{7,6},{8,9},{9,8},{10,11... | collective-permute-start | bytes 9437192 | tf_op jit(solution)/shard_map/ppermute | solution.py:28
  7.6 14.2 %collective-permute-start.1 = (bf16[64,4096]{1,0:T(8,128)(2,1)}, bf16[64,4096]{1,0:T(8,128)(2,1)}, u32[]{:S(2)}, u32[]{:S(2)}) collective-permute-start(bf16[64,4096]{1,0:T(8,128)(2,1)} %slice_multiply_fusion), channel_id=1, source_target_pairs={{0,2},{1,3},{2,0},{3,1},{4,6},{5,7},{6,4},{7,5},{8,10},{9,11},{10,... | collective-permute-start | bytes 1572872 | tf_op jit(solution)/shard_map/ppermute | solution.py:28
  8.9 23.8 %collective-permute-start = (bf16[64,4096]{1,0:T(8,128)(2,1)}, bf16[64,4096]{1,0:T(8,128)(2,1)}, u32[]{:S(2)}, u32[]{:S(2)}) collective-permute-start(bf16[64,4096]{1,0:T(8,128)(2,1)} %slice_multiply_fusion.5), channel_id=1, source_target_pairs={{0,2},{1,3},{2,0},{3,1},{4,6},{5,7},{6,4},{7,5},{8,10},{9,11},{10,... | collective-permute-start | bytes 1572872 | tf_op jit(solution)/shard_map/ppermute | solution.py:28
  10.0 0.7 copy-start
  10.8 0.7 copy-start.4
  11.5 0.7 copy-start.6
  12.2 1.0 copy-start.2
  17.9 3.9 %copy-start.8 = (bf16[384,4096]{1,0:T(8,128)(2,1)S(1)}, bf16[384,4096]{1,0:T(8,128)(2,1)}, u32[]{:S(2)}) copy-start(bf16[384,4096]{1,0:T(8,128)(2,1)} %param.5) | copy-start | bytes 9437188
  21.9 21.8 %collective-permute-start.5 = (bf16[64,4096]{1,0:T(8,128)(2,1)S(1)}, bf16[64,4096]{1,0:T(8,128)(2,1)S(1)}, u32[]{:S(2)}, u32[]{:S(2)}) collective-permute-start(bf16[64,4096]{1,0:T(8,128)(2,1)S(1)} %slice_multiply_fusion.3), channel_id=1, source_target_pairs={{0,2},{1,3},{2,0},{3,1},{4,6},{5,7},{6,4},{7,5},{8,10},{9,11},{10,... | collective-permute-start | bytes 1572872 | tf_op jit(solution)/shard_map/ppermute | solution.py:28
  23.2 20.5 %collective-permute-start.6 = (bf16[64,4096]{1,0:T(8,128)(2,1)}, bf16[64,4096]{1,0:T(8,128)(2,1)S(1)}, u32[]{:S(2)}, u32[]{:S(2)}) collective-permute-start(bf16[64,4096]{1,0:T(8,128)(2,1)} %collective-permute-done.1.refs_0_), channel_id=1, source_target_pairs={{0,4},{1,5},{4,8},{5,9},{6,2},{7,3},{8,12},{9,13},{10,6},{11,7},{1... | collective-permute-start | bytes 1572872 | tf_op jit(solution)/shard_map/ppermute | solution.py:28
  32.8 22.3 %collective-permute-start.3 = (bf16[64,4096]{1,0:T(8,128)(2,1)S(1)}, bf16[64,4096]{1,0:T(8,128)(2,1)S(1)}, u32[]{:S(2)}, u32[]{:S(2)}) collective-permute-start(bf16[64,4096]{1,0:T(8,128)(2,1)S(1)} %slice_multiply_fusion.4), channel_id=1, source_target_pairs={{0,2},{1,3},{2,0},{3,1},{4,6},{5,7},{6,4},{7,5},{8,10},{9,11},{10,... | collective-permute-start | bytes 1572872 | tf_op jit(solution)/shard_map/ppermute | solution.py:28
  34.1 21.0 %collective-permute-start.4 = (bf16[64,4096]{1,0:T(8,128)(2,1)}, bf16[64,4096]{1,0:T(8,128)(2,1)S(1)}, u32[]{:S(2)}, u32[]{:S(2)}) collective-permute-start(bf16[64,4096]{1,0:T(8,128)(2,1)} %collective-permute-done.refs_0_), channel_id=1, source_target_pairs={{0,4},{1,5},{4,8},{5,9},{6,2},{7,3},{8,12},{9,13},{10,6},{11,7},{1... | collective-permute-start | bytes 1572872 | tf_op jit(solution)/shard_map/ppermute | solution.py:28
  43.9 11.2 %collective-permute-start.7 = (bf16[64,4096]{1,0:T(8,128)(2,1)S(1)}, bf16[64,4096]{1,0:T(8,128)(2,1)S(1)}, u32[]{:S(2)}, u32[]{:S(2)}) collective-permute-start(bf16[64,4096]{1,0:T(8,128)(2,1)S(1)} %broadcast_select_fusion.5), channel_id=1, source_target_pairs={{0,1},{1,0},{2,3},{3,2},{4,5},{5,4},{6,7},{7,6},{8,9},{9,8},{10,11... | collective-permute-start | bytes 1572872 | tf_op jit(solution)/shard_map/ppermute | solution.py:28
  46.4 19.9 %collective-permute-start.10 = (bf16[64,4096]{1,0:T(8,128)(2,1)S(1)}, bf16[64,4096]{1,0:T(8,128)(2,1)S(1)}, u32[]{:S(2)}, u32[]{:S(2)}) collective-permute-start(bf16[64,4096]{1,0:T(8,128)(2,1)S(1)} %slice_multiply_fusion.1), channel_id=1, source_target_pairs={{0,2},{1,3},{2,0},{3,1},{4,6},{5,7},{6,4},{7,5},{8,10},{9,11},{10,... | collective-permute-start | bytes 1572872 | tf_op jit(solution)/shard_map/ppermute | solution.py:28
  46.6 19.6 %collective-permute-start.11 = (bf16[64,4096]{1,0:T(8,128)(2,1)S(1)}, bf16[64,4096]{1,0:T(8,128)(2,1)S(1)}, u32[]{:S(2)}, u32[]{:S(2)}) collective-permute-start(bf16[64,4096]{1,0:T(8,128)(2,1)S(1)} %collective-permute-done.5.refs_0_), channel_id=1, source_target_pairs={{0,4},{1,5},{4,8},{5,9},{6,2},{7,3},{8,12},{9,13},{10,6},{11,7},{1... | collective-permute-start | bytes 1572872 | tf_op jit(solution)/shard_map/ppermute | solution.py:28
  55.1 11.2 %collective-permute-start.12 = (bf16[64,4096]{1,0:T(8,128)(2,1)S(1)}, bf16[64,4096]{1,0:T(8,128)(2,1)S(1)}, u32[]{:S(2)}, u32[]{:S(2)}) collective-permute-start(bf16[64,4096]{1,0:T(8,128)(2,1)S(1)} %broadcast_select_fusion.4), channel_id=1, source_target_pairs={{0,1},{1,0},{2,3},{3,2},{4,5},{5,4},{6,7},{7,6},{8,9},{9,8},{10,11... | collective-permute-start | bytes 1572872 | tf_op jit(solution)/shard_map/ppermute | solution.py:28
  57.6 13.4 %copy-start.7 = (bf16[384,384]{1,0:T(8,128)(2,1)S(1)}, bf16[384,384]{1,0:T(8,128)(2,1)}, u32[]{:S(2)}) copy-start(bf16[384,384]{1,0:T(8,128)(2,1)} %copy-done.6) | copy-start | bytes 884740
  57.6 23.0 %collective-permute-start.8 = (bf16[64,4096]{1,0:T(8,128)(2,1)S(1)}, bf16[64,4096]{1,0:T(8,128)(2,1)S(1)}, u32[]{:S(2)}, u32[]{:S(2)}) collective-permute-start(bf16[64,4096]{1,0:T(8,128)(2,1)S(1)} %slice_multiply_fusion.2), channel_id=1, source_target_pairs={{0,2},{1,3},{2,0},{3,1},{4,6},{5,7},{6,4},{7,5},{8,10},{9,11},{10,... | collective-permute-start | bytes 1572872 | tf_op jit(solution)/shard_map/ppermute | solution.py:28
  57.9 24.7 %collective-permute-start.9 = (bf16[64,4096]{1,0:T(8,128)(2,1)S(1)}, bf16[64,4096]{1,0:T(8,128)(2,1)S(1)}, u32[]{:S(2)}, u32[]{:S(2)}) collective-permute-start(bf16[64,4096]{1,0:T(8,128)(2,1)S(1)} %collective-permute-done.3.refs_0_), channel_id=1, source_target_pairs={{0,4},{1,5},{4,8},{5,9},{6,2},{7,3},{8,12},{9,13},{10,6},{11,7},{1... | collective-permute-start | bytes 1572872 | tf_op jit(solution)/shard_map/ppermute | solution.py:28
  66.3 16.3 %collective-permute-start.13 = (bf16[64,4096]{1,0:T(8,128)(2,1)S(1)}, bf16[64,4096]{1,0:T(8,128)(2,1)S(1)}, u32[]{:S(2)}, u32[]{:S(2)}) collective-permute-start(bf16[64,4096]{1,0:T(8,128)(2,1)S(1)} %broadcast_select_fusion.3), channel_id=1, source_target_pairs={{0,1},{1,0},{2,3},{3,2},{4,5},{5,4},{6,7},{7,6},{8,9},{9,8},{10,11... | collective-permute-start | bytes 1572872 | tf_op jit(solution)/shard_map/ppermute | solution.py:28
  67.7 13.0 %copy-start.5 = (bf16[384,384]{1,0:T(8,128)(2,1)S(1)}, bf16[384,384]{1,0:T(8,128)(2,1)}, u32[]{:S(2)}) copy-start(bf16[384,384]{1,0:T(8,128)(2,1)} %copy-done.4) | copy-start | bytes 884740
  67.7 19.1 %collective-permute-start.18 = (bf16[64,4096]{1,0:T(8,128)(2,1)S(1)}, bf16[64,4096]{1,0:T(8,128)(2,1)S(1)}, u32[]{:S(2)}, u32[]{:S(2)}) collective-permute-start(bf16[64,4096]{1,0:T(8,128)(2,1)S(1)} %collective-permute-done.10.refs_0_), channel_id=1, source_target_pairs={{0,4},{1,5},{4,8},{5,9},{6,2},{7,3},{8,12},{9,13},{10,6},{11,7},{1... | collective-permute-start | bytes 1572872 | tf_op jit(solution)/shard_map/ppermute | solution.py:28
  71.0 32.5 %collective-permute-start.16 = (bf16[384,384]{1,0:T(8,128)(2,1)S(1)}, bf16[384,384]{1,0:T(8,128)(2,1)S(1)}, u32[]{:S(2)}, u32[]{:S(2)}) collective-permute-start(bf16[384,384]{1,0:T(8,128)(2,1)S(1)} %copy-done.7), channel_id=1, source_target_pairs={{0,1},{1,2},{2,3},{3,4},{4,5},{5,6},{6,7},{7,8},{8,9},{9,10},{10,1... | collective-permute-start | bytes 884744 | tf_op jit(solution)/shard_map/ppermute | solution.py:28
  80.7 22.9 %collective-permute-start.17 = (bf16[384,384]{1,0:T(8,128)(2,1)S(1)}, bf16[384,384]{1,0:T(8,128)(2,1)S(1)}, u32[]{:S(2)}, u32[]{:S(2)}) collective-permute-start(bf16[384,384]{1,0:T(8,128)(2,1)S(1)} %copy-done.5), channel_id=1, source_target_pairs={{0,2},{1,3},{2,4},{3,5},{4,6},{5,7},{6,8},{7,9},{8,10},{9,11},{10,... | collective-permute-start | bytes 884744 | tf_op jit(solution)/shard_map/ppermute | solution.py:28
  82.7 18.5 %collective-permute-start.20 = (bf16[64,4096]{1,0:T(8,128)(2,1)S(1)}, bf16[64,4096]{1,0:T(8,128)(2,1)S(1)}, u32[]{:S(2)}, u32[]{:S(2)}) collective-permute-start(bf16[64,4096]{1,0:T(8,128)(2,1)S(1)} %broadcast_select_fusion), channel_id=1, source_target_pairs={{0,1},{1,0},{2,3},{3,2},{4,5},{5,4},{6,7},{7,6},{8,9},{9,8},{10,11... | collective-permute-start | bytes 1572872 | tf_op jit(solution)/shard_map/ppermute | solution.py:28
  83.6 15.4 %collective-permute-start.14 = (bf16[64,4096]{1,0:T(8,128)(2,1)S(1)}, bf16[64,4096]{1,0:T(8,128)(2,1)S(1)}, u32[]{:S(2)}, u32[]{:S(2)}) collective-permute-start(bf16[64,4096]{1,0:T(8,128)(2,1)S(1)} %collective-permute-done.8.across), channel_id=1, source_target_pairs={{0,4},{1,5},{4,8},{5,9},{6,2},{7,3},{8,12},{9,13},{10,6},{11,7},{1... | collective-permute-start | bytes 1572872 | tf_op jit(solution)/shard_map/ppermute | solution.py:28
  86.9 15.5 %collective-permute-start.19 = (bf16[64,4096]{1,0:T(8,128)(2,1)S(1)}, bf16[64,4096]{1,0:T(8,128)(2,1)S(1)}, u32[]{:S(2)}, u32[]{:S(2)}) collective-permute-start(bf16[64,4096]{1,0:T(8,128)(2,1)S(1)} %broadcast_select_fusion.1), channel_id=1, source_target_pairs={{0,1},{1,0},{2,3},{3,2},{4,5},{5,4},{6,7},{7,6},{8,9},{9,8},{10,11... | collective-permute-start | bytes 1572872 | tf_op jit(solution)/shard_map/ppermute | solution.py:28
  99.1 11.4 %collective-permute-start.15 = (bf16[64,4096]{1,0:T(8,128)(2,1)S(1)}, bf16[64,4096]{1,0:T(8,128)(2,1)S(1)}, u32[]{:S(2)}, u32[]{:S(2)}) collective-permute-start(bf16[64,4096]{1,0:T(8,128)(2,1)S(1)} %broadcast_select_fusion.2), channel_id=1, source_target_pairs={{0,1},{1,0},{2,3},{3,2},{4,5},{5,4},{6,7},{7,6},{8,9},{9,8},{10,11... | collective-permute-start | bytes 1572872 | tf_op jit(solution)/shard_map/ppermute | solution.py:28
  102.3 1.2 %copy-start.1 = (bf16[384,384]{1,0:T(8,128)(2,1)S(1)}, bf16[384,384]{1,0:T(8,128)(2,1)}, u32[]{:S(2)}) copy-start(bf16[384,384]{1,0:T(8,128)(2,1)} %copy-done) | copy-start | bytes 884740

commit v3 on v2

--- a/solution.py
+++ b/solution.py
@@ -10,7 +10,8 @@
 CUTS = (64,) * 6
 KAT = 5
 LAG = 3
-TILE = 512
+HOLD = 2
+TILE = 1024
 MIB = 2**20
 
 
@@ -45,17 +46,19 @@
         body(pl.ds(pl.multiple_of(i * TILE, TILE), TILE))
         return carry
 
-    lax.fori_loop(0, width // TILE, step, 0)
-
-
-def call(body, out, args, scratch=(), smem=0, aliases=None, limit=16, flops=0):
-    held = [pltpu.with_memory_space_constraint(a, pltpu.VMEM) for a in args[: len(args) - smem]]
+    lax.fori_loop(0, width // TILE, step, 0, unroll=True)
+
+
+def call(body, out, args, scratch=(), smem=0, hbm=0, out_hbm=False, aliases=None, limit=16, flops=0):
+    vectors = args[hbm : len(args) - smem]
+    held = [*(pltpu.with_memory_space_constraint(a, pltpu.HBM) for a in args[:hbm]), *(pltpu.with_memory_space_constraint(a, pltpu.VMEM) for a in vectors)]
     vector, scalar = pl.BlockSpec(memory_space=pltpu.VMEM), pl.BlockSpec(memory_space=pltpu.SMEM)
+    anywhere = pl.BlockSpec(memory_space=pl.ANY)
     return pl.pallas_call(
         body,
         out_shape=out,
-        in_specs=[vector] * len(held) + [scalar] * smem,
-        out_specs=jax.tree.map(lambda _: vector, out),
+        in_specs=[anywhere] * hbm + [vector] * len(vectors) + [scalar] * smem,
+        out_specs=jax.tree.map(lambda _: anywhere if out_hbm else vector, out),
         input_output_aliases=aliases or {},
         scratch_shapes=list(scratch),
         compiler_params=pltpu.CompilerParams(vmem_limit_bytes=limit * MIB),
@@ -119,19 +122,24 @@
     tiles(total.shape[1], tile)
 
 
-def last_body(span, own, across, onward, swap, down0, down1, up0, up1, before, place, out, rows, weights):
+def last_body(span, n, own, *refs):
+    pieces = refs[:n]
+    down0, down1, up0, up1, before, place, out, rows, weights, ready, done = refs[n:]
     at = 0
-    for piece in (across, onward, swap):
+    for piece in pieces:
         rows[at : at + piece.shape[0], :] = piece[...]
         at += piece.shape[0]
     kern = jnp.concatenate(chosen(place[0], (down0, down1), (up0, up1), span))
     weights[...] = weigh(kern, grams(rows[...], own[...])).T.astype(weights.dtype)
-
-    def tile(cols):
+    copies = []
+    for i in range(out.shape[1] // TILE):
+        cols = slice(i * TILE, (i + 1) * TILE)
         part = jnp.dot(weights[...], rows[:, cols], preferred_element_type=jnp.float32)
-        out[:, cols] = (-(before[:, cols] + part)).astype(out.dtype)
-
-    tiles(out.shape[1], tile)
+        ready[:, cols] = (-(before[:, cols] + part)).astype(ready.dtype)
+        copies.append(pltpu.make_async_copy(ready.at[:, cols], out.at[:, cols], done.at[i]))
+        copies[-1].start()
+    for copy in copies:
+        copy.wait()
 
 
 def on_device(orbitals, kern_diag, kern_near, couple, tally):
@@ -179,7 +187,7 @@
         scratch=[pltpu.VMEM((height, height), kind)], flops=4 * height * height * width,
     )
 
-    depth = height + 3 * (height - CUTS[-1])
+    depth = height + 3 * (height - sum(CUTS[-HOLD:]))
 
     def collect(base, pieces):
         state = [held[n] for n in ("rows", "gram") if n in held]
@@ -194,41 +202,59 @@
 
     collect(0, [after(beside, held["total"])])
     join(("across", 0), "rows", "gram")
-    for w in range(1, last + 5):
+    def swap(i):
+        held["swap", i] = send(jnp.where(mixed, held["across", i], held["onward", i]), sibling)
+
+    def collected(i):
+        collect(height + 3 * spans[i].start, pieces(i))
+
+    swaps = collects = 0
+    for w in range(1, last + 1):
         now = held["rows"]
         if w + 1 <= last:
             held["across", w + 1] = send(part(w + 1, now), across)
-        if w - 1 <= last:
-            held["onward", w - 1] = send(held["across", w - 1], onward)
+        held["onward", w - 1] = send(held["across", w - 1], onward)
         if w == KAT:
             for o, down in enumerate((down0, down1)):
                 pairs = [(i, i + o + 1) for i in range(peers - o - 1)]
                 held["down", o] = send(after(down, now), pairs)
-        i = w - LAG
-        if 0 <= i <= last:
-            held["swap", i] = send(jnp.where(mixed, held["across", i], held["onward", i]), sibling)
-        i -= 1
-        if 0 <= i < last:
-            collect(height + 3 * spans[i].start, pieces(i))
-        if w <= last:
-            join(("across", w), ("onward", w - LAG + 1), ("swap", w - LAG), "rows", "gram")
-    downs = [held["down", o] for o in range(2)]
-    state = held["rows"], held["gram"]
-    total = held["total"]
-    from_across, from_onward, swapped = ({last: piece} for piece in pieces(last))
-    rows, gram = state
-    kerns = [*downs, up0, up1]
-    total = call(
-        functools.partial(product_body, spans[:last]), pltpu.VMEM((height, width), jnp.float32),
-        [gram, rows, *kerns, total, place], smem=1, aliases={6: 0},
+        if w >= LAG:
+            swap(w - LAG)
+        if w >= LAG + 1:
+            collected(w - LAG - 1)
+        join(("across", w), ("onward", w - LAG + 1), ("swap", w - LAG), "rows", "gram")
+    held["onward", last] = send(held["across", last], onward)
+    if KAT > last:
+        for o, down in enumerate((down0, down1)):
+            pairs = [(i, i + o + 1) for i in range(peers - o - 1)]
+            held["down", o] = send(after(down, held["rows"]), pairs)
+    kept = last + 1 - HOLD
+    for i in range(last - LAG + 1, kept):
+        swap(i)
+    join(("onward", last - 1), "rows", "gram")
+    for i in range(last - LAG, kept):
+        collected(i)
+    gate = [("onward", i) for i in range(kept, last + 1)]
+    join(*gate, "rows", "gram", ("down", 0), ("down", 1))
+    for i in range(kept, last + 1):
+        swap(i)
+    kerns = [held["down", 0], held["down", 1], up0, up1]
+    held["total"] = call(
+        functools.partial(product_body, spans[:kept]), pltpu.VMEM((height, width), jnp.float32),
+        [held["gram"], held["rows"], *kerns, held["total"], place], smem=1, aliases={6: 0},
         scratch=[pltpu.VMEM((depth, height), kind)], flops=2 * depth * height * width,
     )
-    count = 3 * CUTS[-1]
+    count = 3 * (height - spans[kept].start)
+    final = [held[n, i] for n in ("across", "onward", "swap") for i in range(kept, last + 1)]
     return call(
-        functools.partial(last_body, spans[last]), jax.ShapeDtypeStruct((height, width), kind),
-        [own, from_across[last], from_onward[last], swapped[last], *kerns, total, place], smem=1,
-        scratch=[pltpu.VMEM((count, width), kind), pltpu.VMEM((height, count), kind)],
-        flops=4 * count * height * width,
+        functools.partial(last_body, slice(spans[kept].start, height), len(final)),
+        jax.ShapeDtypeStruct((height, width), kind),
+        [own, *final, *kerns, held["total"], place], smem=1, out_hbm=True,
+        scratch=[
+            pltpu.VMEM((count, width), kind), pltpu.VMEM((height, count), kind), pltpu.VMEM((height, width), kind),
+            pltpu.SemaphoreType.DMA((width // TILE,)),
+        ],
+        limit=16, flops=4 * count * height * width,
     )
 
 

time: 118 us -> 107 us (0.907); the launches traced: 115 us -> 107 us
  waiting for transfers between devices: 37.8 us -> 32.1 us
  Pallas kernels: 29.2 us -> 24.3 us
  starting transfers between devices: 37.1 us -> 39 us
    ppermute x21, waiting for transfers between devices: 37.8 us -> 32.1 us  [send(): return lax.ppermute(array, 'pts', pairs)]
    pallas_call x10 -> x9, Pallas kernels: 29.2 us -> 24.3 us  [call(): pl.pallas_call(body, out_shape=out, in_specs=[anywhere] * hbm + [vector]...]
    ppermute x21, starting transfers between devices: 37.1 us -> 39 us  [send(): return lax.ppermute(array, 'pts', pairs)]
  transfers between devices with their start and end apart: 21 -> 21, of which waited for: 6 -> 7; matrix products, arithmetic and copies ran while one was open for 1% -> 1% of each run, Pallas kernels for 21% -> 18%
where the time goes in v3:
time: 107 us
  starting transfers between devices  39 us (36%)
  waiting for transfers between devices  32.1 us (30%)
  Pallas kernels  24.3 us (23%)
  other arithmetic  6.92 us (6%)
  local copies, waits for them, and re-layouts  3.37 us (3%)
  between operations  1.12 us (1%)
    ppermute x21, starting transfers between devices, send(): return lax.ppermute(array, 'pts', pairs)  39 us
    ppermute x21, waiting for transfers between devices, send(): return lax.ppermute(array, 'pts', pairs)  32.1 us
    pallas_call x9, Pallas kernels, call(): pl.pallas_call(body, out_shape=out, in_specs=[anywhere] * hbm + [vector]...  24.3 us
    mul x6, other arithmetic, part(): return after(orbitals, *gates)[spans[j]] * valid[spans[j]]  4.3 us
    unnamed x20, local copies, waits for them, and re-layouts  3.16 us
    mul x1, other arithmetic, on_device(): own = after(orbitals, second) * valid  2.22 us
  transfers between devices with their start and end apart: 21, of which 7 were waited for; matrix products, arithmetic and copies ran while one was open for 1% of the time, Pallas kernels for 18%

profile of v3, /device:TPU:11, one launch (start us, length us, event | category | flops | bytes accessed | tf_op | source)
XLA Modules:
  0.0 106.8 jit_solution(15110226712723913713)
XLA Ops:
  0.7 0.1 fusion.1
  0.7 1.9 %slice_multiply_fusion = bf16[64,4096]{1,0:T(8,128)(2,1)} fusion(bf16[384,4096]{1,0:T(8,128)(2,1)} %param.5, bf16[64]{0:T(256)(128)(2,1)S(1)} %get-tuple-element.130), kind=kLoop, calls=%fused_computation.1 | loop fusion | flops 262144 | bytes 1048704 | tf_op jit(solution)/shard_map/mul | solution.py:169
  2.7 1.9 %slice_multiply_fusion.5 = bf16[64,4096]{1,0:T(8,128)(2,1)} fusion(bf16[384,4096]{1,0:T(8,128)(2,1)} %param.5, bf16[64]{0:T(256)(128)(2,1)S(1)} %get-tuple-element.129), kind=kLoop, calls=%fused_computation.6 | loop fusion | flops 262144 | bytes 1048704 | tf_op jit(solution)/shard_map/mul | solution.py:169
  4.6 2.2 %broadcast_multiply_fusion.own = bf16[384,4096]{1,0:T(8,128)(2,1)S(1)} fusion(bf16[384,4096]{1,0:T(8,128)(2,1)} %param.5, bf16[384]{0:T(512)(128)(2,1)S(1)} %fusion), kind=kLoop, calls=%fused_computation | loop fusion | flops 1572864 | bytes 6292224 | tf_op jit(solution)/shard_map/mul | solution.py:178
  6.9 0.7 collective-permute-start.1
  7.6 1.3 %collective-permute-start = (bf16[64,4096]{1,0:T(8,128)(2,1)}, bf16[64,4096]{1,0:T(8,128)(2,1)}, u32[]{:S(2)}, u32[]{:S(2)}) collective-permute-start(bf16[64,4096]{1,0:T(8,128)(2,1)} %slice_multiply_fusion), channel_id=1, source_target_pairs={{0,2},{1,3},{2,0},{3,1},{4,6},{5,7},{6,4},{7,5},{8,10},{9,11},{10,... | collective-permute-start | bytes 1572872 | tf_op jit(solution)/shard_map/ppermute | solution.py:29
  8.8 0.2 collective-permute-start.4
  9.1 0.1 copy.15
  9.2 0.1 slice_bitcast_fusion
  9.2 0.8 shard_map.55
  10.0 0.7 copy-done
  10.8 0.7 copy-done.4
  11.5 0.7 copy-done.6
  12.2 1.0 copy-done.2
  13.2 3.5 %shard_map.56.before = f32[384,4096]{1,0:T(8,128)S(1)} custom-call(bf16[384,4096]{1,0:T(8,128)(2,1)S(1)} %broadcast_multiply_fusion.own, bf16[384,384]{1,0:T(8,128)(2,1)S(1)} %copy-done.2), custom_call_target="tpu_custom_call" | custom-call | flops 2415919104 | bytes 24159192 | tf_op jit(solution)/shard_map/pallas_call | solution.py:57
  16.7 0.0 copy-start.8
  16.7 3.8 %shard_map.57 = (bf16[1152,4096]{1,0:T(8,128)(2,1)S(1)}, f32[1152,384]{1,0:T(8,128)S(1)}) custom-call(bf16[384,4096]{1,0:T(8,128)(2,1)S(1)} %broadcast_multiply_fusion.own, bf16[384,4096]{1,0:T(8,128)(2,1)} %collective-permute-done.1.refs_0_), custom_call_target="tpu_custom_call" | custom-call | flops 1207959552 | bytes 12079595 | tf_op jit(solution)/shard_map/pallas_call | solution.py:57
  20.6 0.9 collective-permute-done.refs_0_
  21.4 0.1 slice_multiply_fusion.4
  21.5 1.3 %collective-permute-start.2 = (bf16[64,4096]{1,0:T(8,128)(2,1)S(1)}, bf16[64,4096]{1,0:T(8,128)(2,1)S(1)}, u32[]{:S(2)}, u32[]{:S(2)}) collective-permute-start(bf16[64,4096]{1,0:T(8,128)(2,1)S(1)} %slice_multiply_fusion.4), channel_id=1, source_target_pairs={{0,2},{1,3},{2,0},{3,1},{4,6},{5,7},{6,4},{7,5},{8,10},{9,11},{10,... | collective-permute-start | bytes 1572872 | tf_op jit(solution)/shard_map/ppermute | solution.py:29
  22.8 3.2 %collective-permute-start.3 = (bf16[64,4096]{1,0:T(8,128)(2,1)}, bf16[64,4096]{1,0:T(8,128)(2,1)S(1)}, u32[]{:S(2)}, u32[]{:S(2)}) collective-permute-start(bf16[64,4096]{1,0:T(8,128)(2,1)} %collective-permute-done.refs_0_), channel_id=1, source_target_pairs={{0,4},{1,5},{4,8},{5,9},{6,2},{7,3},{8,12},{9,13},{10,6},{11,7},{1... | collective-permute-start | bytes 1572872 | tf_op jit(solution)/shard_map/ppermute | solution.py:29
  26.0 6.6 %collective-permute-done.4.refs_0_ = bf16[64,4096]{1,0:T(8,128)(2,1)} collective-permute-done((bf16[64,4096]{1,0:T(8,128)(2,1)}, bf16[64,4096]{1,0:T(8,128)(2,1)}, u32[]{:S(2)}, u32[]{:S(2)}) %collective-permute-start.4) | collective-permute-done | bytes 524320 | tf_op jit(solution)/shard_map/ppermute | solution.py:29
  32.6 0.1 slice_multiply_fusion.2
  32.8 1.3 %collective-permute-start.7 = (bf16[64,4096]{1,0:T(8,128)(2,1)S(1)}, bf16[64,4096]{1,0:T(8,128)(2,1)S(1)}, u32[]{:S(2)}, u32[]{:S(2)}) collective-permute-start(bf16[64,4096]{1,0:T(8,128)(2,1)S(1)} %slice_multiply_fusion.2), channel_id=1, source_target_pairs={{0,2},{1,3},{2,0},{3,1},{4,6},{5,7},{6,4},{7,5},{8,10},{9,11},{10,... | collective-permute-start | bytes 1572872 | tf_op jit(solution)/shard_map/ppermute | solution.py:29
  34.1 3.2 %collective-permute-start.8 = (bf16[64,4096]{1,0:T(8,128)(2,1)}, bf16[64,4096]{1,0:T(8,128)(2,1)S(1)}, u32[]{:S(2)}, u32[]{:S(2)}) collective-permute-start(bf16[64,4096]{1,0:T(8,128)(2,1)} %collective-permute-done.4.refs_0_), channel_id=1, source_target_pairs={{0,4},{1,5},{4,8},{5,9},{6,2},{7,3},{8,12},{9,13},{10,6},{11,7},{1... | collective-permute-start | bytes 1572872 | tf_op jit(solution)/shard_map/ppermute | solution.py:29
  37.3 6.5 %collective-permute-done.2.refs_0_ = bf16[64,4096]{1,0:T(8,128)(2,1)S(1)} collective-permute-done((bf16[64,4096]{1,0:T(8,128)(2,1)S(1)}, bf16[64,4096]{1,0:T(8,128)(2,1)S(1)}, u32[]{:S(2)}, u32[]{:S(2)}) %collective-permute-start.2) | collective-permute-done | bytes 524320 | tf_op jit(solution)/shard_map/ppermute | solution.py:29
  43.8 0.0 collective-permute-done.3.refs_1_
  43.8 0.1 broadcast_select_fusion.5
  43.9 2.4 %collective-permute-start.9 = (bf16[64,4096]{1,0:T(8,128)(2,1)S(1)}, bf16[64,4096]{1,0:T(8,128)(2,1)S(1)}, u32[]{:S(2)}, u32[]{:S(2)}) collective-permute-start(bf16[64,4096]{1,0:T(8,128)(2,1)S(1)} %broadcast_select_fusion.5), channel_id=1, source_target_pairs={{0,1},{1,0},{2,3},{3,2},{4,5},{5,4},{6,7},{7,6},{8,9},{9,8},{10,11... | collective-permute-start | bytes 1572872 | tf_op jit(solution)/shard_map/ppermute | solution.py:29
  46.3 0.1 slice_multiply_fusion.3
  46.4 0.3 collective-permute-start.5
  46.6 3.2 %collective-permute-start.6 = (bf16[64,4096]{1,0:T(8,128)(2,1)S(1)}, bf16[64,4096]{1,0:T(8,128)(2,1)S(1)}, u32[]{:S(2)}, u32[]{:S(2)}) collective-permute-start(bf16[64,4096]{1,0:T(8,128)(2,1)S(1)} %collective-permute-done.2.refs_0_), channel_id=1, source_target_pairs={{0,4},{1,5},{4,8},{5,9},{6,2},{7,3},{8,12},{9,13},{10,6},{11,7},{1... | collective-permute-start | bytes 1572872 | tf_op jit(solution)/shard_map/ppermute | solution.py:29
  49.8 5.2 %collective-permute-done.7.refs_0_ = bf16[64,4096]{1,0:T(8,128)(2,1)S(1)} collective-permute-done((bf16[64,4096]{1,0:T(8,128)(2,1)S(1)}, bf16[64,4096]{1,0:T(8,128)(2,1)S(1)}, u32[]{:S(2)}, u32[]{:S(2)}) %collective-permute-start.7) | collective-permute-done | bytes 524320 | tf_op jit(solution)/shard_map/ppermute | solution.py:29
  55.0 0.0 collective-permute-done.8.refs_1_
  55.0 0.0 collective-permute-done.9.refs_2_
  55.0 0.1 broadcast_select_fusion.4
  55.1 2.4 %collective-permute-start.10 = (bf16[64,4096]{1,0:T(8,128)(2,1)S(1)}, bf16[64,4096]{1,0:T(8,128)(2,1)S(1)}, u32[]{:S(2)}, u32[]{:S(2)}) collective-permute-start(bf16[64,4096]{1,0:T(8,128)(2,1)S(1)} %broadcast_select_fusion.4), channel_id=1, source_target_pairs={{0,1},{1,0},{2,3},{3,2},{4,5},{5,4},{6,7},{7,6},{8,9},{9,8},{10,11... | collective-permute-start | bytes 1572872 | tf_op jit(solution)/shard_map/ppermute | solution.py:29
  57.5 0.1 slice_multiply_fusion.1
  57.6 0.3 collective-permute-start.11
  57.9 3.2 %collective-permute-start.12 = (bf16[64,4096]{1,0:T(8,128)(2,1)S(1)}, bf16[64,4096]{1,0:T(8,128)(2,1)S(1)}, u32[]{:S(2)}, u32[]{:S(2)}) collective-permute-start(bf16[64,4096]{1,0:T(8,128)(2,1)S(1)} %collective-permute-done.7.refs_0_), channel_id=1, source_target_pairs={{0,4},{1,5},{4,8},{5,9},{6,2},{7,3},{8,12},{9,13},{10,6},{11,7},{1... | collective-permute-start | bytes 1572872 | tf_op jit(solution)/shard_map/ppermute | solution.py:29
  61.1 2.2 %shard_map.58 = (bf16[1152,4096]{1,0:T(8,128)(2,1)S(1)}, f32[1152,384]{1,0:T(8,128)S(1)}) custom-call(bf16[384,4096]{1,0:T(8,128)(2,1)S(1)} %broadcast_multiply_fusion.own, bf16[64,4096]{1,0:T(8,128)(2,1)} %collective-permute-done.refs_0_, bf16[64,4096]{1,0:T(8,128)(2,1)S(1)} %collective-permute-done.3.refs_1_, ...), custom_call_target="tpu_custom_call", output_to_operand_aliasing={{0}: (4, {}), {1}: (5, {})} | custom-call | flops 603979776 | bytes 6039797 | tf_op jit(solution)/shard_map/pallas_call | solution.py:57
  63.3 2.9 %collective-permute-done.5.refs_0_ = bf16[64,4096]{1,0:T(8,128)(2,1)S(1)} collective-permute-done((bf16[64,4096]{1,0:T(8,128)(2,1)S(1)}, bf16[64,4096]{1,0:T(8,128)(2,1)S(1)}, u32[]{:S(2)}, u32[]{:S(2)}) %collective-permute-start.5) | collective-permute-done | bytes 524320 | tf_op jit(solution)/shard_map/ppermute | solution.py:29
  66.3 0.1 broadcast_select_fusion.3
  66.3 1.4 %collective-permute-start.13 = (bf16[64,4096]{1,0:T(8,128)(2,1)S(1)}, bf16[64,4096]{1,0:T(8,128)(2,1)S(1)}, u32[]{:S(2)}, u32[]{:S(2)}) collective-permute-start(bf16[64,4096]{1,0:T(8,128)(2,1)S(1)} %broadcast_select_fusion.3), channel_id=1, source_target_pairs={{0,1},{1,0},{2,3},{3,2},{4,5},{5,4},{6,7},{7,6},{8,9},{9,8},{10,11... | collective-permute-start | bytes 1572872 | tf_op jit(solution)/shard_map/ppermute | solution.py:29
  67.7 3.3 %collective-permute-start.14 = (bf16[64,4096]{1,0:T(8,128)(2,1)S(1)}, bf16[64,4096]{1,0:T(8,128)(2,1)S(1)}, u32[]{:S(2)}, u32[]{:S(2)}) collective-permute-start(bf16[64,4096]{1,0:T(8,128)(2,1)S(1)} %collective-permute-done.5.refs_0_), channel_id=1, source_target_pairs={{0,4},{1,5},{4,8},{5,9},{6,2},{7,3},{8,12},{9,13},{10,6},{11,7},{1... | collective-permute-start | bytes 1572872 | tf_op jit(solution)/shard_map/ppermute | solution.py:29
  71.0 2.2 %shard_map.59 = (bf16[1152,4096]{1,0:T(8,128)(2,1)S(1)}, f32[1152,384]{1,0:T(8,128)S(1)}) custom-call(bf16[384,4096]{1,0:T(8,128)(2,1)S(1)} %broadcast_multiply_fusion.own, bf16[64,4096]{1,0:T(8,128)(2,1)} %collective-permute-done.4.refs_0_, bf16[64,4096]{1,0:T(8,128)(2,1)S(1)} %collective-permute-done.8.refs_1_, ...), custom_call_target="tpu_custom_call", output_to_operand_aliasing={{0}: (4, {}), {1}: (5, {})} | custom-call | flops 603979776 | bytes 6039797 | tf_op jit(solution)/shard_map/pallas_call | solution.py:57
  73.3 4.2 %collective-permute-done.11.refs_1_ = bf16[64,4096]{1,0:T(8,128)(2,1)S(1)} collective-permute-done((bf16[64,4096]{1,0:T(8,128)(2,1)S(1)}, bf16[64,4096]{1,0:T(8,128)(2,1)S(1)}, u32[]{:S(2)}, u32[]{:S(2)}) %collective-permute-start.11) | collective-permute-done | bytes 524320 | tf_op jit(solution)/shard_map/ppermute | solution.py:29
  77.5 0.1 broadcast_select_fusion.2
  77.6 0.9 collective-permute-start.16
  78.5 3.2 %collective-permute-start.15 = (bf16[64,4096]{1,0:T(8,128)(2,1)S(1)}, bf16[64,4096]{1,0:T(8,128)(2,1)S(1)}, u32[]{:S(2)}, u32[]{:S(2)}) collective-permute-start(bf16[64,4096]{1,0:T(8,128)(2,1)S(1)} %collective-permute-done.11.refs_1_), channel_id=1, source_target_pairs={{0,4},{1,5},{4,8},{5,9},{6,2},{7,3},{8,12},{9,13},{10,6},{11,7},{1... | collective-permute-start | bytes 1572872 | tf_op jit(solution)/shard_map/ppermute | solution.py:29
  81.7 2.2 %collective-permute-start.17 = (bf16[384,384]{1,0:T(8,128)(2,1)S(1)}, bf16[384,384]{1,0:T(8,128)(2,1)S(1)}, u32[]{:S(2)}, u32[]{:S(2)}) collective-permute-start(bf16[384,384]{1,0:T(8,128)(2,1)S(1)} %copy-done.7), channel_id=1, source_target_pairs={{0,1},{1,2},{2,3},{3,4},{4,5},{5,6},{6,7},{7,8},{8,9},{9,10},{10,1... | collective-permute-start | bytes 884744 | tf_op jit(solution)/shard_map/ppermute | solution.py:29
  83.9 4.5 %collective-permute-start.18 = (bf16[384,384]{1,0:T(8,128)(2,1)S(1)}, bf16[384,384]{1,0:T(8,128)(2,1)S(1)}, u32[]{:S(2)}, u32[]{:S(2)}) collective-permute-start(bf16[384,384]{1,0:T(8,128)(2,1)S(1)} %copy-done.5), channel_id=1, source_target_pairs={{0,2},{1,3},{2,4},{3,5},{4,6},{5,7},{6,8},{7,9},{8,10},{9,11},{10,... | collective-permute-start | bytes 884744 | tf_op jit(solution)/shard_map/ppermute | solution.py:29
  88.4 0.0 collective-permute-done.14.refs_2_
  88.4 1.2 %shard_map.60 = (bf16[1152,4096]{1,0:T(8,128)(2,1)S(1)}, f32[1152,384]{1,0:T(8,128)S(1)}) custom-call(bf16[384,4096]{1,0:T(8,128)(2,1)S(1)} %broadcast_multiply_fusion.own, bf16[64,4096]{1,0:T(8,128)(2,1)S(1)} %collective-permute-done.2.refs_0_, bf16[64,4096]{1,0:T(8,128)(2,1)S(1)} %collective-permute-done.6.refs_1_, ...), custom_call_target="tpu_custom_call", output_to_operand_aliasing={{0}: (4, {}), {1}: (5, {})} | custom-call | flops 603979776 | bytes 6039797 | tf_op jit(solution)/shard_map/pallas_call | solution.py:57
  89.6 0.0 collective-permute-done.16.refs_2_
  89.6 1.2 %shard_map.61 = (bf16[1152,4096]{1,0:T(8,128)(2,1)S(1)}, f32[1152,384]{1,0:T(8,128)S(1)}) custom-call(bf16[384,4096]{1,0:T(8,128)(2,1)S(1)} %broadcast_multiply_fusion.own, bf16[64,4096]{1,0:T(8,128)(2,1)S(1)} %collective-permute-done.7.refs_0_, bf16[64,4096]{1,0:T(8,128)(2,1)S(1)} %collective-permute-done.12.refs_1_, ...), custom_call_target="tpu_custom_call", output_to_operand_aliasing={{0}: (4, {}), {1}: (5, {})} | custom-call | flops 603979776 | bytes 6039797 | tf_op jit(solution)/shard_map/pallas_call | solution.py:57
  90.8 5.8 %collective-permute-done.18.down1.refs_7_ = bf16[384,384]{1,0:T(8,128)(2,1)S(1)} collective-permute-done((bf16[384,384]{1,0:T(8,128)(2,1)S(1)}, bf16[384,384]{1,0:T(8,128)(2,1)S(1)}, u32[]{:S(2)}, u32[]{:S(2)}) %collective-permute-start.18) | collective-permute-done | bytes 294944 | tf_op jit(solution)/shard_map/ppermute | solution.py:29
  96.6 0.1 broadcast_select_fusion
  96.6 0.4 collective-permute-start.20
  97.0 0.1 broadcast_select_fusion.1
  97.0 0.3 collective-permute-start.19
  97.3 4.7 %shard_map.62.refs_10_ = f32[384,4096]{1,0:T(8,128)S(1)} custom-call(f32[1152,384]{1,0:T(8,128)S(1)} %get-tuple-element.121.gram, bf16[1152,4096]{1,0:T(8,128)(2,1)S(1)} %get-tuple-element.122.rows, bf16[384,384]{1,0:T(8,128)(2,1)S(1)} %collective-permute-done.17.down0.refs_6_, ...), custom_call_target="tpu_custom_call", output_to_operand_aliasing={{}: (6, {})} | custom-call | flops 3623878656 | bytes 36238784 | tf_op jit(solution)/shard_map/pallas_call | solution.py:57
  102.0 0.0 collective-permute-done.20.refs_5_
  102.1 4.6 %shard_map.63 = bf16[384,4096]{1,0:T(8,128)(2,1)} custom-call(bf16[384,4096]{1,0:T(8,128)(2,1)S(1)} %broadcast_multiply_fusion.own, bf16[64,4096]{1,0:T(8,128)(2,1)S(1)} %collective-permute-done.5.refs_0_, bf16[64,4096]{1,0:T(8,128)(2,1)S(1)} %collective-permute-done.11.refs_1_, bf16[64,4096]{1,0:T(8,128)(2,1)S(1)} %collective-permute-done.14.refs_2_, ...), custom_call_target="tpu_custom_call" | custom-call | flops 2415919104 | bytes 24159192 | tf_op jit(solution)/shard_map/pallas_call | solution.py:57
  (24 shorter events, 0.1 us)
Async XLA Ops:
  4.6 4.5 %copy-start.9 = (bf16[384,2,384]{2,1,0:T(2,128)(2,1)S(1)}, bf16[384,2,384]{2,1,0:T(2,128)(2,1)}, u32[]{:S(2)}) copy-start(bf16[384,2,384]{2,1,0:T(2,128)(2,1)} %param.7) | copy-start | bytes 1769476
  4.6 4.6 %copy-start.3 = (s32[1,2]{1,0:T(1,128)S(1)}, s32[1,2]{1,0:T(1,128)}, u32[]{:S(2)}) copy-start(s32[1,2]{1,0:T(1,128)} %couple.1) | copy-start | bytes 28
  6.9 9.8 %collective-permute-start.1 = (bf16[384,4096]{1,0:T(8,128)(2,1)S(1)}, bf16[384,4096]{1,0:T(8,128)(2,1)}, u32[]{:S(2)}, u32[]{:S(2)}) collective-permute-start(bf16[384,4096]{1,0:T(8,128)(2,1)S(1)} %broadcast_multiply_fusion.own), channel_id=1, source_target_pairs={{0,1},{1,0},{2,3},{3,2},{4,5},{5,4},{6,7},{7,6},{8,9},{9,8},{10,11... | collective-permute-start | bytes 9437192 | tf_op jit(solution)/shard_map/ppermute | solution.py:29
  7.6 13.8 %collective-permute-start = (bf16[64,4096]{1,0:T(8,128)(2,1)}, bf16[64,4096]{1,0:T(8,128)(2,1)}, u32[]{:S(2)}, u32[]{:S(2)}) collective-permute-start(bf16[64,4096]{1,0:T(8,128)(2,1)} %slice_multiply_fusion), channel_id=1, source_target_pairs={{0,2},{1,3},{2,0},{3,1},{4,6},{5,7},{6,4},{7,5},{8,10},{9,11},{10,... | collective-permute-start | bytes 1572872 | tf_op jit(solution)/shard_map/ppermute | solution.py:29
  8.8 23.8 %collective-permute-start.4 = (bf16[64,4096]{1,0:T(8,128)(2,1)}, bf16[64,4096]{1,0:T(8,128)(2,1)}, u32[]{:S(2)}, u32[]{:S(2)}) collective-permute-start(bf16[64,4096]{1,0:T(8,128)(2,1)} %slice_multiply_fusion.5), channel_id=1, source_target_pairs={{0,2},{1,3},{2,0},{3,1},{4,6},{5,7},{6,4},{7,5},{8,10},{9,11},{10,... | collective-permute-start | bytes 1572872 | tf_op jit(solution)/shard_map/ppermute | solution.py:29
  10.0 0.7 copy-start
  10.8 0.7 copy-start.4
  11.5 0.7 copy-start.6
  12.2 1.0 copy-start.2
  16.7 4.7 %copy-start.8 = (bf16[384,4096]{1,0:T(8,128)(2,1)S(1)}, bf16[384,4096]{1,0:T(8,128)(2,1)}, u32[]{:S(2)}) copy-start(bf16[384,4096]{1,0:T(8,128)(2,1)} %param.5) | copy-start | bytes 9437188
  21.5 22.3 %collective-permute-start.2 = (bf16[64,4096]{1,0:T(8,128)(2,1)S(1)}, bf16[64,4096]{1,0:T(8,128)(2,1)S(1)}, u32[]{:S(2)}, u32[]{:S(2)}) collective-permute-start(bf16[64,4096]{1,0:T(8,128)(2,1)S(1)} %slice_multiply_fusion.4), channel_id=1, source_target_pairs={{0,2},{1,3},{2,0},{3,1},{4,6},{5,7},{6,4},{7,5},{8,10},{9,11},{10,... | collective-permute-start | bytes 1572872 | tf_op jit(solution)/shard_map/ppermute | solution.py:29
  22.8 21.0 %collective-permute-start.3 = (bf16[64,4096]{1,0:T(8,128)(2,1)}, bf16[64,4096]{1,0:T(8,128)(2,1)S(1)}, u32[]{:S(2)}, u32[]{:S(2)}) collective-permute-start(bf16[64,4096]{1,0:T(8,128)(2,1)} %collective-permute-done.refs_0_), channel_id=1, source_target_pairs={{0,4},{1,5},{4,8},{5,9},{6,2},{7,3},{8,12},{9,13},{10,6},{11,7},{1... | collective-permute-start | bytes 1572872 | tf_op jit(solution)/shard_map/ppermute | solution.py:29
  32.8 22.3 %collective-permute-start.7 = (bf16[64,4096]{1,0:T(8,128)(2,1)S(1)}, bf16[64,4096]{1,0:T(8,128)(2,1)S(1)}, u32[]{:S(2)}, u32[]{:S(2)}) collective-permute-start(bf16[64,4096]{1,0:T(8,128)(2,1)S(1)} %slice_multiply_fusion.2), channel_id=1, source_target_pairs={{0,2},{1,3},{2,0},{3,1},{4,6},{5,7},{6,4},{7,5},{8,10},{9,11},{10,... | collective-permute-start | bytes 1572872 | tf_op jit(solution)/shard_map/ppermute | solution.py:29
  34.1 21.0 %collective-permute-start.8 = (bf16[64,4096]{1,0:T(8,128)(2,1)}, bf16[64,4096]{1,0:T(8,128)(2,1)S(1)}, u32[]{:S(2)}, u32[]{:S(2)}) collective-permute-start(bf16[64,4096]{1,0:T(8,128)(2,1)} %collective-permute-done.4.refs_0_), channel_id=1, source_target_pairs={{0,4},{1,5},{4,8},{5,9},{6,2},{7,3},{8,12},{9,13},{10,6},{11,7},{1... | collective-permute-start | bytes 1572872 | tf_op jit(solution)/shard_map/ppermute | solution.py:29
  43.9 11.2 %collective-permute-start.9 = (bf16[64,4096]{1,0:T(8,128)(2,1)S(1)}, bf16[64,4096]{1,0:T(8,128)(2,1)S(1)}, u32[]{:S(2)}, u32[]{:S(2)}) collective-permute-start(bf16[64,4096]{1,0:T(8,128)(2,1)S(1)} %broadcast_select_fusion.5), channel_id=1, source_target_pairs={{0,1},{1,0},{2,3},{3,2},{4,5},{5,4},{6,7},{7,6},{8,9},{9,8},{10,11... | collective-permute-start | bytes 1572872 | tf_op jit(solution)/shard_map/ppermute | solution.py:29
  46.4 19.9 %collective-permute-start.5 = (bf16[64,4096]{1,0:T(8,128)(2,1)S(1)}, bf16[64,4096]{1,0:T(8,128)(2,1)S(1)}, u32[]{:S(2)}, u32[]{:S(2)}) collective-permute-start(bf16[64,4096]{1,0:T(8,128)(2,1)S(1)} %slice_multiply_fusion.3), channel_id=1, source_target_pairs={{0,2},{1,3},{2,0},{3,1},{4,6},{5,7},{6,4},{7,5},{8,10},{9,11},{10,... | collective-permute-start | bytes 1572872 | tf_op jit(solution)/shard_map/ppermute | solution.py:29
  46.6 19.6 %collective-permute-start.6 = (bf16[64,4096]{1,0:T(8,128)(2,1)S(1)}, bf16[64,4096]{1,0:T(8,128)(2,1)S(1)}, u32[]{:S(2)}, u32[]{:S(2)}) collective-permute-start(bf16[64,4096]{1,0:T(8,128)(2,1)S(1)} %collective-permute-done.2.refs_0_), channel_id=1, source_target_pairs={{0,4},{1,5},{4,8},{5,9},{6,2},{7,3},{8,12},{9,13},{10,6},{11,7},{1... | collective-permute-start | bytes 1572872 | tf_op jit(solution)/shard_map/ppermute | solution.py:29
  55.1 11.2 %collective-permute-start.10 = (bf16[64,4096]{1,0:T(8,128)(2,1)S(1)}, bf16[64,4096]{1,0:T(8,128)(2,1)S(1)}, u32[]{:S(2)}, u32[]{:S(2)}) collective-permute-start(bf16[64,4096]{1,0:T(8,128)(2,1)S(1)} %broadcast_select_fusion.4), channel_id=1, source_target_pairs={{0,1},{1,0},{2,3},{3,2},{4,5},{5,4},{6,7},{7,6},{8,9},{9,8},{10,11... | collective-permute-start | bytes 1572872 | tf_op jit(solution)/shard_map/ppermute | solution.py:29
  57.6 19.9 %collective-permute-start.11 = (bf16[64,4096]{1,0:T(8,128)(2,1)S(1)}, bf16[64,4096]{1,0:T(8,128)(2,1)S(1)}, u32[]{:S(2)}, u32[]{:S(2)}) collective-permute-start(bf16[64,4096]{1,0:T(8,128)(2,1)S(1)} %slice_multiply_fusion.1), channel_id=1, source_target_pairs={{0,2},{1,3},{2,0},{3,1},{4,6},{5,7},{6,4},{7,5},{8,10},{9,11},{10,... | collective-permute-start | bytes 1572872 | tf_op jit(solution)/shard_map/ppermute | solution.py:29
  57.9 19.6 %collective-permute-start.12 = (bf16[64,4096]{1,0:T(8,128)(2,1)S(1)}, bf16[64,4096]{1,0:T(8,128)(2,1)S(1)}, u32[]{:S(2)}, u32[]{:S(2)}) collective-permute-start(bf16[64,4096]{1,0:T(8,128)(2,1)S(1)} %collective-permute-done.7.refs_0_), channel_id=1, source_target_pairs={{0,4},{1,5},{4,8},{5,9},{6,2},{7,3},{8,12},{9,13},{10,6},{11,7},{1... | collective-permute-start | bytes 1572872 | tf_op jit(solution)/shard_map/ppermute | solution.py:29
  66.3 11.2 %collective-permute-start.13 = (bf16[64,4096]{1,0:T(8,128)(2,1)S(1)}, bf16[64,4096]{1,0:T(8,128)(2,1)S(1)}, u32[]{:S(2)}, u32[]{:S(2)}) collective-permute-start(bf16[64,4096]{1,0:T(8,128)(2,1)S(1)} %broadcast_select_fusion.3), channel_id=1, source_target_pairs={{0,1},{1,0},{2,3},{3,2},{4,5},{5,4},{6,7},{7,6},{8,9},{9,8},{10,11... | collective-permute-start | bytes 1572872 | tf_op jit(solution)/shard_map/ppermute | solution.py:29
  67.7 14.0 %copy-start.7 = (bf16[384,384]{1,0:T(8,128)(2,1)S(1)}, bf16[384,384]{1,0:T(8,128)(2,1)}, u32[]{:S(2)}) copy-start(bf16[384,384]{1,0:T(8,128)(2,1)} %copy-done.6) | copy-start | bytes 884740
  67.7 16.2 %copy-start.5 = (bf16[384,384]{1,0:T(8,128)(2,1)S(1)}, bf16[384,384]{1,0:T(8,128)(2,1)}, u32[]{:S(2)}) copy-start(bf16[384,384]{1,0:T(8,128)(2,1)} %copy-done.4) | copy-start | bytes 884740
  67.7 20.7 %collective-permute-start.14 = (bf16[64,4096]{1,0:T(8,128)(2,1)S(1)}, bf16[64,4096]{1,0:T(8,128)(2,1)S(1)}, u32[]{:S(2)}, u32[]{:S(2)}) collective-permute-start(bf16[64,4096]{1,0:T(8,128)(2,1)S(1)} %collective-permute-done.5.refs_0_), channel_id=1, source_target_pairs={{0,4},{1,5},{4,8},{5,9},{6,2},{7,3},{8,12},{9,13},{10,6},{11,7},{1... | collective-permute-start | bytes 1572872 | tf_op jit(solution)/shard_map/ppermute | solution.py:29
  77.6 12.0 %collective-permute-start.16 = (bf16[64,4096]{1,0:T(8,128)(2,1)S(1)}, bf16[64,4096]{1,0:T(8,128)(2,1)S(1)}, u32[]{:S(2)}, u32[]{:S(2)}) collective-permute-start(bf16[64,4096]{1,0:T(8,128)(2,1)S(1)} %broadcast_select_fusion.2), channel_id=1, source_target_pairs={{0,1},{1,0},{2,3},{3,2},{4,5},{5,4},{6,7},{7,6},{8,9},{9,8},{10,11... | collective-permute-start | bytes 1572872 | tf_op jit(solution)/shard_map/ppermute | solution.py:29
  78.5 18.1 %collective-permute-start.15 = (bf16[64,4096]{1,0:T(8,128)(2,1)S(1)}, bf16[64,4096]{1,0:T(8,128)(2,1)S(1)}, u32[]{:S(2)}, u32[]{:S(2)}) collective-permute-start(bf16[64,4096]{1,0:T(8,128)(2,1)S(1)} %collective-permute-done.11.refs_1_), channel_id=1, source_target_pairs={{0,4},{1,5},{4,8},{5,9},{6,2},{7,3},{8,12},{9,13},{10,6},{11,7},{1... | collective-permute-start | bytes 1572872 | tf_op jit(solution)/shard_map/ppermute | solution.py:29
  81.7 9.1 %collective-permute-start.17 = (bf16[384,384]{1,0:T(8,128)(2,1)S(1)}, bf16[384,384]{1,0:T(8,128)(2,1)S(1)}, u32[]{:S(2)}, u32[]{:S(2)}) collective-permute-start(bf16[384,384]{1,0:T(8,128)(2,1)S(1)} %copy-done.7), channel_id=1, source_target_pairs={{0,1},{1,2},{2,3},{3,4},{4,5},{5,6},{6,7},{7,8},{8,9},{9,10},{10,1... | collective-permute-start | bytes 884744 | tf_op jit(solution)/shard_map/ppermute | solution.py:29
  83.9 12.6 %collective-permute-start.18 = (bf16[384,384]{1,0:T(8,128)(2,1)S(1)}, bf16[384,384]{1,0:T(8,128)(2,1)S(1)}, u32[]{:S(2)}, u32[]{:S(2)}) collective-permute-start(bf16[384,384]{1,0:T(8,128)(2,1)S(1)} %copy-done.5), channel_id=1, source_target_pairs={{0,2},{1,3},{2,4},{3,5},{4,6},{5,7},{6,8},{7,9},{8,10},{9,11},{10,... | collective-permute-start | bytes 884744 | tf_op jit(solution)/shard_map/ppermute | solution.py:29
  90.8 6.5 %copy-start.1 = (bf16[384,384]{1,0:T(8,128)(2,1)S(1)}, bf16[384,384]{1,0:T(8,128)(2,1)}, u32[]{:S(2)}) copy-start(bf16[384,384]{1,0:T(8,128)(2,1)} %copy-done) | copy-start | bytes 884740
  96.6 5.4 %collective-permute-start.20 = (bf16[64,4096]{1,0:T(8,128)(2,1)S(1)}, bf16[64,4096]{1,0:T(8,128)(2,1)S(1)}, u32[]{:S(2)}, u32[]{:S(2)}) collective-permute-start(bf16[64,4096]{1,0:T(8,128)(2,1)S(1)} %broadcast_select_fusion), channel_id=1, source_target_pairs={{0,1},{1,0},{2,3},{3,2},{4,5},{5,4},{6,7},{7,6},{8,9},{9,8},{10,11... | collective-permute-start | bytes 1572872 | tf_op jit(solution)/shard_map/ppermute | solution.py:29
  97.0 5.0 %collective-permute-start.19 = (bf16[64,4096]{1,0:T(8,128)(2,1)S(1)}, bf16[64,4096]{1,0:T(8,128)(2,1)S(1)}, u32[]{:S(2)}, u32[]{:S(2)}) collective-permute-start(bf16[64,4096]{1,0:T(8,128)(2,1)S(1)} %broadcast_select_fusion.1), channel_id=1, source_target_pairs={{0,1},{1,0},{2,3},{3,2},{4,5},{5,4},{6,7},{7,6},{8,9},{9,8},{10,11... | collective-permute-start | bytes 1572872 | tf_op jit(solution)/shard_map/ppermute | solution.py:29

commit v4 on v3

--- a/solution.py
+++ b/solution.py
@@ -12,6 +12,7 @@
 LAG = 3
 HOLD = 2
 TILE = 1024
+SURE = 192
 MIB = 2**20
 
 
@@ -142,6 +143,25 @@
         copy.wait()
 
 
+def begin_body(spans, orbitals, tally, own, *refs):
+    pieces, done = refs[:-1], refs[-1]
+    head = sum(piece.shape[0] for piece in pieces)
+    top = pltpu.make_async_copy(orbitals.at[:head], own.at[:head], done.at[0])
+    rest = pltpu.make_async_copy(orbitals.at[head:], own.at[head:], done.at[1])
+    top.start()
+    rest.start()
+    top.wait()
+    copies = [pltpu.make_async_copy(own.at[span], piece, done.at[i + 2]) for i, (piece, span) in enumerate(zip(pieces, spans))]
+    for copy in copies:
+        copy.start()
+    rest.wait()
+    height, width = own.shape
+    row = lax.broadcasted_iota(jnp.int32, (height - SURE, width), 0) + SURE
+    own[SURE:, :] = jnp.where(row < tally[0], own[SURE:, :], jnp.zeros((), own.dtype))
+    for copy in copies:
+        copy.wait()
+
+
 def on_device(orbitals, kern_diag, kern_near, couple, tally):
     peers = lax.axis_size("pts")
     me = lax.axis_index("pts")
@@ -166,16 +186,22 @@
             held[n] = value
 
     def part(j, *gates):
-        return after(orbitals, *gates)[spans[j]] * valid[spans[j]]
+        return after(own, *gates)[spans[j]]
 
     def pieces(i):
         return [held["across", i], held["onward", i], held["swap", i]]
 
-    first = part(0)
+    begun = [pltpu.HBM((CUTS[j], width), kind) for j in range(2)]
+    own, first, second = pl.pallas_call(
+        functools.partial(begin_body, spans[:2]),
+        out_shape=(pltpu.VMEM((height, width), kind), *begun),
+        in_specs=[pl.BlockSpec(memory_space=pltpu.HBM), pl.BlockSpec(memory_space=pltpu.SMEM)],
+        out_specs=(pl.BlockSpec(memory_space=pltpu.VMEM),) + (pl.BlockSpec(memory_space=pltpu.HBM),) * 2,
+        scratch_shapes=[pltpu.SemaphoreType.DMA((4,))],
+        compiler_params=pltpu.CompilerParams(vmem_limit_bytes=8 * MIB),
+    )(pltpu.with_memory_space_constraint(orbitals, pltpu.HBM), tally)
     held["across", 0] = send(first, across)
-    second = part(1, first)
     held["across", 1] = send(second, across)
-    own = after(orbitals, second) * valid
     beside = send(own, sibling)
     near = after(kern_near, own)
     square = jax.ShapeDtypeStruct((height, height), kind)
@@ -200,8 +226,7 @@
             flops=2 * count * height * width,
         )
 
-    collect(0, [after(beside, held["total"])])
-    join(("across", 0), "rows", "gram")
+    join(("across", 0), "total")
     def swap(i):
         held["swap", i] = send(jnp.where(mixed, held["across", i], held["onward", i]), sibling)
 
@@ -210,7 +235,7 @@
 
     swaps = collects = 0
     for w in range(1, last + 1):
-        now = held["rows"]
+        now = held["total"]
         if w + 1 <= last:
             held["across", w + 1] = send(part(w + 1, now), across)
         held["onward", w - 1] = send(held["across", w - 1], onward)
@@ -220,9 +245,11 @@
                 held["down", o] = send(after(down, now), pairs)
         if w >= LAG:
             swap(w - LAG)
+        if w == LAG:
+            collect(0, [after(beside, held["total"])])
         if w >= LAG + 1:
             collected(w - LAG - 1)
-        join(("across", w), ("onward", w - LAG + 1), ("swap", w - LAG), "rows", "gram")
+        join(("across", w), ("onward", w - LAG + 1), ("swap", w - LAG), "rows", "gram", "total")
     held["onward", last] = send(held["across", last], onward)
     if KAT > last:
         for o, down in enumerate((down0, down1)):

time: 107 us -> 105 us (0.981)
  other arithmetic: 6.92 us -> 1.44 us
  Pallas kernels: 24.3 us -> 27.6 us
  waiting for transfers between devices: 32.1 us -> 29.2 us
  starting transfers between devices: 39 us -> 40.5 us
    mul x7 -> x0, other arithmetic: 6.52 us -> none  [the longest x6 4.3 us: part(): return after(orbitals, *gates)[spans[j]] * valid[spans[j]]]
    ppermute x21, waiting for transfers between devices: 32.1 us -> 29.2 us  [send(): return lax.ppermute(array, 'pts', pairs)]
    pallas_call x0 -> x1, Pallas kernels: none -> 2.25 us  [on_device(): pl.pallas_call(functools.partial(begin_body, spans[:2]), out_shape=(pltpu...]
    ppermute x21, starting transfers between devices: 39 us -> 40.5 us  [send(): return lax.ppermute(array, 'pts', pairs)]
    unnamed x20 -> x24, local copies, waits for them, and re-layouts: 3.16 us -> 2.69 us
  transfers between devices with their start and end apart: 21 -> 21, of which waited for: 7 -> 8; matrix products, arithmetic and copies ran while one was open for 1% -> 2% of each run, Pallas kernels for 18% -> 20%
where the time goes in v4:
time: 105 us; the launch traced here: 104 us
  starting transfers between devices  40.5 us (39%)
  waiting for transfers between devices  29.2 us (28%)
  Pallas kernels  27.6 us (26%)
  local copies, waits for them, and re-layouts  3.76 us (4%)
  other arithmetic  1.44 us (1%)
  between operations  1.28 us (1%)
    ppermute x21, starting transfers between devices, send(): return lax.ppermute(array, 'pts', pairs)  40.5 us
    ppermute x21, waiting for transfers between devices, send(): return lax.ppermute(array, 'pts', pairs)  29.2 us
    pallas_call x9, Pallas kernels, call(): pl.pallas_call(body, out_shape=out, in_specs=[anywhere] * hbm + [vector]...  25.3 us
    unnamed x24, local copies, waits for them, and re-layouts  2.69 us
    pallas_call x1, Pallas kernels, on_device(): pl.pallas_call(functools.partial(begin_body, spans[:2]), out_shape=(pltpu...  2.25 us
  transfers between devices with their start and end apart: 21, of which 8 were waited for; matrix products, arithmetic and copies ran while one was open for 2% of the time, Pallas kernels for 20%

profile of v4, /device:TPU:11, one launch (start us, length us, event | category | flops | bytes accessed | tf_op | source)
XLA Modules:
  0.0 103.8 jit_solution(8000335319383362767)
XLA Ops:
  0.7 2.2 %shard_map.55 = (bf16[384,4096]{1,0:T(8,128)(2,1)S(1)}, bf16[64,4096]{1,0:T(8,128)(2,1)}, bf16[64,4096]{1,0:T(8,128)(2,1)}) custom-call(bf16[384,4096]{1,0:T(8,128)(2,1)} %orbitals.1, s32[1]{0:T(128)S(6)} %copy.26.tally), custom_call_target="tpu_custom_call" | custom-call | tf_op jit(solution)/shard_map/pallas_call | solution.py:195
  3.0 0.7 collective-permute-start.9
  3.7 1.3 %collective-permute-start = (bf16[64,4096]{1,0:T(8,128)(2,1)}, bf16[64,4096]{1,0:T(8,128)(2,1)}, u32[]{:S(2)}, u32[]{:S(2)}) collective-permute-start(bf16[64,4096]{1,0:T(8,128)(2,1)} %get-tuple-element.66), channel_id=1, source_target_pairs={{0,2},{1,3},{2,0},{3,1},{4,6},{5,7},{6,4},{7,5},{8,10},{9,11},{10,... | collective-permute-start | bytes 1572872 | tf_op jit(solution)/shard_map/ppermute | solution.py:30
  5.0 0.2 collective-permute-start.3
  5.2 0.1 copy.15
  5.3 0.1 slice_bitcast_fusion
  5.4 0.8 shard_map.56
  6.2 3.5 %shard_map.57.before = f32[384,4096]{1,0:T(8,128)S(1)} custom-call(bf16[384,4096]{1,0:T(8,128)(2,1)S(1)} %get-tuple-element.92.own, bf16[384,384]{1,0:T(8,128)(2,1)S(1)} %copy-done.3), custom_call_target="tpu_custom_call" | custom-call | flops 2415919104 | bytes 24159192 | tf_op jit(solution)/shard_map/pallas_call | solution.py:58
  9.8 2.6 %copy-done = f32[384,4096]{1,0:T(8,128)} copy-done((f32[384,4096]{1,0:T(8,128)}, f32[384,4096]{1,0:T(8,128)S(1)}, u32[]{:S(2)}) %copy-start) | copy-done | bytes 6291480
  12.4 5.2 %collective-permute-done.refs_0_ = bf16[64,4096]{1,0:T(8,128)(2,1)} collective-permute-done((bf16[64,4096]{1,0:T(8,128)(2,1)}, bf16[64,4096]{1,0:T(8,128)(2,1)}, u32[]{:S(2)}, u32[]{:S(2)}) %collective-permute-start) | collective-permute-done | bytes 524320 | tf_op jit(solution)/shard_map/ppermute | solution.py:30
  17.6 0.8 slice.20
  18.4 1.2 %collective-permute-start.1 = (bf16[64,4096]{1,0:T(8,128)(2,1)}, bf16[64,4096]{1,0:T(8,128)(2,1)}, u32[]{:S(2)}, u32[]{:S(2)}) collective-permute-start(bf16[64,4096]{1,0:T(8,128)(2,1)} %slice.20), channel_id=1, source_target_pairs={{0,2},{1,3},{2,0},{3,1},{4,6},{5,7},{6,4},{7,5},{8,10},{9,11},{10,... | collective-permute-start | bytes 1572872 | tf_op jit(solution)/shard_map/ppermute | solution.py:30
  19.6 3.2 %collective-permute-start.2 = (bf16[64,4096]{1,0:T(8,128)(2,1)}, bf16[64,4096]{1,0:T(8,128)(2,1)}, u32[]{:S(2)}, u32[]{:S(2)}) collective-permute-start(bf16[64,4096]{1,0:T(8,128)(2,1)} %collective-permute-done.refs_0_), channel_id=1, source_target_pairs={{0,4},{1,5},{4,8},{5,9},{6,2},{7,3},{8,12},{9,13},{10,6},{11,7},{1... | collective-permute-start | bytes 1572872 | tf_op jit(solution)/shard_map/ppermute | solution.py:30
  22.8 6.0 %collective-permute-done.3.refs_0_ = bf16[64,4096]{1,0:T(8,128)(2,1)} collective-permute-done((bf16[64,4096]{1,0:T(8,128)(2,1)}, bf16[64,4096]{1,0:T(8,128)(2,1)}, u32[]{:S(2)}, u32[]{:S(2)}) %collective-permute-start.3) | collective-permute-done | bytes 524320 | tf_op jit(solution)/shard_map/ppermute | solution.py:30
  28.8 1.3 %collective-permute-start.6 = (bf16[64,4096]{1,0:T(8,128)(2,1)S(1)}, bf16[64,4096]{1,0:T(8,128)(2,1)S(1)}, u32[]{:S(2)}, u32[]{:S(2)}) collective-permute-start(bf16[64,4096]{1,0:T(8,128)(2,1)S(1)} %slice.22), channel_id=1, source_target_pairs={{0,2},{1,3},{2,0},{3,1},{4,6},{5,7},{6,4},{7,5},{8,10},{9,11},{10,... | collective-permute-start | bytes 1572872 | tf_op jit(solution)/shard_map/ppermute | solution.py:30
  30.1 3.2 %collective-permute-start.7 = (bf16[64,4096]{1,0:T(8,128)(2,1)}, bf16[64,4096]{1,0:T(8,128)(2,1)S(1)}, u32[]{:S(2)}, u32[]{:S(2)}) collective-permute-start(bf16[64,4096]{1,0:T(8,128)(2,1)} %collective-permute-done.3.refs_0_), channel_id=1, source_target_pairs={{0,4},{1,5},{4,8},{5,9},{6,2},{7,3},{8,12},{9,13},{10,6},{11,7},{1... | collective-permute-start | bytes 1572872 | tf_op jit(solution)/shard_map/ppermute | solution.py:30
  33.3 6.7 %collective-permute-done.1.refs_0_ = bf16[64,4096]{1,0:T(8,128)(2,1)} collective-permute-done((bf16[64,4096]{1,0:T(8,128)(2,1)}, bf16[64,4096]{1,0:T(8,128)(2,1)}, u32[]{:S(2)}, u32[]{:S(2)}) %collective-permute-start.1) | collective-permute-done | bytes 524320 | tf_op jit(solution)/shard_map/ppermute | solution.py:30
  40.0 0.0 collective-permute-done.2.refs_1_
  40.0 1.1 %broadcast_select_fusion.5 = bf16[64,4096]{1,0:T(8,128)(2,1)S(1)} fusion(bf16[64,4096]{1,0:T(8,128)(2,1)} %collective-permute-done.refs_0_, bf16[64,4096]{1,0:T(8,128)(2,1)} %collective-permute-done.2.refs_1_, pred[]{:T(512)S(6)} %eq.11), kind=kLoop, calls=%fused_computation.5 | loop fusion | flops 262144 | bytes 1572865 | tf_op jit(solution)/shard_map/jit(_where)/select_n | solution.py:231
  41.1 1.4 %collective-permute-start.8 = (bf16[64,4096]{1,0:T(8,128)(2,1)S(1)}, bf16[64,4096]{1,0:T(8,128)(2,1)S(1)}, u32[]{:S(2)}, u32[]{:S(2)}) collective-permute-start(bf16[64,4096]{1,0:T(8,128)(2,1)S(1)} %broadcast_select_fusion.5), channel_id=1, source_target_pairs={{0,1},{1,0},{2,3},{3,2},{4,5},{5,4},{6,7},{7,6},{8,9},{9,8},{10,11... | collective-permute-start | bytes 1572872 | tf_op jit(solution)/shard_map/ppermute | solution.py:30
  42.5 1.3 %collective-permute-start.4 = (bf16[64,4096]{1,0:T(8,128)(2,1)S(1)}, bf16[64,4096]{1,0:T(8,128)(2,1)S(1)}, u32[]{:S(2)}, u32[]{:S(2)}) collective-permute-start(bf16[64,4096]{1,0:T(8,128)(2,1)S(1)} %slice.21), channel_id=1, source_target_pairs={{0,2},{1,3},{2,0},{3,1},{4,6},{5,7},{6,4},{7,5},{8,10},{9,11},{10,... | collective-permute-start | bytes 1572872 | tf_op jit(solution)/shard_map/ppermute | solution.py:30
  43.8 0.0 collective-permute-done.9.refs_0_
  43.8 3.2 %collective-permute-start.5 = (bf16[64,4096]{1,0:T(8,128)(2,1)}, bf16[64,4096]{1,0:T(8,128)(2,1)S(1)}, u32[]{:S(2)}, u32[]{:S(2)}) collective-permute-start(bf16[64,4096]{1,0:T(8,128)(2,1)} %collective-permute-done.1.refs_0_), channel_id=1, source_target_pairs={{0,4},{1,5},{4,8},{5,9},{6,2},{7,3},{8,12},{9,13},{10,6},{11,7},{1... | collective-permute-start | bytes 1572872 | tf_op jit(solution)/shard_map/ppermute | solution.py:30
  47.0 3.7 %shard_map.58 = (bf16[1152,4096]{1,0:T(8,128)(2,1)S(1)}, f32[1152,384]{1,0:T(8,128)S(1)}) custom-call(bf16[384,4096]{1,0:T(8,128)(2,1)S(1)} %get-tuple-element.92.own, bf16[384,4096]{1,0:T(8,128)(2,1)} %collective-permute-done.9.refs_0_), custom_call_target="tpu_custom_call" | custom-call | flops 1207959552 | bytes 12079595 | tf_op jit(solution)/shard_map/pallas_call | solution.py:58
  50.7 0.4 collective-permute-done.6.refs_0_
  51.2 0.0 collective-permute-done.7.refs_1_
  51.2 0.0 collective-permute-done.8.refs_2_
  51.2 0.1 broadcast_select_fusion.4
  51.2 2.4 %collective-permute-start.10 = (bf16[64,4096]{1,0:T(8,128)(2,1)S(1)}, bf16[64,4096]{1,0:T(8,128)(2,1)S(1)}, u32[]{:S(2)}, u32[]{:S(2)}) collective-permute-start(bf16[64,4096]{1,0:T(8,128)(2,1)S(1)} %broadcast_select_fusion.4), channel_id=1, source_target_pairs={{0,1},{1,0},{2,3},{3,2},{4,5},{5,4},{6,7},{7,6},{8,9},{9,8},{10,11... | collective-permute-start | bytes 1572872 | tf_op jit(solution)/shard_map/ppermute | solution.py:30
  53.7 0.3 collective-permute-start.11
  53.9 3.2 %collective-permute-start.12 = (bf16[64,4096]{1,0:T(8,128)(2,1)S(1)}, bf16[64,4096]{1,0:T(8,128)(2,1)S(1)}, u32[]{:S(2)}, u32[]{:S(2)}) collective-permute-start(bf16[64,4096]{1,0:T(8,128)(2,1)S(1)} %collective-permute-done.6.refs_0_), channel_id=1, source_target_pairs={{0,4},{1,5},{4,8},{5,9},{6,2},{7,3},{8,12},{9,13},{10,6},{11,7},{1... | collective-permute-start | bytes 1572872 | tf_op jit(solution)/shard_map/ppermute | solution.py:30
  57.1 2.4 %shard_map.59 = (bf16[1152,4096]{1,0:T(8,128)(2,1)S(1)}, f32[1152,384]{1,0:T(8,128)S(1)}) custom-call(bf16[384,4096]{1,0:T(8,128)(2,1)S(1)} %get-tuple-element.92.own, bf16[64,4096]{1,0:T(8,128)(2,1)} %collective-permute-done.refs_0_, bf16[64,4096]{1,0:T(8,128)(2,1)} %collective-permute-done.2.refs_1_, ...), custom_call_target="tpu_custom_call", output_to_operand_aliasing={{0}: (4, {}), {1}: (5, {})} | custom-call | flops 603979776 | bytes 6039797 | tf_op jit(solution)/shard_map/pallas_call | solution.py:58
  59.5 2.8 %collective-permute-done.4.refs_0_ = bf16[64,4096]{1,0:T(8,128)(2,1)S(1)} collective-permute-done((bf16[64,4096]{1,0:T(8,128)(2,1)S(1)}, bf16[64,4096]{1,0:T(8,128)(2,1)S(1)}, u32[]{:S(2)}, u32[]{:S(2)}) %collective-permute-start.4) | collective-permute-done | bytes 524320 | tf_op jit(solution)/shard_map/ppermute | solution.py:30
  62.4 0.0 collective-permute-done.5.refs_1_
  62.4 0.0 collective-permute-done.10.refs_2_
  62.4 0.1 broadcast_select_fusion.3
  62.5 2.4 %collective-permute-start.13 = (bf16[64,4096]{1,0:T(8,128)(2,1)S(1)}, bf16[64,4096]{1,0:T(8,128)(2,1)S(1)}, u32[]{:S(2)}, u32[]{:S(2)}) collective-permute-start(bf16[64,4096]{1,0:T(8,128)(2,1)S(1)} %broadcast_select_fusion.3), channel_id=1, source_target_pairs={{0,1},{1,0},{2,3},{3,2},{4,5},{5,4},{6,7},{7,6},{8,9},{9,8},{10,11... | collective-permute-start | bytes 1572872 | tf_op jit(solution)/shard_map/ppermute | solution.py:30
  64.9 3.2 %collective-permute-start.14 = (bf16[64,4096]{1,0:T(8,128)(2,1)S(1)}, bf16[64,4096]{1,0:T(8,128)(2,1)S(1)}, u32[]{:S(2)}, u32[]{:S(2)}) collective-permute-start(bf16[64,4096]{1,0:T(8,128)(2,1)S(1)} %collective-permute-done.4.refs_0_), channel_id=1, source_target_pairs={{0,4},{1,5},{4,8},{5,9},{6,2},{7,3},{8,12},{9,13},{10,6},{11,7},{1... | collective-permute-start | bytes 1572872 | tf_op jit(solution)/shard_map/ppermute | solution.py:30
  68.1 2.2 %shard_map.60 = (bf16[1152,4096]{1,0:T(8,128)(2,1)S(1)}, f32[1152,384]{1,0:T(8,128)S(1)}) custom-call(bf16[384,4096]{1,0:T(8,128)(2,1)S(1)} %get-tuple-element.92.own, bf16[64,4096]{1,0:T(8,128)(2,1)} %collective-permute-done.3.refs_0_, bf16[64,4096]{1,0:T(8,128)(2,1)S(1)} %collective-permute-done.7.refs_1_, ...), custom_call_target="tpu_custom_call", output_to_operand_aliasing={{0}: (4, {}), {1}: (5, {})} | custom-call | flops 603979776 | bytes 6039797 | tf_op jit(solution)/shard_map/pallas_call | solution.py:58
  70.3 3.3 %collective-permute-done.11.refs_1_ = bf16[64,4096]{1,0:T(8,128)(2,1)S(1)} collective-permute-done((bf16[64,4096]{1,0:T(8,128)(2,1)S(1)}, bf16[64,4096]{1,0:T(8,128)(2,1)S(1)}, u32[]{:S(2)}, u32[]{:S(2)}) %collective-permute-start.11) | collective-permute-done | bytes 524320 | tf_op jit(solution)/shard_map/ppermute | solution.py:30
  73.6 0.0 collective-permute-done.12.refs_1_
  73.6 0.0 collective-permute-done.13.refs_2_
  73.6 0.1 broadcast_select_fusion.2
  73.7 0.9 collective-permute-start.16
  74.6 3.2 %collective-permute-start.15 = (bf16[64,4096]{1,0:T(8,128)(2,1)S(1)}, bf16[64,4096]{1,0:T(8,128)(2,1)S(1)}, u32[]{:S(2)}, u32[]{:S(2)}) collective-permute-start(bf16[64,4096]{1,0:T(8,128)(2,1)S(1)} %collective-permute-done.11.refs_1_), channel_id=1, source_target_pairs={{0,4},{1,5},{4,8},{5,9},{6,2},{7,3},{8,12},{9,13},{10,6},{11,7},{1... | collective-permute-start | bytes 1572872 | tf_op jit(solution)/shard_map/ppermute | solution.py:30
  77.8 2.2 %collective-permute-start.17 = (bf16[384,384]{1,0:T(8,128)(2,1)S(1)}, bf16[384,384]{1,0:T(8,128)(2,1)S(1)}, u32[]{:S(2)}, u32[]{:S(2)}) collective-permute-start(bf16[384,384]{1,0:T(8,128)(2,1)S(1)} %copy-done.8), channel_id=1, source_target_pairs={{0,1},{1,2},{2,3},{3,4},{4,5},{5,6},{6,7},{7,8},{8,9},{9,10},{10,1... | collective-permute-start | bytes 884744 | tf_op jit(solution)/shard_map/ppermute | solution.py:30
  80.1 4.5 %collective-permute-start.18 = (bf16[384,384]{1,0:T(8,128)(2,1)S(1)}, bf16[384,384]{1,0:T(8,128)(2,1)S(1)}, u32[]{:S(2)}, u32[]{:S(2)}) collective-permute-start(bf16[384,384]{1,0:T(8,128)(2,1)S(1)} %copy-done.6), channel_id=1, source_target_pairs={{0,2},{1,3},{2,4},{3,5},{4,6},{5,7},{6,8},{7,9},{8,10},{9,11},{10,... | collective-permute-start | bytes 884744 | tf_op jit(solution)/shard_map/ppermute | solution.py:30
  84.5 0.0 collective-permute-done.14.refs_2_
  84.5 2.2 %shard_map.61 = (bf16[1152,4096]{1,0:T(8,128)(2,1)S(1)}, f32[1152,384]{1,0:T(8,128)S(1)}) custom-call(bf16[384,4096]{1,0:T(8,128)(2,1)S(1)} %get-tuple-element.92.own, bf16[64,4096]{1,0:T(8,128)(2,1)} %collective-permute-done.1.refs_0_, bf16[64,4096]{1,0:T(8,128)(2,1)S(1)} %collective-permute-done.5.refs_1_, ...), custom_call_target="tpu_custom_call", output_to_operand_aliasing={{0}: (4, {}), {1}: (5, {})} | custom-call | flops 603979776 | bytes 6039797 | tf_op jit(solution)/shard_map/pallas_call | solution.py:58
  86.8 0.0 collective-permute-done.16.refs_2_
  86.8 0.0 slice-start
  86.8 0.0 slice-start.1
  86.8 1.2 %shard_map.62 = (bf16[1152,4096]{1,0:T(8,128)(2,1)S(1)}, f32[1152,384]{1,0:T(8,128)S(1)}) custom-call(bf16[384,4096]{1,0:T(8,128)(2,1)S(1)} %get-tuple-element.92.own, bf16[64,4096]{1,0:T(8,128)(2,1)S(1)} %collective-permute-done.6.refs_0_, bf16[64,4096]{1,0:T(8,128)(2,1)S(1)} %collective-permute-done.12.refs_1_, ...), custom_call_target="tpu_custom_call", output_to_operand_aliasing={{0}: (4, {}), {1}: (5, {})} | custom-call | flops 603979776 | bytes 6039797 | tf_op jit(solution)/shard_map/pallas_call | solution.py:58
  88.0 0.0 collective-permute-done.17.down0.refs_6_
  88.0 4.7 %collective-permute-done.18.down1.refs_7_ = bf16[384,384]{1,0:T(8,128)(2,1)S(1)} collective-permute-done((bf16[384,384]{1,0:T(8,128)(2,1)S(1)}, bf16[384,384]{1,0:T(8,128)(2,1)S(1)}, u32[]{:S(2)}, u32[]{:S(2)}) %collective-permute-start.18) | collective-permute-done | bytes 294944 | tf_op jit(solution)/shard_map/ppermute | solution.py:30
  92.7 0.2 collective-permute-done.15.refs_3_
  92.9 0.1 broadcast_select_fusion
  92.9 1.2 %collective-permute-start.20 = (bf16[64,4096]{1,0:T(8,128)(2,1)S(1)}, bf16[64,4096]{1,0:T(8,128)(2,1)S(1)}, u32[]{:S(2)}, u32[]{:S(2)}) collective-permute-start(bf16[64,4096]{1,0:T(8,128)(2,1)S(1)} %broadcast_select_fusion), channel_id=1, source_target_pairs={{0,1},{1,0},{2,3},{3,2},{4,5},{5,4},{6,7},{7,6},{8,9},{9,8},{10,11... | collective-permute-start | bytes 1572872 | tf_op jit(solution)/shard_map/ppermute | solution.py:30
  94.1 0.1 broadcast_select_fusion.1
  94.2 0.1 collective-permute-start.19
  94.3 4.7 %shard_map.63.refs_10_ = f32[384,4096]{1,0:T(8,128)S(1)} custom-call(f32[1152,384]{1,0:T(8,128)S(1)} %get-tuple-element.122.gram, bf16[1152,4096]{1,0:T(8,128)(2,1)S(1)} %get-tuple-element.123.rows, bf16[384,384]{1,0:T(8,128)(2,1)S(1)} %collective-permute-done.17.down0.refs_6_, ...), custom_call_target="tpu_custom_call", output_to_operand_aliasing={{}: (6, {})} | custom-call | flops 3623878656 | bytes 36238784 | tf_op jit(solution)/shard_map/pallas_call | solution.py:58
  99.0 0.0 collective-permute-done.20.refs_5_
  99.0 0.0 collective-permute-done.19.refs_4_
  99.0 4.6 %shard_map.64 = bf16[384,4096]{1,0:T(8,128)(2,1)} custom-call(bf16[384,4096]{1,0:T(8,128)(2,1)S(1)} %get-tuple-element.92.own, bf16[64,4096]{1,0:T(8,128)(2,1)S(1)} %collective-permute-done.4.refs_0_, bf16[64,4096]{1,0:T(8,128)(2,1)S(1)} %collective-permute-done.11.refs_1_, bf16[64,4096]{1,0:T(8,128)(2,1)S(1)} %collective-permute-done.14.refs_2_, ...), custom_call_target="tpu_custom_call" | custom-call | flops 2415919104 | bytes 24159192 | tf_op jit(solution)/shard_map/pallas_call | solution.py:58
  (25 shorter events, 0.1 us)
Async XLA Ops:
  0.0 5.2 %copy-start.9 = (bf16[384,2,384]{2,1,0:T(2,128)(2,1)S(1)}, bf16[384,2,384]{2,1,0:T(2,128)(2,1)}, u32[]{:S(2)}) copy-start(bf16[384,2,384]{2,1,0:T(2,128)(2,1)} %param.7) | copy-start | bytes 1769476
  0.0 5.4 %copy-start.4 = (s32[1,2]{1,0:T(1,128)S(1)}, s32[1,2]{1,0:T(1,128)}, u32[]{:S(2)}) copy-start(s32[1,2]{1,0:T(1,128)} %couple.1) | copy-start | bytes 28
  0.0 6.2 %copy-start.3 = (bf16[384,384]{1,0:T(8,128)(2,1)S(1)}, bf16[384,384]{1,0:T(8,128)(2,1)}, u32[]{:S(2)}) copy-start(bf16[384,384]{1,0:T(8,128)(2,1)} %kern) | copy-start | bytes 884740
  3.0 40.9 %collective-permute-start.9 = (bf16[384,4096]{1,0:T(8,128)(2,1)S(1)}, bf16[384,4096]{1,0:T(8,128)(2,1)}, u32[]{:S(2)}, u32[]{:S(2)}) collective-permute-start(bf16[384,4096]{1,0:T(8,128)(2,1)S(1)} %get-tuple-element.92.own), channel_id=1, source_target_pairs={{0,1},{1,0},{2,3},{3,2},{4,5},{5,4},{6,7},{7,6},{8,9},{9,8},{10,11... | collective-permute-start | bytes 9437192 | tf_op jit(solution)/shard_map/ppermute | solution.py:30
  3.7 13.8 %collective-permute-start = (bf16[64,4096]{1,0:T(8,128)(2,1)}, bf16[64,4096]{1,0:T(8,128)(2,1)}, u32[]{:S(2)}, u32[]{:S(2)}) collective-permute-start(bf16[64,4096]{1,0:T(8,128)(2,1)} %get-tuple-element.66), channel_id=1, source_target_pairs={{0,2},{1,3},{2,0},{3,1},{4,6},{5,7},{6,4},{7,5},{8,10},{9,11},{10,... | collective-permute-start | bytes 1572872 | tf_op jit(solution)/shard_map/ppermute | solution.py:30
  5.0 23.8 %collective-permute-start.3 = (bf16[64,4096]{1,0:T(8,128)(2,1)}, bf16[64,4096]{1,0:T(8,128)(2,1)}, u32[]{:S(2)}, u32[]{:S(2)}) collective-permute-start(bf16[64,4096]{1,0:T(8,128)(2,1)} %get-tuple-element.73), channel_id=1, source_target_pairs={{0,2},{1,3},{2,0},{3,1},{4,6},{5,7},{6,4},{7,5},{8,10},{9,11},{10,... | collective-permute-start | bytes 1572872 | tf_op jit(solution)/shard_map/ppermute | solution.py:30
  6.2 3.6 %copy-start.1 = (bf16[384,384]{1,0:T(8,128)(2,1)}, bf16[384,384]{1,0:T(8,128)(2,1)S(1)}, u32[]{:S(2)}) copy-start(bf16[384,384]{1,0:T(8,128)(2,1)S(1)} %get-tuple-element.121.up1.refs_9_) | copy-start | bytes 884740
  6.2 3.6 %copy-start.5 = (bf16[384,384]{1,0:T(8,128)(2,1)}, bf16[384,384]{1,0:T(8,128)(2,1)S(1)}, u32[]{:S(2)}) copy-start(bf16[384,384]{1,0:T(8,128)(2,1)S(1)} %get-tuple-element.116) | copy-start | bytes 884740
  6.2 3.6 %copy-start.7 = (bf16[384,384]{1,0:T(8,128)(2,1)}, bf16[384,384]{1,0:T(8,128)(2,1)S(1)}, u32[]{:S(2)}) copy-start(bf16[384,384]{1,0:T(8,128)(2,1)S(1)} %get-tuple-element.114) | copy-start | bytes 884740
  9.7 2.7 %copy-start = (f32[384,4096]{1,0:T(8,128)}, f32[384,4096]{1,0:T(8,128)S(1)}, u32[]{:S(2)}) copy-start(f32[384,4096]{1,0:T(8,128)S(1)} %shard_map.57.before) | copy-start | bytes 18874372
  18.4 21.6 %collective-permute-start.1 = (bf16[64,4096]{1,0:T(8,128)(2,1)}, bf16[64,4096]{1,0:T(8,128)(2,1)}, u32[]{:S(2)}, u32[]{:S(2)}) collective-permute-start(bf16[64,4096]{1,0:T(8,128)(2,1)} %slice.20), channel_id=1, source_target_pairs={{0,2},{1,3},{2,0},{3,1},{4,6},{5,7},{6,4},{7,5},{8,10},{9,11},{10,... | collective-permute-start | bytes 1572872 | tf_op jit(solution)/shard_map/ppermute | solution.py:30
  19.6 20.4 %collective-permute-start.2 = (bf16[64,4096]{1,0:T(8,128)(2,1)}, bf16[64,4096]{1,0:T(8,128)(2,1)}, u32[]{:S(2)}, u32[]{:S(2)}) collective-permute-start(bf16[64,4096]{1,0:T(8,128)(2,1)} %collective-permute-done.refs_0_), channel_id=1, source_target_pairs={{0,4},{1,5},{4,8},{5,9},{6,2},{7,3},{8,12},{9,13},{10,6},{11,7},{1... | collective-permute-start | bytes 1572872 | tf_op jit(solution)/shard_map/ppermute | solution.py:30
  28.8 22.3 %collective-permute-start.6 = (bf16[64,4096]{1,0:T(8,128)(2,1)S(1)}, bf16[64,4096]{1,0:T(8,128)(2,1)S(1)}, u32[]{:S(2)}, u32[]{:S(2)}) collective-permute-start(bf16[64,4096]{1,0:T(8,128)(2,1)S(1)} %slice.22), channel_id=1, source_target_pairs={{0,2},{1,3},{2,0},{3,1},{4,6},{5,7},{6,4},{7,5},{8,10},{9,11},{10,... | collective-permute-start | bytes 1572872 | tf_op jit(solution)/shard_map/ppermute | solution.py:30
  30.1 21.0 %collective-permute-start.7 = (bf16[64,4096]{1,0:T(8,128)(2,1)}, bf16[64,4096]{1,0:T(8,128)(2,1)S(1)}, u32[]{:S(2)}, u32[]{:S(2)}) collective-permute-start(bf16[64,4096]{1,0:T(8,128)(2,1)} %collective-permute-done.3.refs_0_), channel_id=1, source_target_pairs={{0,4},{1,5},{4,8},{5,9},{6,2},{7,3},{8,12},{9,13},{10,6},{11,7},{1... | collective-permute-start | bytes 1572872 | tf_op jit(solution)/shard_map/ppermute | solution.py:30
  41.1 10.0 %collective-permute-start.8 = (bf16[64,4096]{1,0:T(8,128)(2,1)S(1)}, bf16[64,4096]{1,0:T(8,128)(2,1)S(1)}, u32[]{:S(2)}, u32[]{:S(2)}) collective-permute-start(bf16[64,4096]{1,0:T(8,128)(2,1)S(1)} %broadcast_select_fusion.5), channel_id=1, source_target_pairs={{0,1},{1,0},{2,3},{3,2},{4,5},{5,4},{6,7},{7,6},{8,9},{9,8},{10,11... | collective-permute-start | bytes 1572872 | tf_op jit(solution)/shard_map/ppermute | solution.py:30
  42.5 19.9 %collective-permute-start.4 = (bf16[64,4096]{1,0:T(8,128)(2,1)S(1)}, bf16[64,4096]{1,0:T(8,128)(2,1)S(1)}, u32[]{:S(2)}, u32[]{:S(2)}) collective-permute-start(bf16[64,4096]{1,0:T(8,128)(2,1)S(1)} %slice.21), channel_id=1, source_target_pairs={{0,2},{1,3},{2,0},{3,1},{4,6},{5,7},{6,4},{7,5},{8,10},{9,11},{10,... | collective-permute-start | bytes 1572872 | tf_op jit(solution)/shard_map/ppermute | solution.py:30
  43.8 18.5 %collective-permute-start.5 = (bf16[64,4096]{1,0:T(8,128)(2,1)}, bf16[64,4096]{1,0:T(8,128)(2,1)S(1)}, u32[]{:S(2)}, u32[]{:S(2)}) collective-permute-start(bf16[64,4096]{1,0:T(8,128)(2,1)} %collective-permute-done.1.refs_0_), channel_id=1, source_target_pairs={{0,4},{1,5},{4,8},{5,9},{6,2},{7,3},{8,12},{9,13},{10,6},{11,7},{1... | collective-permute-start | bytes 1572872 | tf_op jit(solution)/shard_map/ppermute | solution.py:30
  51.2 11.2 %collective-permute-start.10 = (bf16[64,4096]{1,0:T(8,128)(2,1)S(1)}, bf16[64,4096]{1,0:T(8,128)(2,1)S(1)}, u32[]{:S(2)}, u32[]{:S(2)}) collective-permute-start(bf16[64,4096]{1,0:T(8,128)(2,1)S(1)} %broadcast_select_fusion.4), channel_id=1, source_target_pairs={{0,1},{1,0},{2,3},{3,2},{4,5},{5,4},{6,7},{7,6},{8,9},{9,8},{10,11... | collective-permute-start | bytes 1572872 | tf_op jit(solution)/shard_map/ppermute | solution.py:30
  53.7 19.9 %collective-permute-start.11 = (bf16[64,4096]{1,0:T(8,128)(2,1)S(1)}, bf16[64,4096]{1,0:T(8,128)(2,1)S(1)}, u32[]{:S(2)}, u32[]{:S(2)}) collective-permute-start(bf16[64,4096]{1,0:T(8,128)(2,1)S(1)} %slice.23), channel_id=1, source_target_pairs={{0,2},{1,3},{2,0},{3,1},{4,6},{5,7},{6,4},{7,5},{8,10},{9,11},{10,... | collective-permute-start | bytes 1572872 | tf_op jit(solution)/shard_map/ppermute | solution.py:30
  53.9 19.7 %collective-permute-start.12 = (bf16[64,4096]{1,0:T(8,128)(2,1)S(1)}, bf16[64,4096]{1,0:T(8,128)(2,1)S(1)}, u32[]{:S(2)}, u32[]{:S(2)}) collective-permute-start(bf16[64,4096]{1,0:T(8,128)(2,1)S(1)} %collective-permute-done.6.refs_0_), channel_id=1, source_target_pairs={{0,4},{1,5},{4,8},{5,9},{6,2},{7,3},{8,12},{9,13},{10,6},{11,7},{1... | collective-permute-start | bytes 1572872 | tf_op jit(solution)/shard_map/ppermute | solution.py:30
  62.5 15.3 %copy-start.8 = (bf16[384,384]{1,0:T(8,128)(2,1)S(1)}, bf16[384,384]{1,0:T(8,128)(2,1)}, u32[]{:S(2)}) copy-start(bf16[384,384]{1,0:T(8,128)(2,1)} %copy-done.7) | copy-start | bytes 884740
  62.5 17.6 %copy-start.6 = (bf16[384,384]{1,0:T(8,128)(2,1)S(1)}, bf16[384,384]{1,0:T(8,128)(2,1)}, u32[]{:S(2)}) copy-start(bf16[384,384]{1,0:T(8,128)(2,1)} %copy-done.5) | copy-start | bytes 884740
  62.5 11.1 %collective-permute-start.13 = (bf16[64,4096]{1,0:T(8,128)(2,1)S(1)}, bf16[64,4096]{1,0:T(8,128)(2,1)S(1)}, u32[]{:S(2)}, u32[]{:S(2)}) collective-permute-start(bf16[64,4096]{1,0:T(8,128)(2,1)S(1)} %broadcast_select_fusion.3), channel_id=1, source_target_pairs={{0,1},{1,0},{2,3},{3,2},{4,5},{5,4},{6,7},{7,6},{8,9},{9,8},{10,11... | collective-permute-start | bytes 1572872 | tf_op jit(solution)/shard_map/ppermute | solution.py:30
  64.9 19.6 %collective-permute-start.14 = (bf16[64,4096]{1,0:T(8,128)(2,1)S(1)}, bf16[64,4096]{1,0:T(8,128)(2,1)S(1)}, u32[]{:S(2)}, u32[]{:S(2)}) collective-permute-start(bf16[64,4096]{1,0:T(8,128)(2,1)S(1)} %collective-permute-done.4.refs_0_), channel_id=1, source_target_pairs={{0,4},{1,5},{4,8},{5,9},{6,2},{7,3},{8,12},{9,13},{10,6},{11,7},{1... | collective-permute-start | bytes 1572872 | tf_op jit(solution)/shard_map/ppermute | solution.py:30
  73.7 13.1 %collective-permute-start.16 = (bf16[64,4096]{1,0:T(8,128)(2,1)S(1)}, bf16[64,4096]{1,0:T(8,128)(2,1)S(1)}, u32[]{:S(2)}, u32[]{:S(2)}) collective-permute-start(bf16[64,4096]{1,0:T(8,128)(2,1)S(1)} %broadcast_select_fusion.2), channel_id=1, source_target_pairs={{0,1},{1,0},{2,3},{3,2},{4,5},{5,4},{6,7},{7,6},{8,9},{9,8},{10,11... | collective-permute-start | bytes 1572872 | tf_op jit(solution)/shard_map/ppermute | solution.py:30
  74.6 18.2 %collective-permute-start.15 = (bf16[64,4096]{1,0:T(8,128)(2,1)S(1)}, bf16[64,4096]{1,0:T(8,128)(2,1)S(1)}, u32[]{:S(2)}, u32[]{:S(2)}) collective-permute-start(bf16[64,4096]{1,0:T(8,128)(2,1)S(1)} %collective-permute-done.11.refs_1_), channel_id=1, source_target_pairs={{0,4},{1,5},{4,8},{5,9},{6,2},{7,3},{8,12},{9,13},{10,6},{11,7},{1... | collective-permute-start | bytes 1572872 | tf_op jit(solution)/shard_map/ppermute | solution.py:30
  77.8 10.2 %collective-permute-start.17 = (bf16[384,384]{1,0:T(8,128)(2,1)S(1)}, bf16[384,384]{1,0:T(8,128)(2,1)S(1)}, u32[]{:S(2)}, u32[]{:S(2)}) collective-permute-start(bf16[384,384]{1,0:T(8,128)(2,1)S(1)} %copy-done.8), channel_id=1, source_target_pairs={{0,1},{1,2},{2,3},{3,4},{4,5},{5,6},{6,7},{7,8},{8,9},{9,10},{10,1... | collective-permute-start | bytes 884744 | tf_op jit(solution)/shard_map/ppermute | solution.py:30
  80.1 12.6 %collective-permute-start.18 = (bf16[384,384]{1,0:T(8,128)(2,1)S(1)}, bf16[384,384]{1,0:T(8,128)(2,1)S(1)}, u32[]{:S(2)}, u32[]{:S(2)}) collective-permute-start(bf16[384,384]{1,0:T(8,128)(2,1)S(1)} %copy-done.6), channel_id=1, source_target_pairs={{0,2},{1,3},{2,4},{3,5},{4,6},{5,7},{6,8},{7,9},{8,10},{9,11},{10,... | collective-permute-start | bytes 884744 | tf_op jit(solution)/shard_map/ppermute | solution.py:30
  86.8 7.5 %slice-start = ((s8[6291456]{0:T(1024)(128)(4,1)}), s8[4194304]{0:T(1024)(128)(4,1)S(1)}, s32[]{:S(2)}) async-start(s8[6291456]{0:T(1024)(128)(4,1)} %bitcast.5), calls=%async_computation | async-start | bytes 8388608
  86.8 7.5 %slice-start.1 = ((s8[6291456]{0:T(1024)(128)(4,1)}), s8[2097152]{0:T(1024)(128)(4,1)S(1)}, s32[]{:S(2)}) async-start(s8[6291456]{0:T(1024)(128)(4,1)} %bitcast.5), calls=%async_computation.1 | async-start | bytes 4194304
  88.0 6.3 %copy-start.2 = (bf16[384,384]{1,0:T(8,128)(2,1)S(1)}, bf16[384,384]{1,0:T(8,128)(2,1)}, u32[]{:S(2)}) copy-start(bf16[384,384]{1,0:T(8,128)(2,1)} %copy-done.1) | copy-start | bytes 884740
  92.9 6.1 %collective-permute-start.20 = (bf16[64,4096]{1,0:T(8,128)(2,1)S(1)}, bf16[64,4096]{1,0:T(8,128)(2,1)S(1)}, u32[]{:S(2)}, u32[]{:S(2)}) collective-permute-start(bf16[64,4096]{1,0:T(8,128)(2,1)S(1)} %broadcast_select_fusion), channel_id=1, source_target_pairs={{0,1},{1,0},{2,3},{3,2},{4,5},{5,4},{6,7},{7,6},{8,9},{9,8},{10,11... | collective-permute-start | bytes 1572872 | tf_op jit(solution)/shard_map/ppermute | solution.py:30
  94.2 4.9 %collective-permute-start.19 = (bf16[64,4096]{1,0:T(8,128)(2,1)S(1)}, bf16[64,4096]{1,0:T(8,128)(2,1)S(1)}, u32[]{:S(2)}, u32[]{:S(2)}) collective-permute-start(bf16[64,4096]{1,0:T(8,128)(2,1)S(1)} %broadcast_select_fusion.1), channel_id=1, source_target_pairs={{0,1},{1,0},{2,3},{3,2},{4,5},{5,4},{6,7},{7,6},{8,9},{9,8},{10,11... | collective-permute-start | bytes 1572872 | tf_op jit(solution)/shard_map/ppermute | solution.py:30

commit v5 on v4

--- a/solution.py
+++ b/solution.py
@@ -7,8 +7,8 @@
 from jax.experimental.pallas import tpu as pltpu
 from jax.sharding import PartitionSpec as P
 
-CUTS = (64,) * 6
-KAT = 5
+CUTS = (48,) * 8
+KAT = 7
 LAG = 3
 HOLD = 2
 TILE = 1024
@@ -240,7 +240,7 @@
             held["across", w + 1] = send(part(w + 1, now), across)
         held["onward", w - 1] = send(held["across", w - 1], onward)
         if w == KAT:
-            for o, down in enumerate((down0, down1)):
+            for o, down in ((1, down1), (0, down0)):
                 pairs = [(i, i + o + 1) for i in range(peers - o - 1)]
                 held["down", o] = send(after(down, now), pairs)
         if w >= LAG:
@@ -252,7 +252,7 @@
         join(("across", w), ("onward", w - LAG + 1), ("swap", w - LAG), "rows", "gram", "total")
     held["onward", last] = send(held["across", last], onward)
     if KAT > last:
-        for o, down in enumerate((down0, down1)):
+        for o, down in ((1, down1), (0, down0)):
             pairs = [(i, i + o + 1) for i in range(peers - o - 1)]
             held["down", o] = send(after(down, held["rows"]), pairs)
     kept = last + 1 - HOLD

time: 105 us -> 103 us (0.981)
  waiting for transfers between devices: 29.2 us -> 19.4 us
  starting transfers between devices: 40.5 us -> 48.9 us
    ppermute x21 -> x27, waiting for transfers between devices: 29.2 us -> 19.4 us  [send(): return lax.ppermute(array, 'pts', pairs)]
    ppermute x21 -> x27, starting transfers between devices: 40.5 us -> 48.9 us  [send(): return lax.ppermute(array, 'pts', pairs)]
    pallas_call x9 -> x11, Pallas kernels: 25.3 us -> 25.7 us  [call(): pl.pallas_call(body, out_shape=out, in_specs=[anywhere] * hbm + [vector]...]
    unnamed x24 -> x28, local copies, waits for them, and re-layouts: 2.69 us -> 2.72 us
  transfers between devices with their start and end apart: 21 -> 27, of which waited for: 8 -> 7; matrix products, arithmetic and copies ran while one was open for 2% -> 2% of each run, Pallas kernels for 20% -> 21%
where the time goes in v5:
time: 103 us
  starting transfers between devices  48.9 us (47%)
  Pallas kernels  27.8 us (27%)
  waiting for transfers between devices  19.4 us (19%)
  local copies, waits for them, and re-layouts  3.76 us (4%)
  between operations  1.39 us (1%)
  other arithmetic  1.37 us (1%)
    ppermute x27, starting transfers between devices, send(): return lax.ppermute(array, 'pts', pairs)  48.9 us
    pallas_call x11, Pallas kernels, call(): pl.pallas_call(body, out_shape=out, in_specs=[anywhere] * hbm + [vector]...  25.7 us
    ppermute x27, waiting for transfers between devices, send(): return lax.ppermute(array, 'pts', pairs)  19.4 us
    unnamed x28, local copies, waits for them, and re-layouts  2.72 us
    pallas_call x1, Pallas kernels, on_device(): pl.pallas_call(functools.partial(begin_body, spans[:2]), out_shape=(pltpu...  2.07 us
  transfers between devices with their start and end apart: 27, of which 7 were waited for; matrix products, arithmetic and copies ran while one was open for 2% of the time, Pallas kernels for 21%

profile of v5, /device:TPU:11, one launch (start us, length us, event | category | flops | bytes accessed | tf_op | source)
XLA Modules:
  0.0 102.6 jit_solution(8307438193442737685)
XLA Ops:
  0.7 2.1 %shard_map.55 = (bf16[384,4096]{1,0:T(8,128)(2,1)S(1)}, bf16[48,4096]{1,0:T(8,128)(2,1)}, bf16[48,4096]{1,0:T(8,128)(2,1)}) custom-call(bf16[384,4096]{1,0:T(8,128)(2,1)} %orbitals.1, s32[1]{0:T(128)S(6)} %copy.34.tally), custom_call_target="tpu_custom_call" | custom-call | tf_op jit(solution)/shard_map/pallas_call | solution.py:195
  2.8 0.7 collective-permute-start.9
  3.6 1.3 %collective-permute-start = (bf16[48,4096]{1,0:T(8,128)(2,1)}, bf16[48,4096]{1,0:T(8,128)(2,1)}, u32[]{:S(2)}, u32[]{:S(2)}) collective-permute-start(bf16[48,4096]{1,0:T(8,128)(2,1)} %get-tuple-element.84), channel_id=1, source_target_pairs={{0,2},{1,3},{2,0},{3,1},{4,6},{5,7},{6,4},{7,5},{8,10},{9,11},{10,... | collective-permute-start | bytes 1179656 | tf_op jit(solution)/shard_map/ppermute | solution.py:30
  4.8 0.2 collective-permute-start.3
  5.0 0.1 copy.19
  5.1 0.1 slice_bitcast_fusion
  5.2 0.8 shard_map.56
  6.0 3.5 %shard_map.57.before = f32[384,4096]{1,0:T(8,128)S(1)} custom-call(bf16[384,4096]{1,0:T(8,128)(2,1)S(1)} %get-tuple-element.128.own, bf16[384,384]{1,0:T(8,128)(2,1)S(1)} %copy-done.5), custom_call_target="tpu_custom_call" | custom-call | flops 2415919104 | bytes 24159192 | tf_op jit(solution)/shard_map/pallas_call | solution.py:58
  9.6 2.7 %copy-done = f32[384,4096]{1,0:T(8,128)} copy-done((f32[384,4096]{1,0:T(8,128)}, f32[384,4096]{1,0:T(8,128)S(1)}, u32[]{:S(2)}) %copy-start) | copy-done | bytes 6291480
  12.3 2.3 %collective-permute-done.refs_0_ = bf16[48,4096]{1,0:T(8,128)(2,1)} collective-permute-done((bf16[48,4096]{1,0:T(8,128)(2,1)}, bf16[48,4096]{1,0:T(8,128)(2,1)}, u32[]{:S(2)}, u32[]{:S(2)}) %collective-permute-start) | collective-permute-done | bytes 393248 | tf_op jit(solution)/shard_map/ppermute | solution.py:30
  14.6 0.8 slice.26
  15.3 1.2 %collective-permute-start.1 = (bf16[48,4096]{1,0:T(8,128)(2,1)}, bf16[48,4096]{1,0:T(8,128)(2,1)S(1)}, u32[]{:S(2)}, u32[]{:S(2)}) collective-permute-start(bf16[48,4096]{1,0:T(8,128)(2,1)} %slice.26), channel_id=1, source_target_pairs={{0,2},{1,3},{2,0},{3,1},{4,6},{5,7},{6,4},{7,5},{8,10},{9,11},{10,... | collective-permute-start | bytes 1179656 | tf_op jit(solution)/shard_map/ppermute | solution.py:30
  16.6 3.2 %collective-permute-start.2 = (bf16[48,4096]{1,0:T(8,128)(2,1)}, bf16[48,4096]{1,0:T(8,128)(2,1)}, u32[]{:S(2)}, u32[]{:S(2)}) collective-permute-start(bf16[48,4096]{1,0:T(8,128)(2,1)} %collective-permute-done.refs_0_), channel_id=1, source_target_pairs={{0,4},{1,5},{4,8},{5,9},{6,2},{7,3},{8,12},{9,13},{10,6},{11,7},{1... | collective-permute-start | bytes 1179656 | tf_op jit(solution)/shard_map/ppermute | solution.py:30
  19.8 3.2 %collective-permute-done.3.refs_0_ = bf16[48,4096]{1,0:T(8,128)(2,1)} collective-permute-done((bf16[48,4096]{1,0:T(8,128)(2,1)}, bf16[48,4096]{1,0:T(8,128)(2,1)}, u32[]{:S(2)}, u32[]{:S(2)}) %collective-permute-start.3) | collective-permute-done | bytes 393248 | tf_op jit(solution)/shard_map/ppermute | solution.py:30
  23.0 1.3 %collective-permute-start.6 = (bf16[48,4096]{1,0:T(8,128)(2,1)S(1)}, bf16[48,4096]{1,0:T(8,128)(2,1)S(1)}, u32[]{:S(2)}, u32[]{:S(2)}) collective-permute-start(bf16[48,4096]{1,0:T(8,128)(2,1)S(1)} %slice.28), channel_id=1, source_target_pairs={{0,2},{1,3},{2,0},{3,1},{4,6},{5,7},{6,4},{7,5},{8,10},{9,11},{10,... | collective-permute-start | bytes 1179656 | tf_op jit(solution)/shard_map/ppermute | solution.py:30
  24.3 3.2 %collective-permute-start.7 = (bf16[48,4096]{1,0:T(8,128)(2,1)}, bf16[48,4096]{1,0:T(8,128)(2,1)S(1)}, u32[]{:S(2)}, u32[]{:S(2)}) collective-permute-start(bf16[48,4096]{1,0:T(8,128)(2,1)} %collective-permute-done.3.refs_0_), channel_id=1, source_target_pairs={{0,4},{1,5},{4,8},{5,9},{6,2},{7,3},{8,12},{9,13},{10,6},{11,7},{1... | collective-permute-start | bytes 1179656 | tf_op jit(solution)/shard_map/ppermute | solution.py:30
  27.5 3.8 %collective-permute-done.1.refs_0_ = bf16[48,4096]{1,0:T(8,128)(2,1)S(1)} collective-permute-done((bf16[48,4096]{1,0:T(8,128)(2,1)}, bf16[48,4096]{1,0:T(8,128)(2,1)S(1)}, u32[]{:S(2)}, u32[]{:S(2)}) %collective-permute-start.1) | collective-permute-done | bytes 393248 | tf_op jit(solution)/shard_map/ppermute | solution.py:30
  31.3 0.0 collective-permute-done.2.refs_1_
  31.3 1.0 %broadcast_select_fusion.7 = bf16[48,4096]{1,0:T(8,128)(2,1)S(1)} fusion(bf16[48,4096]{1,0:T(8,128)(2,1)} %collective-permute-done.refs_0_, bf16[48,4096]{1,0:T(8,128)(2,1)} %collective-permute-done.2.refs_1_, pred[]{:T(512)S(6)} %eq.11), kind=kLoop, calls=%fused_computation.7 | loop fusion | flops 196608 | bytes 1179649 | tf_op jit(solution)/shard_map/jit(_where)/select_n | solution.py:231
  32.4 1.4 %collective-permute-start.8 = (bf16[48,4096]{1,0:T(8,128)(2,1)S(1)}, bf16[48,4096]{1,0:T(8,128)(2,1)S(1)}, u32[]{:S(2)}, u32[]{:S(2)}) collective-permute-start(bf16[48,4096]{1,0:T(8,128)(2,1)S(1)} %broadcast_select_fusion.7), channel_id=1, source_target_pairs={{0,1},{1,0},{2,3},{3,2},{4,5},{5,4},{6,7},{7,6},{8,9},{9,8},{10,11... | collective-permute-start | bytes 1179656 | tf_op jit(solution)/shard_map/ppermute | solution.py:30
  33.8 1.3 %collective-permute-start.4 = (bf16[48,4096]{1,0:T(8,128)(2,1)S(1)}, bf16[48,4096]{1,0:T(8,128)(2,1)S(1)}, u32[]{:S(2)}, u32[]{:S(2)}) collective-permute-start(bf16[48,4096]{1,0:T(8,128)(2,1)S(1)} %slice.27), channel_id=1, source_target_pairs={{0,2},{1,3},{2,0},{3,1},{4,6},{5,7},{6,4},{7,5},{8,10},{9,11},{10,... | collective-permute-start | bytes 1179656 | tf_op jit(solution)/shard_map/ppermute | solution.py:30
  35.1 0.0 collective-permute-done.9.refs_0_
  35.1 3.2 %collective-permute-start.5 = (bf16[48,4096]{1,0:T(8,128)(2,1)S(1)}, bf16[48,4096]{1,0:T(8,128)(2,1)S(1)}, u32[]{:S(2)}, u32[]{:S(2)}) collective-permute-start(bf16[48,4096]{1,0:T(8,128)(2,1)S(1)} %collective-permute-done.1.refs_0_), channel_id=1, source_target_pairs={{0,4},{1,5},{4,8},{5,9},{6,2},{7,3},{8,12},{9,13},{10,6},{11,7},{1... | collective-permute-start | bytes 1179656 | tf_op jit(solution)/shard_map/ppermute | solution.py:30
  38.3 3.7 %shard_map.58 = (bf16[1248,4096]{1,0:T(8,128)(2,1)S(1)}, f32[1248,384]{1,0:T(8,128)S(1)}) custom-call(bf16[384,4096]{1,0:T(8,128)(2,1)S(1)} %get-tuple-element.128.own, bf16[384,4096]{1,0:T(8,128)(2,1)} %collective-permute-done.9.refs_0_), custom_call_target="tpu_custom_call" | custom-call | flops 1207959552 | bytes 12079595 | tf_op jit(solution)/shard_map/pallas_call | solution.py:58
  42.0 0.0 collective-permute-done.6.refs_0_
  42.0 0.0 collective-permute-done.8.refs_2_
  42.0 0.1 broadcast_select_fusion.6
  42.1 1.6 %collective-permute-start.10 = (bf16[48,4096]{1,0:T(8,128)(2,1)S(1)}, bf16[48,4096]{1,0:T(8,128)(2,1)S(1)}, u32[]{:S(2)}, u32[]{:S(2)}) collective-permute-start(bf16[48,4096]{1,0:T(8,128)(2,1)S(1)} %broadcast_select_fusion.6), channel_id=1, source_target_pairs={{0,1},{1,0},{2,3},{3,2},{4,5},{5,4},{6,7},{7,6},{8,9},{9,8},{10,11... | collective-permute-start | bytes 1179656 | tf_op jit(solution)/shard_map/ppermute | solution.py:30
  43.7 0.1 collective-permute-start.13
  43.8 3.2 %collective-permute-start.14 = (bf16[48,4096]{1,0:T(8,128)(2,1)S(1)}, bf16[48,4096]{1,0:T(8,128)(2,1)S(1)}, u32[]{:S(2)}, u32[]{:S(2)}) collective-permute-start(bf16[48,4096]{1,0:T(8,128)(2,1)S(1)} %collective-permute-done.6.refs_0_), channel_id=1, source_target_pairs={{0,4},{1,5},{4,8},{5,9},{6,2},{7,3},{8,12},{9,13},{10,6},{11,7},{1... | collective-permute-start | bytes 1179656 | tf_op jit(solution)/shard_map/ppermute | solution.py:30
  47.0 2.2 %shard_map.59 = (bf16[1248,4096]{1,0:T(8,128)(2,1)S(1)}, f32[1248,384]{1,0:T(8,128)S(1)}) custom-call(bf16[384,4096]{1,0:T(8,128)(2,1)S(1)} %get-tuple-element.128.own, bf16[48,4096]{1,0:T(8,128)(2,1)} %collective-permute-done.refs_0_, bf16[48,4096]{1,0:T(8,128)(2,1)} %collective-permute-done.2.refs_1_, ...), custom_call_target="tpu_custom_call", output_to_operand_aliasing={{0}: (4, {}), {1}: (5, {})} | custom-call | flops 452984832 | bytes 4529848 | tf_op jit(solution)/shard_map/pallas_call | solution.py:58
  49.3 0.0 collective-permute-done.5.refs_1_
  49.3 0.0 collective-permute-done.10.refs_2_
  49.3 0.4 collective-permute-start.15
  49.7 1.2 %collective-permute-start.11 = (bf16[48,4096]{1,0:T(8,128)(2,1)S(1)}, bf16[48,4096]{1,0:T(8,128)(2,1)S(1)}, u32[]{:S(2)}, u32[]{:S(2)}) collective-permute-start(bf16[48,4096]{1,0:T(8,128)(2,1)S(1)} %slice.29), channel_id=1, source_target_pairs={{0,2},{1,3},{2,0},{3,1},{4,6},{5,7},{6,4},{7,5},{8,10},{9,11},{10,... | collective-permute-start | bytes 1179656 | tf_op jit(solution)/shard_map/ppermute | solution.py:30
  50.9 3.2 %collective-permute-start.12 = (bf16[48,4096]{1,0:T(8,128)(2,1)S(1)}, bf16[48,4096]{1,0:T(8,128)(2,1)S(1)}, u32[]{:S(2)}, u32[]{:S(2)}) collective-permute-start(bf16[48,4096]{1,0:T(8,128)(2,1)S(1)} %collective-permute-done.4.refs_0_), channel_id=1, source_target_pairs={{0,4},{1,5},{4,8},{5,9},{6,2},{7,3},{8,12},{9,13},{10,6},{11,7},{1... | collective-permute-start | bytes 1179656 | tf_op jit(solution)/shard_map/ppermute | solution.py:30
  54.1 2.1 %shard_map.60 = (bf16[1248,4096]{1,0:T(8,128)(2,1)S(1)}, f32[1248,384]{1,0:T(8,128)S(1)}) custom-call(bf16[384,4096]{1,0:T(8,128)(2,1)S(1)} %get-tuple-element.128.own, bf16[48,4096]{1,0:T(8,128)(2,1)} %collective-permute-done.3.refs_0_, bf16[48,4096]{1,0:T(8,128)(2,1)S(1)} %collective-permute-done.7.refs_1_, ...), custom_call_target="tpu_custom_call", output_to_operand_aliasing={{0}: (4, {}), {1}: (5, {})} | custom-call | flops 452984832 | bytes 4529848 | tf_op jit(solution)/shard_map/pallas_call | solution.py:58
  56.2 0.4 collective-permute-done.13.refs_0_
  56.6 1.4 %collective-permute-start.16 = (bf16[48,4096]{1,0:T(8,128)(2,1)S(1)}, bf16[48,4096]{1,0:T(8,128)(2,1)S(1)}, u32[]{:S(2)}, u32[]{:S(2)}) collective-permute-start(bf16[48,4096]{1,0:T(8,128)(2,1)S(1)} %broadcast_select_fusion.4), channel_id=1, source_target_pairs={{0,1},{1,0},{2,3},{3,2},{4,5},{5,4},{6,7},{7,6},{8,9},{9,8},{10,11... | collective-permute-start | bytes 1179656 | tf_op jit(solution)/shard_map/ppermute | solution.py:30
  58.0 1.6 %collective-permute-start.17 = (bf16[48,4096]{1,0:T(8,128)(2,1)S(1)}, bf16[48,4096]{1,0:T(8,128)(2,1)S(1)}, u32[]{:S(2)}, u32[]{:S(2)}) collective-permute-start(bf16[48,4096]{1,0:T(8,128)(2,1)S(1)} %slice.31), channel_id=1, source_target_pairs={{0,2},{1,3},{2,0},{3,1},{4,6},{5,7},{6,4},{7,5},{8,10},{9,11},{10,... | collective-permute-start | bytes 1179656 | tf_op jit(solution)/shard_map/ppermute | solution.py:30
  59.6 3.2 %collective-permute-start.18 = (bf16[48,4096]{1,0:T(8,128)(2,1)S(1)}, bf16[48,4096]{1,0:T(8,128)(2,1)S(1)}, u32[]{:S(2)}, u32[]{:S(2)}) collective-permute-start(bf16[48,4096]{1,0:T(8,128)(2,1)S(1)} %collective-permute-done.13.refs_0_), channel_id=1, source_target_pairs={{0,4},{1,5},{4,8},{5,9},{6,2},{7,3},{8,12},{9,13},{10,6},{11,7},{1... | collective-permute-start | bytes 1179656 | tf_op jit(solution)/shard_map/ppermute | solution.py:30
  62.8 1.1 %shard_map.61 = (bf16[1248,4096]{1,0:T(8,128)(2,1)S(1)}, f32[1248,384]{1,0:T(8,128)S(1)}) custom-call(bf16[384,4096]{1,0:T(8,128)(2,1)S(1)} %get-tuple-element.128.own, bf16[48,4096]{1,0:T(8,128)(2,1)S(1)} %collective-permute-done.1.refs_0_, bf16[48,4096]{1,0:T(8,128)(2,1)S(1)} %collective-permute-done.5.refs_1_, ...), custom_call_target="tpu_custom_call", output_to_operand_aliasing={{0}: (4, {}), {1}: (5, {})} | custom-call | flops 452984832 | bytes 4529848 | tf_op jit(solution)/shard_map/pallas_call | solution.py:58
  63.9 1.1 %collective-permute-done.11.refs_0_ = bf16[48,4096]{1,0:T(8,128)(2,1)S(1)} collective-permute-done((bf16[48,4096]{1,0:T(8,128)(2,1)S(1)}, bf16[48,4096]{1,0:T(8,128)(2,1)S(1)}, u32[]{:S(2)}, u32[]{:S(2)}) %collective-permute-start.11) | collective-permute-done | bytes 393248 | tf_op jit(solution)/shard_map/ppermute | solution.py:30
  65.0 0.0 collective-permute-done.12.refs_1_
  65.0 0.0 collective-permute-done.16.refs_2_
  65.1 1.4 %collective-permute-start.19 = (bf16[48,4096]{1,0:T(8,128)(2,1)S(1)}, bf16[48,4096]{1,0:T(8,128)(2,1)S(1)}, u32[]{:S(2)}, u32[]{:S(2)}) collective-permute-start(bf16[48,4096]{1,0:T(8,128)(2,1)S(1)} %broadcast_select_fusion.3), channel_id=1, source_target_pairs={{0,1},{1,0},{2,3},{3,2},{4,5},{5,4},{6,7},{7,6},{8,9},{9,8},{10,11... | collective-permute-start | bytes 1179656 | tf_op jit(solution)/shard_map/ppermute | solution.py:30
  66.5 3.2 %collective-permute-start.20 = (bf16[48,4096]{1,0:T(8,128)(2,1)S(1)}, bf16[48,4096]{1,0:T(8,128)(2,1)S(1)}, u32[]{:S(2)}, u32[]{:S(2)}) collective-permute-start(bf16[48,4096]{1,0:T(8,128)(2,1)S(1)} %collective-permute-done.11.refs_0_), channel_id=1, source_target_pairs={{0,4},{1,5},{4,8},{5,9},{6,2},{7,3},{8,12},{9,13},{10,6},{11,7},{1... | collective-permute-start | bytes 1179656 | tf_op jit(solution)/shard_map/ppermute | solution.py:30
  69.7 1.1 %shard_map.62 = (bf16[1248,4096]{1,0:T(8,128)(2,1)S(1)}, f32[1248,384]{1,0:T(8,128)S(1)}) custom-call(bf16[384,4096]{1,0:T(8,128)(2,1)S(1)} %get-tuple-element.128.own, bf16[48,4096]{1,0:T(8,128)(2,1)S(1)} %collective-permute-done.6.refs_0_, bf16[48,4096]{1,0:T(8,128)(2,1)S(1)} %collective-permute-done.14.refs_1_, ...), custom_call_target="tpu_custom_call", output_to_operand_aliasing={{0}: (4, {}), {1}: (5, {})} | custom-call | flops 452984832 | bytes 4529848 | tf_op jit(solution)/shard_map/pallas_call | solution.py:58
  70.8 2.7 %collective-permute-done.17.refs_1_ = bf16[48,4096]{1,0:T(8,128)(2,1)S(1)} collective-permute-done((bf16[48,4096]{1,0:T(8,128)(2,1)S(1)}, bf16[48,4096]{1,0:T(8,128)(2,1)S(1)}, u32[]{:S(2)}, u32[]{:S(2)}) %collective-permute-start.17) | collective-permute-done | bytes 393248 | tf_op jit(solution)/shard_map/ppermute | solution.py:30
  73.4 0.0 collective-permute-done.19.refs_2_
  73.5 1.1 %collective-permute-start.22 = (bf16[48,4096]{1,0:T(8,128)(2,1)S(1)}, bf16[48,4096]{1,0:T(8,128)(2,1)S(1)}, u32[]{:S(2)}, u32[]{:S(2)}) collective-permute-start(bf16[48,4096]{1,0:T(8,128)(2,1)S(1)} %broadcast_select_fusion.2), channel_id=1, source_target_pairs={{0,1},{1,0},{2,3},{3,2},{4,5},{5,4},{6,7},{7,6},{8,9},{9,8},{10,11... | collective-permute-start | bytes 1179656 | tf_op jit(solution)/shard_map/ppermute | solution.py:30
  74.6 3.2 %collective-permute-start.21 = (bf16[48,4096]{1,0:T(8,128)(2,1)S(1)}, bf16[48,4096]{1,0:T(8,128)(2,1)S(1)}, u32[]{:S(2)}, u32[]{:S(2)}) collective-permute-start(bf16[48,4096]{1,0:T(8,128)(2,1)S(1)} %collective-permute-done.17.refs_1_), channel_id=1, source_target_pairs={{0,4},{1,5},{4,8},{5,9},{6,2},{7,3},{8,12},{9,13},{10,6},{11,7},{1... | collective-permute-start | bytes 1179656 | tf_op jit(solution)/shard_map/ppermute | solution.py:30
  77.8 2.7 %collective-permute-start.23 = (bf16[384,384]{1,0:T(8,128)(2,1)S(1)}, bf16[384,384]{1,0:T(8,128)(2,1)S(1)}, u32[]{:S(2)}, u32[]{:S(2)}) collective-permute-start(bf16[384,384]{1,0:T(8,128)(2,1)S(1)} %copy-done.10), channel_id=1, source_target_pairs={{0,1},{1,2},{2,3},{3,4},{4,5},{5,6},{6,7},{7,8},{8,9},{9,10},{10,1... | collective-permute-start | bytes 884744 | tf_op jit(solution)/shard_map/ppermute | solution.py:30
  80.6 3.9 %collective-permute-start.24 = (bf16[384,384]{1,0:T(8,128)(2,1)S(1)}, bf16[384,384]{1,0:T(8,128)(2,1)S(1)}, u32[]{:S(2)}, u32[]{:S(2)}) collective-permute-start(bf16[384,384]{1,0:T(8,128)(2,1)S(1)} %copy-done.8), channel_id=1, source_target_pairs={{0,2},{1,3},{2,4},{3,5},{4,6},{5,7},{6,8},{7,9},{8,10},{9,11},{10,... | collective-permute-start | bytes 884744 | tf_op jit(solution)/shard_map/ppermute | solution.py:30
  84.5 1.1 %shard_map.63 = (bf16[1248,4096]{1,0:T(8,128)(2,1)S(1)}, f32[1248,384]{1,0:T(8,128)S(1)}) custom-call(bf16[384,4096]{1,0:T(8,128)(2,1)S(1)} %get-tuple-element.128.own, bf16[48,4096]{1,0:T(8,128)(2,1)S(1)} %collective-permute-done.4.refs_0_, bf16[48,4096]{1,0:T(8,128)(2,1)S(1)} %collective-permute-done.12.refs_1_, ...), custom_call_target="tpu_custom_call", output_to_operand_aliasing={{0}: (4, {}), {1}: (5, {})} | custom-call | flops 452984832 | bytes 4529848 | tf_op jit(solution)/shard_map/pallas_call | solution.py:58
  85.6 0.0 slice-start
  85.6 0.0 slice-start.1
  85.7 1.1 %shard_map.64 = (bf16[1248,4096]{1,0:T(8,128)(2,1)S(1)}, f32[1248,384]{1,0:T(8,128)S(1)}) custom-call(bf16[384,4096]{1,0:T(8,128)(2,1)S(1)} %get-tuple-element.128.own, bf16[48,4096]{1,0:T(8,128)(2,1)S(1)} %collective-permute-done.13.refs_0_, bf16[48,4096]{1,0:T(8,128)(2,1)S(1)} %collective-permute-done.18.refs_1_, ...), custom_call_target="tpu_custom_call", output_to_operand_aliasing={{0}: (4, {}), {1}: (5, {})} | custom-call | flops 452984832 | bytes 4529848 | tf_op jit(solution)/shard_map/pallas_call | solution.py:58
  86.8 5.9 %collective-permute-done.24.down1.refs_7_ = bf16[384,384]{1,0:T(8,128)(2,1)S(1)} collective-permute-done((bf16[384,384]{1,0:T(8,128)(2,1)S(1)}, bf16[384,384]{1,0:T(8,128)(2,1)S(1)}, u32[]{:S(2)}, u32[]{:S(2)}) %collective-permute-start.24) | collective-permute-done | bytes 294944 | tf_op jit(solution)/shard_map/ppermute | solution.py:30
  92.7 0.4 collective-permute-start.26
  93.1 0.1 broadcast_select_fusion.1
  93.2 0.3 collective-permute-start.25
  93.5 4.7 %shard_map.65.refs_10_ = f32[384,4096]{1,0:T(8,128)S(1)} custom-call(f32[1248,384]{1,0:T(8,128)S(1)} %get-tuple-element.158.gram, bf16[1248,4096]{1,0:T(8,128)(2,1)S(1)} %get-tuple-element.159.rows, bf16[384,384]{1,0:T(8,128)(2,1)S(1)} %collective-permute-done.23.down0.refs_6_, ...), custom_call_target="tpu_custom_call", output_to_operand_aliasing={{}: (6, {})} | custom-call | flops 3925868544 | bytes 39258684 | tf_op jit(solution)/shard_map/pallas_call | solution.py:58
  98.2 4.2 %shard_map.66 = bf16[384,4096]{1,0:T(8,128)(2,1)} custom-call(bf16[384,4096]{1,0:T(8,128)(2,1)S(1)} %get-tuple-element.128.own, bf16[48,4096]{1,0:T(8,128)(2,1)S(1)} %collective-permute-done.11.refs_0_, bf16[48,4096]{1,0:T(8,128)(2,1)S(1)} %collective-permute-done.17.refs_1_, bf16[48,4096]{1,0:T(8,128)(2,1)S(1)} %collective-permute-done.20.refs_2_, ...), custom_call_target="tpu_custom_call" | custom-call | flops 1811939328 | bytes 18119392 | tf_op jit(solution)/shard_map/pallas_call | solution.py:58
  (47 shorter events, 0.4 us)
Async XLA Ops:
  0.0 5.0 %copy-start.11 = (bf16[384,2,384]{2,1,0:T(2,128)(2,1)S(1)}, bf16[384,2,384]{2,1,0:T(2,128)(2,1)}, u32[]{:S(2)}) copy-start(bf16[384,2,384]{2,1,0:T(2,128)(2,1)} %param.7) | copy-start | bytes 1769476
  0.0 5.2 %copy-start.6 = (s32[1,2]{1,0:T(1,128)S(1)}, s32[1,2]{1,0:T(1,128)}, u32[]{:S(2)}) copy-start(s32[1,2]{1,0:T(1,128)} %couple.1) | copy-start | bytes 28
  0.0 6.0 %copy-start.5 = (bf16[384,384]{1,0:T(8,128)(2,1)S(1)}, bf16[384,384]{1,0:T(8,128)(2,1)}, u32[]{:S(2)}) copy-start(bf16[384,384]{1,0:T(8,128)(2,1)} %kern) | copy-start | bytes 884740
  2.8 32.3 %collective-permute-start.9 = (bf16[384,4096]{1,0:T(8,128)(2,1)S(1)}, bf16[384,4096]{1,0:T(8,128)(2,1)}, u32[]{:S(2)}, u32[]{:S(2)}) collective-permute-start(bf16[384,4096]{1,0:T(8,128)(2,1)S(1)} %get-tuple-element.128.own), channel_id=1, source_target_pairs={{0,1},{1,0},{2,3},{3,2},{4,5},{5,4},{6,7},{7,6},{8,9},{9,8},{10,11... | collective-permute-start | bytes 9437192 | tf_op jit(solution)/shard_map/ppermute | solution.py:30
  3.6 11.0 %collective-permute-start = (bf16[48,4096]{1,0:T(8,128)(2,1)}, bf16[48,4096]{1,0:T(8,128)(2,1)}, u32[]{:S(2)}, u32[]{:S(2)}) collective-permute-start(bf16[48,4096]{1,0:T(8,128)(2,1)} %get-tuple-element.84), channel_id=1, source_target_pairs={{0,2},{1,3},{2,0},{3,1},{4,6},{5,7},{6,4},{7,5},{8,10},{9,11},{10,... | collective-permute-start | bytes 1179656 | tf_op jit(solution)/shard_map/ppermute | solution.py:30
  4.8 18.2 %collective-permute-start.3 = (bf16[48,4096]{1,0:T(8,128)(2,1)}, bf16[48,4096]{1,0:T(8,128)(2,1)}, u32[]{:S(2)}, u32[]{:S(2)}) collective-permute-start(bf16[48,4096]{1,0:T(8,128)(2,1)} %get-tuple-element.91), channel_id=1, source_target_pairs={{0,2},{1,3},{2,0},{3,1},{4,6},{5,7},{6,4},{7,5},{8,10},{9,11},{10,... | collective-permute-start | bytes 1179656 | tf_op jit(solution)/shard_map/ppermute | solution.py:30
  6.0 3.6 %copy-start.1 = (bf16[384,384]{1,0:T(8,128)(2,1)}, bf16[384,384]{1,0:T(8,128)(2,1)S(1)}, u32[]{:S(2)}) copy-start(bf16[384,384]{1,0:T(8,128)(2,1)S(1)} %get-tuple-element.86.up0.refs_8_) | copy-start | bytes 884740
  6.0 3.6 %copy-start.3 = (bf16[384,384]{1,0:T(8,128)(2,1)}, bf16[384,384]{1,0:T(8,128)(2,1)S(1)}, u32[]{:S(2)}) copy-start(bf16[384,384]{1,0:T(8,128)(2,1)S(1)} %get-tuple-element.157.up1.refs_9_) | copy-start | bytes 884740
  6.0 3.6 %copy-start.7 = (bf16[384,384]{1,0:T(8,128)(2,1)}, bf16[384,384]{1,0:T(8,128)(2,1)S(1)}, u32[]{:S(2)}) copy-start(bf16[384,384]{1,0:T(8,128)(2,1)S(1)} %get-tuple-element.152) | copy-start | bytes 884740
  6.0 3.6 %copy-start.9 = (bf16[384,384]{1,0:T(8,128)(2,1)}, bf16[384,384]{1,0:T(8,128)(2,1)S(1)}, u32[]{:S(2)}) copy-start(bf16[384,384]{1,0:T(8,128)(2,1)S(1)} %get-tuple-element.150) | copy-start | bytes 884740
  9.6 2.7 %copy-start = (f32[384,4096]{1,0:T(8,128)}, f32[384,4096]{1,0:T(8,128)S(1)}, u32[]{:S(2)}) copy-start(f32[384,4096]{1,0:T(8,128)S(1)} %shard_map.57.before) | copy-start | bytes 18874372
  15.3 16.0 %collective-permute-start.1 = (bf16[48,4096]{1,0:T(8,128)(2,1)}, bf16[48,4096]{1,0:T(8,128)(2,1)S(1)}, u32[]{:S(2)}, u32[]{:S(2)}) collective-permute-start(bf16[48,4096]{1,0:T(8,128)(2,1)} %slice.26), channel_id=1, source_target_pairs={{0,2},{1,3},{2,0},{3,1},{4,6},{5,7},{6,4},{7,5},{8,10},{9,11},{10,... | collective-permute-start | bytes 1179656 | tf_op jit(solution)/shard_map/ppermute | solution.py:30
  16.6 14.7 %collective-permute-start.2 = (bf16[48,4096]{1,0:T(8,128)(2,1)}, bf16[48,4096]{1,0:T(8,128)(2,1)}, u32[]{:S(2)}, u32[]{:S(2)}) collective-permute-start(bf16[48,4096]{1,0:T(8,128)(2,1)} %collective-permute-done.refs_0_), channel_id=1, source_target_pairs={{0,4},{1,5},{4,8},{5,9},{6,2},{7,3},{8,12},{9,13},{10,6},{11,7},{1... | collective-permute-start | bytes 1179656 | tf_op jit(solution)/shard_map/ppermute | solution.py:30
  23.0 18.9 %collective-permute-start.6 = (bf16[48,4096]{1,0:T(8,128)(2,1)S(1)}, bf16[48,4096]{1,0:T(8,128)(2,1)S(1)}, u32[]{:S(2)}, u32[]{:S(2)}) collective-permute-start(bf16[48,4096]{1,0:T(8,128)(2,1)S(1)} %slice.28), channel_id=1, source_target_pairs={{0,2},{1,3},{2,0},{3,1},{4,6},{5,7},{6,4},{7,5},{8,10},{9,11},{10,... | collective-permute-start | bytes 1179656 | tf_op jit(solution)/shard_map/ppermute | solution.py:30
  24.3 17.7 %collective-permute-start.7 = (bf16[48,4096]{1,0:T(8,128)(2,1)}, bf16[48,4096]{1,0:T(8,128)(2,1)S(1)}, u32[]{:S(2)}, u32[]{:S(2)}) collective-permute-start(bf16[48,4096]{1,0:T(8,128)(2,1)} %collective-permute-done.3.refs_0_), channel_id=1, source_target_pairs={{0,4},{1,5},{4,8},{5,9},{6,2},{7,3},{8,12},{9,13},{10,6},{11,7},{1... | collective-permute-start | bytes 1179656 | tf_op jit(solution)/shard_map/ppermute | solution.py:30
  32.4 9.6 %collective-permute-start.8 = (bf16[48,4096]{1,0:T(8,128)(2,1)S(1)}, bf16[48,4096]{1,0:T(8,128)(2,1)S(1)}, u32[]{:S(2)}, u32[]{:S(2)}) collective-permute-start(bf16[48,4096]{1,0:T(8,128)(2,1)S(1)} %broadcast_select_fusion.7), channel_id=1, source_target_pairs={{0,1},{1,0},{2,3},{3,2},{4,5},{5,4},{6,7},{7,6},{8,9},{9,8},{10,11... | collective-permute-start | bytes 1179656 | tf_op jit(solution)/shard_map/ppermute | solution.py:30
  33.8 15.5 %collective-permute-start.4 = (bf16[48,4096]{1,0:T(8,128)(2,1)S(1)}, bf16[48,4096]{1,0:T(8,128)(2,1)S(1)}, u32[]{:S(2)}, u32[]{:S(2)}) collective-permute-start(bf16[48,4096]{1,0:T(8,128)(2,1)S(1)} %slice.27), channel_id=1, source_target_pairs={{0,2},{1,3},{2,0},{3,1},{4,6},{5,7},{6,4},{7,5},{8,10},{9,11},{10,... | collective-permute-start | bytes 1179656 | tf_op jit(solution)/shard_map/ppermute | solution.py:30
  35.1 14.2 %collective-permute-start.5 = (bf16[48,4096]{1,0:T(8,128)(2,1)S(1)}, bf16[48,4096]{1,0:T(8,128)(2,1)S(1)}, u32[]{:S(2)}, u32[]{:S(2)}) collective-permute-start(bf16[48,4096]{1,0:T(8,128)(2,1)S(1)} %collective-permute-done.1.refs_0_), channel_id=1, source_target_pairs={{0,4},{1,5},{4,8},{5,9},{6,2},{7,3},{8,12},{9,13},{10,6},{11,7},{1... | collective-permute-start | bytes 1179656 | tf_op jit(solution)/shard_map/ppermute | solution.py:30
  42.1 7.2 %collective-permute-start.10 = (bf16[48,4096]{1,0:T(8,128)(2,1)S(1)}, bf16[48,4096]{1,0:T(8,128)(2,1)S(1)}, u32[]{:S(2)}, u32[]{:S(2)}) collective-permute-start(bf16[48,4096]{1,0:T(8,128)(2,1)S(1)} %broadcast_select_fusion.6), channel_id=1, source_target_pairs={{0,1},{1,0},{2,3},{3,2},{4,5},{5,4},{6,7},{7,6},{8,9},{9,8},{10,11... | collective-permute-start | bytes 1179656 | tf_op jit(solution)/shard_map/ppermute | solution.py:30
  43.7 12.9 %collective-permute-start.13 = (bf16[48,4096]{1,0:T(8,128)(2,1)S(1)}, bf16[48,4096]{1,0:T(8,128)(2,1)S(1)}, u32[]{:S(2)}, u32[]{:S(2)}) collective-permute-start(bf16[48,4096]{1,0:T(8,128)(2,1)S(1)} %slice.30), channel_id=1, source_target_pairs={{0,2},{1,3},{2,0},{3,1},{4,6},{5,7},{6,4},{7,5},{8,10},{9,11},{10,... | collective-permute-start | bytes 1179656 | tf_op jit(solution)/shard_map/ppermute | solution.py:30
  43.8 12.8 %collective-permute-start.14 = (bf16[48,4096]{1,0:T(8,128)(2,1)S(1)}, bf16[48,4096]{1,0:T(8,128)(2,1)S(1)}, u32[]{:S(2)}, u32[]{:S(2)}) collective-permute-start(bf16[48,4096]{1,0:T(8,128)(2,1)S(1)} %collective-permute-done.6.refs_0_), channel_id=1, source_target_pairs={{0,4},{1,5},{4,8},{5,9},{6,2},{7,3},{8,12},{9,13},{10,6},{11,7},{1... | collective-permute-start | bytes 1179656 | tf_op jit(solution)/shard_map/ppermute | solution.py:30
  49.3 7.3 %collective-permute-start.15 = (bf16[48,4096]{1,0:T(8,128)(2,1)S(1)}, bf16[48,4096]{1,0:T(8,128)(2,1)S(1)}, u32[]{:S(2)}, u32[]{:S(2)}) collective-permute-start(bf16[48,4096]{1,0:T(8,128)(2,1)S(1)} %broadcast_select_fusion.5), channel_id=1, source_target_pairs={{0,1},{1,0},{2,3},{3,2},{4,5},{5,4},{6,7},{7,6},{8,9},{9,8},{10,11... | collective-permute-start | bytes 1179656 | tf_op jit(solution)/shard_map/ppermute | solution.py:30
  49.7 15.3 %collective-permute-start.11 = (bf16[48,4096]{1,0:T(8,128)(2,1)S(1)}, bf16[48,4096]{1,0:T(8,128)(2,1)S(1)}, u32[]{:S(2)}, u32[]{:S(2)}) collective-permute-start(bf16[48,4096]{1,0:T(8,128)(2,1)S(1)} %slice.29), channel_id=1, source_target_pairs={{0,2},{1,3},{2,0},{3,1},{4,6},{5,7},{6,4},{7,5},{8,10},{9,11},{10,... | collective-permute-start | bytes 1179656 | tf_op jit(solution)/shard_map/ppermute | solution.py:30
  50.9 14.1 %collective-permute-start.12 = (bf16[48,4096]{1,0:T(8,128)(2,1)S(1)}, bf16[48,4096]{1,0:T(8,128)(2,1)S(1)}, u32[]{:S(2)}, u32[]{:S(2)}) collective-permute-start(bf16[48,4096]{1,0:T(8,128)(2,1)S(1)} %collective-permute-done.4.refs_0_), channel_id=1, source_target_pairs={{0,4},{1,5},{4,8},{5,9},{6,2},{7,3},{8,12},{9,13},{10,6},{11,7},{1... | collective-permute-start | bytes 1179656 | tf_op jit(solution)/shard_map/ppermute | solution.py:30
  56.6 8.4 %collective-permute-start.16 = (bf16[48,4096]{1,0:T(8,128)(2,1)S(1)}, bf16[48,4096]{1,0:T(8,128)(2,1)S(1)}, u32[]{:S(2)}, u32[]{:S(2)}) collective-permute-start(bf16[48,4096]{1,0:T(8,128)(2,1)S(1)} %broadcast_select_fusion.4), channel_id=1, source_target_pairs={{0,1},{1,0},{2,3},{3,2},{4,5},{5,4},{6,7},{7,6},{8,9},{9,8},{10,11... | collective-permute-start | bytes 1179656 | tf_op jit(solution)/shard_map/ppermute | solution.py:30
  58.0 15.4 %collective-permute-start.17 = (bf16[48,4096]{1,0:T(8,128)(2,1)S(1)}, bf16[48,4096]{1,0:T(8,128)(2,1)S(1)}, u32[]{:S(2)}, u32[]{:S(2)}) collective-permute-start(bf16[48,4096]{1,0:T(8,128)(2,1)S(1)} %slice.31), channel_id=1, source_target_pairs={{0,2},{1,3},{2,0},{3,1},{4,6},{5,7},{6,4},{7,5},{8,10},{9,11},{10,... | collective-permute-start | bytes 1179656 | tf_op jit(solution)/shard_map/ppermute | solution.py:30
  59.6 13.9 %collective-permute-start.18 = (bf16[48,4096]{1,0:T(8,128)(2,1)S(1)}, bf16[48,4096]{1,0:T(8,128)(2,1)S(1)}, u32[]{:S(2)}, u32[]{:S(2)}) collective-permute-start(bf16[48,4096]{1,0:T(8,128)(2,1)S(1)} %collective-permute-done.13.refs_0_), channel_id=1, source_target_pairs={{0,4},{1,5},{4,8},{5,9},{6,2},{7,3},{8,12},{9,13},{10,6},{11,7},{1... | collective-permute-start | bytes 1179656 | tf_op jit(solution)/shard_map/ppermute | solution.py:30
  65.1 12.7 %copy-start.10 = (bf16[384,384]{1,0:T(8,128)(2,1)S(1)}, bf16[384,384]{1,0:T(8,128)(2,1)}, u32[]{:S(2)}) copy-start(bf16[384,384]{1,0:T(8,128)(2,1)} %copy-done.9) | copy-start | bytes 884740
  65.1 15.5 %copy-start.8 = (bf16[384,384]{1,0:T(8,128)(2,1)S(1)}, bf16[384,384]{1,0:T(8,128)(2,1)}, u32[]{:S(2)}) copy-start(bf16[384,384]{1,0:T(8,128)(2,1)} %copy-done.7) | copy-start | bytes 884740
  65.1 8.4 %collective-permute-start.19 = (bf16[48,4096]{1,0:T(8,128)(2,1)S(1)}, bf16[48,4096]{1,0:T(8,128)(2,1)S(1)}, u32[]{:S(2)}, u32[]{:S(2)}) collective-permute-start(bf16[48,4096]{1,0:T(8,128)(2,1)S(1)} %broadcast_select_fusion.3), channel_id=1, source_target_pairs={{0,1},{1,0},{2,3},{3,2},{4,5},{5,4},{6,7},{7,6},{8,9},{9,8},{10,11... | collective-permute-start | bytes 1179656 | tf_op jit(solution)/shard_map/ppermute | solution.py:30
  66.5 18.0 %collective-permute-start.20 = (bf16[48,4096]{1,0:T(8,128)(2,1)S(1)}, bf16[48,4096]{1,0:T(8,128)(2,1)S(1)}, u32[]{:S(2)}, u32[]{:S(2)}) collective-permute-start(bf16[48,4096]{1,0:T(8,128)(2,1)S(1)} %collective-permute-done.11.refs_0_), channel_id=1, source_target_pairs={{0,4},{1,5},{4,8},{5,9},{6,2},{7,3},{8,12},{9,13},{10,6},{11,7},{1... | collective-permute-start | bytes 1179656 | tf_op jit(solution)/shard_map/ppermute | solution.py:30
  73.5 12.1 %collective-permute-start.22 = (bf16[48,4096]{1,0:T(8,128)(2,1)S(1)}, bf16[48,4096]{1,0:T(8,128)(2,1)S(1)}, u32[]{:S(2)}, u32[]{:S(2)}) collective-permute-start(bf16[48,4096]{1,0:T(8,128)(2,1)S(1)} %broadcast_select_fusion.2), channel_id=1, source_target_pairs={{0,1},{1,0},{2,3},{3,2},{4,5},{5,4},{6,7},{7,6},{8,9},{9,8},{10,11... | collective-permute-start | bytes 1179656 | tf_op jit(solution)/shard_map/ppermute | solution.py:30
  74.6 18.1 %collective-permute-start.21 = (bf16[48,4096]{1,0:T(8,128)(2,1)S(1)}, bf16[48,4096]{1,0:T(8,128)(2,1)S(1)}, u32[]{:S(2)}, u32[]{:S(2)}) collective-permute-start(bf16[48,4096]{1,0:T(8,128)(2,1)S(1)} %collective-permute-done.17.refs_1_), channel_id=1, source_target_pairs={{0,4},{1,5},{4,8},{5,9},{6,2},{7,3},{8,12},{9,13},{10,6},{11,7},{1... | collective-permute-start | bytes 1179656 | tf_op jit(solution)/shard_map/ppermute | solution.py:30
  77.8 9.0 %collective-permute-start.23 = (bf16[384,384]{1,0:T(8,128)(2,1)S(1)}, bf16[384,384]{1,0:T(8,128)(2,1)S(1)}, u32[]{:S(2)}, u32[]{:S(2)}) collective-permute-start(bf16[384,384]{1,0:T(8,128)(2,1)S(1)} %copy-done.10), channel_id=1, source_target_pairs={{0,1},{1,2},{2,3},{3,4},{4,5},{5,6},{6,7},{7,8},{8,9},{9,10},{10,1... | collective-permute-start | bytes 884744 | tf_op jit(solution)/shard_map/ppermute | solution.py:30
  80.6 12.1 %collective-permute-start.24 = (bf16[384,384]{1,0:T(8,128)(2,1)S(1)}, bf16[384,384]{1,0:T(8,128)(2,1)S(1)}, u32[]{:S(2)}, u32[]{:S(2)}) collective-permute-start(bf16[384,384]{1,0:T(8,128)(2,1)S(1)} %copy-done.8), channel_id=1, source_target_pairs={{0,2},{1,3},{2,4},{3,5},{4,6},{5,7},{6,8},{7,9},{8,10},{9,11},{10,... | collective-permute-start | bytes 884744 | tf_op jit(solution)/shard_map/ppermute | solution.py:30
  85.6 7.8 %slice-start = ((s8[6291456]{0:T(1024)(128)(4,1)}), s8[4194304]{0:T(1024)(128)(4,1)S(1)}, s32[]{:S(2)}) async-start(s8[6291456]{0:T(1024)(128)(4,1)} %bitcast.5), calls=%async_computation | async-start | bytes 8388608
  85.6 7.8 %slice-start.1 = ((s8[6291456]{0:T(1024)(128)(4,1)}), s8[2097152]{0:T(1024)(128)(4,1)S(1)}, s32[]{:S(2)}) async-start(s8[6291456]{0:T(1024)(128)(4,1)} %bitcast.5), calls=%async_computation.1 | async-start | bytes 4194304
  85.6 7.8 %copy-start.2 = (bf16[384,384]{1,0:T(8,128)(2,1)S(1)}, bf16[384,384]{1,0:T(8,128)(2,1)}, u32[]{:S(2)}) copy-start(bf16[384,384]{1,0:T(8,128)(2,1)} %copy-done.1) | copy-start | bytes 884740
  85.7 7.8 %copy-start.4 = (bf16[384,384]{1,0:T(8,128)(2,1)S(1)}, bf16[384,384]{1,0:T(8,128)(2,1)}, u32[]{:S(2)}) copy-start(bf16[384,384]{1,0:T(8,128)(2,1)} %copy-done.3) | copy-start | bytes 884740
  92.7 5.4 %collective-permute-start.26 = (bf16[48,4096]{1,0:T(8,128)(2,1)S(1)}, bf16[48,4096]{1,0:T(8,128)(2,1)S(1)}, u32[]{:S(2)}, u32[]{:S(2)}) collective-permute-start(bf16[48,4096]{1,0:T(8,128)(2,1)S(1)} %broadcast_select_fusion), channel_id=1, source_target_pairs={{0,1},{1,0},{2,3},{3,2},{4,5},{5,4},{6,7},{7,6},{8,9},{9,8},{10,11... | collective-permute-start | bytes 1179656 | tf_op jit(solution)/shard_map/ppermute | solution.py:30
  93.2 5.0 %collective-permute-start.25 = (bf16[48,4096]{1,0:T(8,128)(2,1)S(1)}, bf16[48,4096]{1,0:T(8,128)(2,1)S(1)}, u32[]{:S(2)}, u32[]{:S(2)}) collective-permute-start(bf16[48,4096]{1,0:T(8,128)(2,1)S(1)} %broadcast_select_fusion.1), channel_id=1, source_target_pairs={{0,1},{1,0},{2,3},{3,2},{4,5},{5,4},{6,7},{7,6},{8,9},{9,8},{10,11... | collective-permute-start | bytes 1179656 | tf_op jit(solution)/shard_map/ppermute | solution.py:30

commit v6 on v5

--- a/solution.py
+++ b/solution.py
@@ -262,7 +262,7 @@
     for i in range(last - LAG, kept):
         collected(i)
     gate = [("onward", i) for i in range(kept, last + 1)]
-    join(*gate, "rows", "gram", ("down", 0), ("down", 1))
+    join(*gate, "rows", "gram")
     for i in range(kept, last + 1):
         swap(i)
     kerns = [held["down", 0], held["down", 1], up0, up1]

time: 103 us -> 102 us (level)
  waiting for transfers between devices: 19.4 us -> 18.3 us
    ppermute x27, waiting for transfers between devices: 19.4 us -> 18.3 us  [send(): return lax.ppermute(array, 'pts', pairs)]
  transfers between devices with their start and end apart: 27 -> 27, of which waited for: 7 -> 8; matrix products, arithmetic and copies ran while one was open for 2% -> 2% of each run, Pallas kernels for 21% -> 21%
where the time goes in v6:
time: 102 us
  starting transfers between devices  49.2 us (48%)
  Pallas kernels  27.8 us (27%)
  waiting for transfers between devices  18.3 us (18%)
  local copies, waits for them, and re-layouts  3.76 us (4%)
  between operations  1.4 us (1%)
  other arithmetic  1.37 us (1%)
    ppermute x27, starting transfers between devices, send(): return lax.ppermute(array, 'pts', pairs)  49.2 us
    pallas_call x11, Pallas kernels, call(): pl.pallas_call(body, out_shape=out, in_specs=[anywhere] * hbm + [vector]...  25.7 us
    ppermute x27, waiting for transfers between devices, send(): return lax.ppermute(array, 'pts', pairs)  18.3 us
    unnamed x28, local copies, waits for them, and re-layouts  2.72 us
    pallas_call x1, Pallas kernels, on_device(): pl.pallas_call(functools.partial(begin_body, spans[:2]), out_shape=(pltpu...  2.07 us
  transfers between devices with their start and end apart: 27, of which 8 were waited for; matrix products, arithmetic and copies ran while one was open for 2% of the time, Pallas kernels for 21%

profile of v6, /device:TPU:11, one launch (start us, length us, event | category | flops | bytes accessed | tf_op | source)
XLA Modules:
  0.0 101.9 jit_solution(6603007812359435698)
XLA Ops:
  0.7 2.1 %shard_map.55 = (bf16[384,4096]{1,0:T(8,128)(2,1)S(1)}, bf16[48,4096]{1,0:T(8,128)(2,1)}, bf16[48,4096]{1,0:T(8,128)(2,1)}) custom-call(bf16[384,4096]{1,0:T(8,128)(2,1)} %orbitals.1, s32[1]{0:T(128)S(6)} %copy.34.tally), custom_call_target="tpu_custom_call" | custom-call | tf_op jit(solution)/shard_map/pallas_call | solution.py:195
  2.8 0.7 collective-permute-start.9
  3.6 1.3 %collective-permute-start = (bf16[48,4096]{1,0:T(8,128)(2,1)}, bf16[48,4096]{1,0:T(8,128)(2,1)}, u32[]{:S(2)}, u32[]{:S(2)}) collective-permute-start(bf16[48,4096]{1,0:T(8,128)(2,1)} %get-tuple-element.82), channel_id=1, source_target_pairs={{0,2},{1,3},{2,0},{3,1},{4,6},{5,7},{6,4},{7,5},{8,10},{9,11},{10,... | collective-permute-start | bytes 1179656 | tf_op jit(solution)/shard_map/ppermute | solution.py:30
  4.8 0.2 collective-permute-start.3
  5.0 0.1 copy.19
  5.1 0.1 slice_bitcast_fusion
  5.2 0.8 shard_map.56
  6.0 3.5 %shard_map.57.before = f32[384,4096]{1,0:T(8,128)S(1)} custom-call(bf16[384,4096]{1,0:T(8,128)(2,1)S(1)} %get-tuple-element.126.own, bf16[384,384]{1,0:T(8,128)(2,1)S(1)} %copy-done.5), custom_call_target="tpu_custom_call" | custom-call | flops 2415919104 | bytes 24159192 | tf_op jit(solution)/shard_map/pallas_call | solution.py:58
  9.6 2.7 %copy-done = f32[384,4096]{1,0:T(8,128)} copy-done((f32[384,4096]{1,0:T(8,128)}, f32[384,4096]{1,0:T(8,128)S(1)}, u32[]{:S(2)}) %copy-start) | copy-done | bytes 6291480
  12.3 2.3 %collective-permute-done.refs_0_ = bf16[48,4096]{1,0:T(8,128)(2,1)} collective-permute-done((bf16[48,4096]{1,0:T(8,128)(2,1)}, bf16[48,4096]{1,0:T(8,128)(2,1)}, u32[]{:S(2)}, u32[]{:S(2)}) %collective-permute-start) | collective-permute-done | bytes 393248 | tf_op jit(solution)/shard_map/ppermute | solution.py:30
  14.6 0.8 slice.26
  15.3 1.2 %collective-permute-start.1 = (bf16[48,4096]{1,0:T(8,128)(2,1)}, bf16[48,4096]{1,0:T(8,128)(2,1)S(1)}, u32[]{:S(2)}, u32[]{:S(2)}) collective-permute-start(bf16[48,4096]{1,0:T(8,128)(2,1)} %slice.26), channel_id=1, source_target_pairs={{0,2},{1,3},{2,0},{3,1},{4,6},{5,7},{6,4},{7,5},{8,10},{9,11},{10,... | collective-permute-start | bytes 1179656 | tf_op jit(solution)/shard_map/ppermute | solution.py:30
  16.6 3.2 %collective-permute-start.2 = (bf16[48,4096]{1,0:T(8,128)(2,1)}, bf16[48,4096]{1,0:T(8,128)(2,1)}, u32[]{:S(2)}, u32[]{:S(2)}) collective-permute-start(bf16[48,4096]{1,0:T(8,128)(2,1)} %collective-permute-done.refs_0_), channel_id=1, source_target_pairs={{0,4},{1,5},{4,8},{5,9},{6,2},{7,3},{8,12},{9,13},{10,6},{11,7},{1... | collective-permute-start | bytes 1179656 | tf_op jit(solution)/shard_map/ppermute | solution.py:30
  19.8 3.2 %collective-permute-done.3.refs_0_ = bf16[48,4096]{1,0:T(8,128)(2,1)} collective-permute-done((bf16[48,4096]{1,0:T(8,128)(2,1)}, bf16[48,4096]{1,0:T(8,128)(2,1)}, u32[]{:S(2)}, u32[]{:S(2)}) %collective-permute-start.3) | collective-permute-done | bytes 393248 | tf_op jit(solution)/shard_map/ppermute | solution.py:30
  23.0 1.3 %collective-permute-start.6 = (bf16[48,4096]{1,0:T(8,128)(2,1)S(1)}, bf16[48,4096]{1,0:T(8,128)(2,1)S(1)}, u32[]{:S(2)}, u32[]{:S(2)}) collective-permute-start(bf16[48,4096]{1,0:T(8,128)(2,1)S(1)} %slice.28), channel_id=1, source_target_pairs={{0,2},{1,3},{2,0},{3,1},{4,6},{5,7},{6,4},{7,5},{8,10},{9,11},{10,... | collective-permute-start | bytes 1179656 | tf_op jit(solution)/shard_map/ppermute | solution.py:30
  24.3 3.2 %collective-permute-start.7 = (bf16[48,4096]{1,0:T(8,128)(2,1)}, bf16[48,4096]{1,0:T(8,128)(2,1)S(1)}, u32[]{:S(2)}, u32[]{:S(2)}) collective-permute-start(bf16[48,4096]{1,0:T(8,128)(2,1)} %collective-permute-done.3.refs_0_), channel_id=1, source_target_pairs={{0,4},{1,5},{4,8},{5,9},{6,2},{7,3},{8,12},{9,13},{10,6},{11,7},{1... | collective-permute-start | bytes 1179656 | tf_op jit(solution)/shard_map/ppermute | solution.py:30
  27.5 3.8 %collective-permute-done.1.refs_0_ = bf16[48,4096]{1,0:T(8,128)(2,1)S(1)} collective-permute-done((bf16[48,4096]{1,0:T(8,128)(2,1)}, bf16[48,4096]{1,0:T(8,128)(2,1)S(1)}, u32[]{:S(2)}, u32[]{:S(2)}) %collective-permute-start.1) | collective-permute-done | bytes 393248 | tf_op jit(solution)/shard_map/ppermute | solution.py:30
  31.3 0.0 collective-permute-done.2.refs_1_
  31.3 1.0 %broadcast_select_fusion.7 = bf16[48,4096]{1,0:T(8,128)(2,1)S(1)} fusion(bf16[48,4096]{1,0:T(8,128)(2,1)} %collective-permute-done.refs_0_, bf16[48,4096]{1,0:T(8,128)(2,1)} %collective-permute-done.2.refs_1_, pred[]{:T(512)S(6)} %eq.11), kind=kLoop, calls=%fused_computation.7 | loop fusion | flops 196608 | bytes 1179649 | tf_op jit(solution)/shard_map/jit(_where)/select_n | solution.py:231
  32.4 1.4 %collective-permute-start.8 = (bf16[48,4096]{1,0:T(8,128)(2,1)S(1)}, bf16[48,4096]{1,0:T(8,128)(2,1)S(1)}, u32[]{:S(2)}, u32[]{:S(2)}) collective-permute-start(bf16[48,4096]{1,0:T(8,128)(2,1)S(1)} %broadcast_select_fusion.7), channel_id=1, source_target_pairs={{0,1},{1,0},{2,3},{3,2},{4,5},{5,4},{6,7},{7,6},{8,9},{9,8},{10,11... | collective-permute-start | bytes 1179656 | tf_op jit(solution)/shard_map/ppermute | solution.py:30
  33.8 1.3 %collective-permute-start.4 = (bf16[48,4096]{1,0:T(8,128)(2,1)S(1)}, bf16[48,4096]{1,0:T(8,128)(2,1)S(1)}, u32[]{:S(2)}, u32[]{:S(2)}) collective-permute-start(bf16[48,4096]{1,0:T(8,128)(2,1)S(1)} %slice.27), channel_id=1, source_target_pairs={{0,2},{1,3},{2,0},{3,1},{4,6},{5,7},{6,4},{7,5},{8,10},{9,11},{10,... | collective-permute-start | bytes 1179656 | tf_op jit(solution)/shard_map/ppermute | solution.py:30
  35.1 0.0 collective-permute-done.9.refs_0_
  35.1 3.2 %collective-permute-start.5 = (bf16[48,4096]{1,0:T(8,128)(2,1)S(1)}, bf16[48,4096]{1,0:T(8,128)(2,1)S(1)}, u32[]{:S(2)}, u32[]{:S(2)}) collective-permute-start(bf16[48,4096]{1,0:T(8,128)(2,1)S(1)} %collective-permute-done.1.refs_0_), channel_id=1, source_target_pairs={{0,4},{1,5},{4,8},{5,9},{6,2},{7,3},{8,12},{9,13},{10,6},{11,7},{1... | collective-permute-start | bytes 1179656 | tf_op jit(solution)/shard_map/ppermute | solution.py:30
  38.3 3.7 %shard_map.58 = (bf16[1248,4096]{1,0:T(8,128)(2,1)S(1)}, f32[1248,384]{1,0:T(8,128)S(1)}) custom-call(bf16[384,4096]{1,0:T(8,128)(2,1)S(1)} %get-tuple-element.126.own, bf16[384,4096]{1,0:T(8,128)(2,1)} %collective-permute-done.9.refs_0_), custom_call_target="tpu_custom_call" | custom-call | flops 1207959552 | bytes 12079595 | tf_op jit(solution)/shard_map/pallas_call | solution.py:58
  42.0 0.0 collective-permute-done.6.refs_0_
  42.0 0.0 collective-permute-done.8.refs_2_
  42.0 0.1 broadcast_select_fusion.6
  42.1 1.6 %collective-permute-start.10 = (bf16[48,4096]{1,0:T(8,128)(2,1)S(1)}, bf16[48,4096]{1,0:T(8,128)(2,1)S(1)}, u32[]{:S(2)}, u32[]{:S(2)}) collective-permute-start(bf16[48,4096]{1,0:T(8,128)(2,1)S(1)} %broadcast_select_fusion.6), channel_id=1, source_target_pairs={{0,1},{1,0},{2,3},{3,2},{4,5},{5,4},{6,7},{7,6},{8,9},{9,8},{10,11... | collective-permute-start | bytes 1179656 | tf_op jit(solution)/shard_map/ppermute | solution.py:30
  43.7 0.1 collective-permute-start.13
  43.8 3.2 %collective-permute-start.14 = (bf16[48,4096]{1,0:T(8,128)(2,1)S(1)}, bf16[48,4096]{1,0:T(8,128)(2,1)S(1)}, u32[]{:S(2)}, u32[]{:S(2)}) collective-permute-start(bf16[48,4096]{1,0:T(8,128)(2,1)S(1)} %collective-permute-done.6.refs_0_), channel_id=1, source_target_pairs={{0,4},{1,5},{4,8},{5,9},{6,2},{7,3},{8,12},{9,13},{10,6},{11,7},{1... | collective-permute-start | bytes 1179656 | tf_op jit(solution)/shard_map/ppermute | solution.py:30
  47.0 2.2 %shard_map.59 = (bf16[1248,4096]{1,0:T(8,128)(2,1)S(1)}, f32[1248,384]{1,0:T(8,128)S(1)}) custom-call(bf16[384,4096]{1,0:T(8,128)(2,1)S(1)} %get-tuple-element.126.own, bf16[48,4096]{1,0:T(8,128)(2,1)} %collective-permute-done.refs_0_, bf16[48,4096]{1,0:T(8,128)(2,1)} %collective-permute-done.2.refs_1_, ...), custom_call_target="tpu_custom_call", output_to_operand_aliasing={{0}: (4, {}), {1}: (5, {})} | custom-call | flops 452984832 | bytes 4529848 | tf_op jit(solution)/shard_map/pallas_call | solution.py:58
  49.3 0.0 collective-permute-done.5.refs_1_
  49.3 0.0 collective-permute-done.10.refs_2_
  49.3 0.4 collective-permute-start.15
  49.7 1.2 %collective-permute-start.11 = (bf16[48,4096]{1,0:T(8,128)(2,1)S(1)}, bf16[48,4096]{1,0:T(8,128)(2,1)S(1)}, u32[]{:S(2)}, u32[]{:S(2)}) collective-permute-start(bf16[48,4096]{1,0:T(8,128)(2,1)S(1)} %slice.29), channel_id=1, source_target_pairs={{0,2},{1,3},{2,0},{3,1},{4,6},{5,7},{6,4},{7,5},{8,10},{9,11},{10,... | collective-permute-start | bytes 1179656 | tf_op jit(solution)/shard_map/ppermute | solution.py:30
  50.9 3.2 %collective-permute-start.12 = (bf16[48,4096]{1,0:T(8,128)(2,1)S(1)}, bf16[48,4096]{1,0:T(8,128)(2,1)S(1)}, u32[]{:S(2)}, u32[]{:S(2)}) collective-permute-start(bf16[48,4096]{1,0:T(8,128)(2,1)S(1)} %collective-permute-done.4.refs_0_), channel_id=1, source_target_pairs={{0,4},{1,5},{4,8},{5,9},{6,2},{7,3},{8,12},{9,13},{10,6},{11,7},{1... | collective-permute-start | bytes 1179656 | tf_op jit(solution)/shard_map/ppermute | solution.py:30
  54.1 2.1 %shard_map.60 = (bf16[1248,4096]{1,0:T(8,128)(2,1)S(1)}, f32[1248,384]{1,0:T(8,128)S(1)}) custom-call(bf16[384,4096]{1,0:T(8,128)(2,1)S(1)} %get-tuple-element.126.own, bf16[48,4096]{1,0:T(8,128)(2,1)} %collective-permute-done.3.refs_0_, bf16[48,4096]{1,0:T(8,128)(2,1)S(1)} %collective-permute-done.7.refs_1_, ...), custom_call_target="tpu_custom_call", output_to_operand_aliasing={{0}: (4, {}), {1}: (5, {})} | custom-call | flops 452984832 | bytes 4529848 | tf_op jit(solution)/shard_map/pallas_call | solution.py:58
  56.2 0.4 collective-permute-done.13.refs_0_
  56.6 1.4 %collective-permute-start.16 = (bf16[48,4096]{1,0:T(8,128)(2,1)S(1)}, bf16[48,4096]{1,0:T(8,128)(2,1)S(1)}, u32[]{:S(2)}, u32[]{:S(2)}) collective-permute-start(bf16[48,4096]{1,0:T(8,128)(2,1)S(1)} %broadcast_select_fusion.4), channel_id=1, source_target_pairs={{0,1},{1,0},{2,3},{3,2},{4,5},{5,4},{6,7},{7,6},{8,9},{9,8},{10,11... | collective-permute-start | bytes 1179656 | tf_op jit(solution)/shard_map/ppermute | solution.py:30
  58.0 1.6 %collective-permute-start.17 = (bf16[48,4096]{1,0:T(8,128)(2,1)S(1)}, bf16[48,4096]{1,0:T(8,128)(2,1)S(1)}, u32[]{:S(2)}, u32[]{:S(2)}) collective-permute-start(bf16[48,4096]{1,0:T(8,128)(2,1)S(1)} %slice.31), channel_id=1, source_target_pairs={{0,2},{1,3},{2,0},{3,1},{4,6},{5,7},{6,4},{7,5},{8,10},{9,11},{10,... | collective-permute-start | bytes 1179656 | tf_op jit(solution)/shard_map/ppermute | solution.py:30
  59.6 3.2 %collective-permute-start.18 = (bf16[48,4096]{1,0:T(8,128)(2,1)S(1)}, bf16[48,4096]{1,0:T(8,128)(2,1)S(1)}, u32[]{:S(2)}, u32[]{:S(2)}) collective-permute-start(bf16[48,4096]{1,0:T(8,128)(2,1)S(1)} %collective-permute-done.13.refs_0_), channel_id=1, source_target_pairs={{0,4},{1,5},{4,8},{5,9},{6,2},{7,3},{8,12},{9,13},{10,6},{11,7},{1... | collective-permute-start | bytes 1179656 | tf_op jit(solution)/shard_map/ppermute | solution.py:30
  62.8 1.1 %shard_map.61 = (bf16[1248,4096]{1,0:T(8,128)(2,1)S(1)}, f32[1248,384]{1,0:T(8,128)S(1)}) custom-call(bf16[384,4096]{1,0:T(8,128)(2,1)S(1)} %get-tuple-element.126.own, bf16[48,4096]{1,0:T(8,128)(2,1)S(1)} %collective-permute-done.1.refs_0_, bf16[48,4096]{1,0:T(8,128)(2,1)S(1)} %collective-permute-done.5.refs_1_, ...), custom_call_target="tpu_custom_call", output_to_operand_aliasing={{0}: (4, {}), {1}: (5, {})} | custom-call | flops 452984832 | bytes 4529848 | tf_op jit(solution)/shard_map/pallas_call | solution.py:58
  63.9 1.1 %collective-permute-done.11.refs_0_ = bf16[48,4096]{1,0:T(8,128)(2,1)S(1)} collective-permute-done((bf16[48,4096]{1,0:T(8,128)(2,1)S(1)}, bf16[48,4096]{1,0:T(8,128)(2,1)S(1)}, u32[]{:S(2)}, u32[]{:S(2)}) %collective-permute-start.11) | collective-permute-done | bytes 393248 | tf_op jit(solution)/shard_map/ppermute | solution.py:30
  65.0 0.0 collective-permute-done.12.refs_1_
  65.0 0.0 collective-permute-done.16.refs_2_
  65.1 1.4 %collective-permute-start.19 = (bf16[48,4096]{1,0:T(8,128)(2,1)S(1)}, bf16[48,4096]{1,0:T(8,128)(2,1)S(1)}, u32[]{:S(2)}, u32[]{:S(2)}) collective-permute-start(bf16[48,4096]{1,0:T(8,128)(2,1)S(1)} %broadcast_select_fusion.3), channel_id=1, source_target_pairs={{0,1},{1,0},{2,3},{3,2},{4,5},{5,4},{6,7},{7,6},{8,9},{9,8},{10,11... | collective-permute-start | bytes 1179656 | tf_op jit(solution)/shard_map/ppermute | solution.py:30
  66.5 3.2 %collective-permute-start.20 = (bf16[48,4096]{1,0:T(8,128)(2,1)S(1)}, bf16[48,4096]{1,0:T(8,128)(2,1)S(1)}, u32[]{:S(2)}, u32[]{:S(2)}) collective-permute-start(bf16[48,4096]{1,0:T(8,128)(2,1)S(1)} %collective-permute-done.11.refs_0_), channel_id=1, source_target_pairs={{0,4},{1,5},{4,8},{5,9},{6,2},{7,3},{8,12},{9,13},{10,6},{11,7},{1... | collective-permute-start | bytes 1179656 | tf_op jit(solution)/shard_map/ppermute | solution.py:30
  69.7 1.1 %shard_map.62 = (bf16[1248,4096]{1,0:T(8,128)(2,1)S(1)}, f32[1248,384]{1,0:T(8,128)S(1)}) custom-call(bf16[384,4096]{1,0:T(8,128)(2,1)S(1)} %get-tuple-element.126.own, bf16[48,4096]{1,0:T(8,128)(2,1)S(1)} %collective-permute-done.6.refs_0_, bf16[48,4096]{1,0:T(8,128)(2,1)S(1)} %collective-permute-done.14.refs_1_, ...), custom_call_target="tpu_custom_call", output_to_operand_aliasing={{0}: (4, {}), {1}: (5, {})} | custom-call | flops 452984832 | bytes 4529848 | tf_op jit(solution)/shard_map/pallas_call | solution.py:58
  70.8 2.7 %collective-permute-done.17.refs_1_ = bf16[48,4096]{1,0:T(8,128)(2,1)S(1)} collective-permute-done((bf16[48,4096]{1,0:T(8,128)(2,1)S(1)}, bf16[48,4096]{1,0:T(8,128)(2,1)S(1)}, u32[]{:S(2)}, u32[]{:S(2)}) %collective-permute-start.17) | collective-permute-done | bytes 393248 | tf_op jit(solution)/shard_map/ppermute | solution.py:30
  73.4 0.0 collective-permute-done.19.refs_2_
  73.5 1.1 %collective-permute-start.22 = (bf16[48,4096]{1,0:T(8,128)(2,1)S(1)}, bf16[48,4096]{1,0:T(8,128)(2,1)S(1)}, u32[]{:S(2)}, u32[]{:S(2)}) collective-permute-start(bf16[48,4096]{1,0:T(8,128)(2,1)S(1)} %broadcast_select_fusion.2), channel_id=1, source_target_pairs={{0,1},{1,0},{2,3},{3,2},{4,5},{5,4},{6,7},{7,6},{8,9},{9,8},{10,11... | collective-permute-start | bytes 1179656 | tf_op jit(solution)/shard_map/ppermute | solution.py:30
  74.6 3.2 %collective-permute-start.21 = (bf16[48,4096]{1,0:T(8,128)(2,1)S(1)}, bf16[48,4096]{1,0:T(8,128)(2,1)S(1)}, u32[]{:S(2)}, u32[]{:S(2)}) collective-permute-start(bf16[48,4096]{1,0:T(8,128)(2,1)S(1)} %collective-permute-done.17.refs_1_), channel_id=1, source_target_pairs={{0,4},{1,5},{4,8},{5,9},{6,2},{7,3},{8,12},{9,13},{10,6},{11,7},{1... | collective-permute-start | bytes 1179656 | tf_op jit(solution)/shard_map/ppermute | solution.py:30
  77.8 2.7 %collective-permute-start.25 = (bf16[384,384]{1,0:T(8,128)(2,1)S(1)}, bf16[384,384]{1,0:T(8,128)(2,1)S(1)}, u32[]{:S(2)}, u32[]{:S(2)}) collective-permute-start(bf16[384,384]{1,0:T(8,128)(2,1)S(1)} %copy-done.10), channel_id=1, source_target_pairs={{0,1},{1,2},{2,3},{3,4},{4,5},{5,6},{6,7},{7,8},{8,9},{9,10},{10,1... | collective-permute-start | bytes 884744 | tf_op jit(solution)/shard_map/ppermute | solution.py:30
  80.6 3.9 %collective-permute-start.26 = (bf16[384,384]{1,0:T(8,128)(2,1)S(1)}, bf16[384,384]{1,0:T(8,128)(2,1)S(1)}, u32[]{:S(2)}, u32[]{:S(2)}) collective-permute-start(bf16[384,384]{1,0:T(8,128)(2,1)S(1)} %copy-done.8), channel_id=1, source_target_pairs={{0,2},{1,3},{2,4},{3,5},{4,6},{5,7},{6,8},{7,9},{8,10},{9,11},{10,... | collective-permute-start | bytes 884744 | tf_op jit(solution)/shard_map/ppermute | solution.py:30
  84.5 1.1 %shard_map.63 = (bf16[1248,4096]{1,0:T(8,128)(2,1)S(1)}, f32[1248,384]{1,0:T(8,128)S(1)}) custom-call(bf16[384,4096]{1,0:T(8,128)(2,1)S(1)} %get-tuple-element.126.own, bf16[48,4096]{1,0:T(8,128)(2,1)S(1)} %collective-permute-done.4.refs_0_, bf16[48,4096]{1,0:T(8,128)(2,1)S(1)} %collective-permute-done.12.refs_1_, ...), custom_call_target="tpu_custom_call", output_to_operand_aliasing={{0}: (4, {}), {1}: (5, {})} | custom-call | flops 452984832 | bytes 4529848 | tf_op jit(solution)/shard_map/pallas_call | solution.py:58
  85.6 0.0 slice-start
  85.7 1.1 %shard_map.64 = (bf16[1248,4096]{1,0:T(8,128)(2,1)S(1)}, f32[1248,384]{1,0:T(8,128)S(1)}) custom-call(bf16[384,4096]{1,0:T(8,128)(2,1)S(1)} %get-tuple-element.126.own, bf16[48,4096]{1,0:T(8,128)(2,1)S(1)} %collective-permute-done.13.refs_0_, bf16[48,4096]{1,0:T(8,128)(2,1)S(1)} %collective-permute-done.18.refs_1_, ...), custom_call_target="tpu_custom_call", output_to_operand_aliasing={{0}: (4, {}), {1}: (5, {})} | custom-call | flops 452984832 | bytes 4529848 | tf_op jit(solution)/shard_map/pallas_call | solution.py:58
  86.8 3.4 %collective-permute-done.21.refs_3_ = bf16[48,4096]{1,0:T(8,128)(2,1)S(1)} collective-permute-done((bf16[48,4096]{1,0:T(8,128)(2,1)S(1)}, bf16[48,4096]{1,0:T(8,128)(2,1)S(1)}, u32[]{:S(2)}, u32[]{:S(2)}) %collective-permute-start.21) | collective-permute-done | bytes 393248 | tf_op jit(solution)/shard_map/ppermute | solution.py:30
  90.2 0.9 collective-permute-start.24
  91.0 0.1 broadcast_select_fusion.1
  91.1 0.1 collective-permute-start.23
  91.2 1.5 %collective-permute-done.26.down1.refs_7_ = bf16[384,384]{1,0:T(8,128)(2,1)S(1)} collective-permute-done((bf16[384,384]{1,0:T(8,128)(2,1)S(1)}, bf16[384,384]{1,0:T(8,128)(2,1)S(1)}, u32[]{:S(2)}, u32[]{:S(2)}) %collective-permute-start.26) | collective-permute-done | bytes 294944 | tf_op jit(solution)/shard_map/ppermute | solution.py:30
  92.7 4.7 %shard_map.65.refs_10_ = f32[384,4096]{1,0:T(8,128)S(1)} custom-call(f32[1248,384]{1,0:T(8,128)S(1)} %get-tuple-element.154.gram, bf16[1248,4096]{1,0:T(8,128)(2,1)S(1)} %get-tuple-element.155.rows, bf16[384,384]{1,0:T(8,128)(2,1)S(1)} %collective-permute-done.25.down0.refs_6_, ...), custom_call_target="tpu_custom_call", output_to_operand_aliasing={{}: (6, {})} | custom-call | flops 3925868544 | bytes 39258684 | tf_op jit(solution)/shard_map/pallas_call | solution.py:58
  97.5 4.2 %shard_map.66 = bf16[384,4096]{1,0:T(8,128)(2,1)} custom-call(bf16[384,4096]{1,0:T(8,128)(2,1)S(1)} %get-tuple-element.126.own, bf16[48,4096]{1,0:T(8,128)(2,1)S(1)} %collective-permute-done.11.refs_0_, bf16[48,4096]{1,0:T(8,128)(2,1)S(1)} %collective-permute-done.17.refs_1_, bf16[48,4096]{1,0:T(8,128)(2,1)S(1)} %collective-permute-done.20.refs_2_, ...), custom_call_target="tpu_custom_call" | custom-call | flops 1811939328 | bytes 18119392 | tf_op jit(solution)/shard_map/pallas_call | solution.py:58
  (47 shorter events, 0.4 us)
Async XLA Ops:
  0.0 5.0 %copy-start.11 = (bf16[384,2,384]{2,1,0:T(2,128)(2,1)S(1)}, bf16[384,2,384]{2,1,0:T(2,128)(2,1)}, u32[]{:S(2)}) copy-start(bf16[384,2,384]{2,1,0:T(2,128)(2,1)} %param.7) | copy-start | bytes 1769476
  0.0 5.2 %copy-start.6 = (s32[1,2]{1,0:T(1,128)S(1)}, s32[1,2]{1,0:T(1,128)}, u32[]{:S(2)}) copy-start(s32[1,2]{1,0:T(1,128)} %couple.1) | copy-start | bytes 28
  0.0 6.0 %copy-start.5 = (bf16[384,384]{1,0:T(8,128)(2,1)S(1)}, bf16[384,384]{1,0:T(8,128)(2,1)}, u32[]{:S(2)}) copy-start(bf16[384,384]{1,0:T(8,128)(2,1)} %kern) | copy-start | bytes 884740
  2.8 32.3 %collective-permute-start.9 = (bf16[384,4096]{1,0:T(8,128)(2,1)S(1)}, bf16[384,4096]{1,0:T(8,128)(2,1)}, u32[]{:S(2)}, u32[]{:S(2)}) collective-permute-start(bf16[384,4096]{1,0:T(8,128)(2,1)S(1)} %get-tuple-element.126.own), channel_id=1, source_target_pairs={{0,1},{1,0},{2,3},{3,2},{4,5},{5,4},{6,7},{7,6},{8,9},{9,8},{10,11... | collective-permute-start | bytes 9437192 | tf_op jit(solution)/shard_map/ppermute | solution.py:30
  3.6 11.0 %collective-permute-start = (bf16[48,4096]{1,0:T(8,128)(2,1)}, bf16[48,4096]{1,0:T(8,128)(2,1)}, u32[]{:S(2)}, u32[]{:S(2)}) collective-permute-start(bf16[48,4096]{1,0:T(8,128)(2,1)} %get-tuple-element.82), channel_id=1, source_target_pairs={{0,2},{1,3},{2,0},{3,1},{4,6},{5,7},{6,4},{7,5},{8,10},{9,11},{10,... | collective-permute-start | bytes 1179656 | tf_op jit(solution)/shard_map/ppermute | solution.py:30
  4.8 18.2 %collective-permute-start.3 = (bf16[48,4096]{1,0:T(8,128)(2,1)}, bf16[48,4096]{1,0:T(8,128)(2,1)}, u32[]{:S(2)}, u32[]{:S(2)}) collective-permute-start(bf16[48,4096]{1,0:T(8,128)(2,1)} %get-tuple-element.89), channel_id=1, source_target_pairs={{0,2},{1,3},{2,0},{3,1},{4,6},{5,7},{6,4},{7,5},{8,10},{9,11},{10,... | collective-permute-start | bytes 1179656 | tf_op jit(solution)/shard_map/ppermute | solution.py:30
  6.0 3.6 %copy-start.1 = (bf16[384,384]{1,0:T(8,128)(2,1)}, bf16[384,384]{1,0:T(8,128)(2,1)S(1)}, u32[]{:S(2)}) copy-start(bf16[384,384]{1,0:T(8,128)(2,1)S(1)} %get-tuple-element.84.up0.refs_8_) | copy-start | bytes 884740
  6.0 3.6 %copy-start.3 = (bf16[384,384]{1,0:T(8,128)(2,1)}, bf16[384,384]{1,0:T(8,128)(2,1)S(1)}, u32[]{:S(2)}) copy-start(bf16[384,384]{1,0:T(8,128)(2,1)S(1)} %get-tuple-element.153.up1.refs_9_) | copy-start | bytes 884740
  6.0 3.6 %copy-start.7 = (bf16[384,384]{1,0:T(8,128)(2,1)}, bf16[384,384]{1,0:T(8,128)(2,1)S(1)}, u32[]{:S(2)}) copy-start(bf16[384,384]{1,0:T(8,128)(2,1)S(1)} %get-tuple-element.152) | copy-start | bytes 884740
  6.0 3.6 %copy-start.9 = (bf16[384,384]{1,0:T(8,128)(2,1)}, bf16[384,384]{1,0:T(8,128)(2,1)S(1)}, u32[]{:S(2)}) copy-start(bf16[384,384]{1,0:T(8,128)(2,1)S(1)} %get-tuple-element.150) | copy-start | bytes 884740
  9.6 2.7 %copy-start = (f32[384,4096]{1,0:T(8,128)}, f32[384,4096]{1,0:T(8,128)S(1)}, u32[]{:S(2)}) copy-start(f32[384,4096]{1,0:T(8,128)S(1)} %shard_map.57.before) | copy-start | bytes 18874372
  15.3 16.0 %collective-permute-start.1 = (bf16[48,4096]{1,0:T(8,128)(2,1)}, bf16[48,4096]{1,0:T(8,128)(2,1)S(1)}, u32[]{:S(2)}, u32[]{:S(2)}) collective-permute-start(bf16[48,4096]{1,0:T(8,128)(2,1)} %slice.26), channel_id=1, source_target_pairs={{0,2},{1,3},{2,0},{3,1},{4,6},{5,7},{6,4},{7,5},{8,10},{9,11},{10,... | collective-permute-start | bytes 1179656 | tf_op jit(solution)/shard_map/ppermute | solution.py:30
  16.6 14.7 %collective-permute-start.2 = (bf16[48,4096]{1,0:T(8,128)(2,1)}, bf16[48,4096]{1,0:T(8,128)(2,1)}, u32[]{:S(2)}, u32[]{:S(2)}) collective-permute-start(bf16[48,4096]{1,0:T(8,128)(2,1)} %collective-permute-done.refs_0_), channel_id=1, source_target_pairs={{0,4},{1,5},{4,8},{5,9},{6,2},{7,3},{8,12},{9,13},{10,6},{11,7},{1... | collective-permute-start | bytes 1179656 | tf_op jit(solution)/shard_map/ppermute | solution.py:30
  23.0 18.9 %collective-permute-start.6 = (bf16[48,4096]{1,0:T(8,128)(2,1)S(1)}, bf16[48,4096]{1,0:T(8,128)(2,1)S(1)}, u32[]{:S(2)}, u32[]{:S(2)}) collective-permute-start(bf16[48,4096]{1,0:T(8,128)(2,1)S(1)} %slice.28), channel_id=1, source_target_pairs={{0,2},{1,3},{2,0},{3,1},{4,6},{5,7},{6,4},{7,5},{8,10},{9,11},{10,... | collective-permute-start | bytes 1179656 | tf_op jit(solution)/shard_map/ppermute | solution.py:30
  24.3 17.7 %collective-permute-start.7 = (bf16[48,4096]{1,0:T(8,128)(2,1)}, bf16[48,4096]{1,0:T(8,128)(2,1)S(1)}, u32[]{:S(2)}, u32[]{:S(2)}) collective-permute-start(bf16[48,4096]{1,0:T(8,128)(2,1)} %collective-permute-done.3.refs_0_), channel_id=1, source_target_pairs={{0,4},{1,5},{4,8},{5,9},{6,2},{7,3},{8,12},{9,13},{10,6},{11,7},{1... | collective-permute-start | bytes 1179656 | tf_op jit(solution)/shard_map/ppermute | solution.py:30
  32.4 9.6 %collective-permute-start.8 = (bf16[48,4096]{1,0:T(8,128)(2,1)S(1)}, bf16[48,4096]{1,0:T(8,128)(2,1)S(1)}, u32[]{:S(2)}, u32[]{:S(2)}) collective-permute-start(bf16[48,4096]{1,0:T(8,128)(2,1)S(1)} %broadcast_select_fusion.7), channel_id=1, source_target_pairs={{0,1},{1,0},{2,3},{3,2},{4,5},{5,4},{6,7},{7,6},{8,9},{9,8},{10,11... | collective-permute-start | bytes 1179656 | tf_op jit(solution)/shard_map/ppermute | solution.py:30
  33.8 15.5 %collective-permute-start.4 = (bf16[48,4096]{1,0:T(8,128)(2,1)S(1)}, bf16[48,4096]{1,0:T(8,128)(2,1)S(1)}, u32[]{:S(2)}, u32[]{:S(2)}) collective-permute-start(bf16[48,4096]{1,0:T(8,128)(2,1)S(1)} %slice.27), channel_id=1, source_target_pairs={{0,2},{1,3},{2,0},{3,1},{4,6},{5,7},{6,4},{7,5},{8,10},{9,11},{10,... | collective-permute-start | bytes 1179656 | tf_op jit(solution)/shard_map/ppermute | solution.py:30
  35.1 14.2 %collective-permute-start.5 = (bf16[48,4096]{1,0:T(8,128)(2,1)S(1)}, bf16[48,4096]{1,0:T(8,128)(2,1)S(1)}, u32[]{:S(2)}, u32[]{:S(2)}) collective-permute-start(bf16[48,4096]{1,0:T(8,128)(2,1)S(1)} %collective-permute-done.1.refs_0_), channel_id=1, source_target_pairs={{0,4},{1,5},{4,8},{5,9},{6,2},{7,3},{8,12},{9,13},{10,6},{11,7},{1... | collective-permute-start | bytes 1179656 | tf_op jit(solution)/shard_map/ppermute | solution.py:30
  42.1 7.2 %collective-permute-start.10 = (bf16[48,4096]{1,0:T(8,128)(2,1)S(1)}, bf16[48,4096]{1,0:T(8,128)(2,1)S(1)}, u32[]{:S(2)}, u32[]{:S(2)}) collective-permute-start(bf16[48,4096]{1,0:T(8,128)(2,1)S(1)} %broadcast_select_fusion.6), channel_id=1, source_target_pairs={{0,1},{1,0},{2,3},{3,2},{4,5},{5,4},{6,7},{7,6},{8,9},{9,8},{10,11... | collective-permute-start | bytes 1179656 | tf_op jit(solution)/shard_map/ppermute | solution.py:30
  43.7 12.9 %collective-permute-start.13 = (bf16[48,4096]{1,0:T(8,128)(2,1)S(1)}, bf16[48,4096]{1,0:T(8,128)(2,1)S(1)}, u32[]{:S(2)}, u32[]{:S(2)}) collective-permute-start(bf16[48,4096]{1,0:T(8,128)(2,1)S(1)} %slice.30), channel_id=1, source_target_pairs={{0,2},{1,3},{2,0},{3,1},{4,6},{5,7},{6,4},{7,5},{8,10},{9,11},{10,... | collective-permute-start | bytes 1179656 | tf_op jit(solution)/shard_map/ppermute | solution.py:30
  43.8 12.8 %collective-permute-start.14 = (bf16[48,4096]{1,0:T(8,128)(2,1)S(1)}, bf16[48,4096]{1,0:T(8,128)(2,1)S(1)}, u32[]{:S(2)}, u32[]{:S(2)}) collective-permute-start(bf16[48,4096]{1,0:T(8,128)(2,1)S(1)} %collective-permute-done.6.refs_0_), channel_id=1, source_target_pairs={{0,4},{1,5},{4,8},{5,9},{6,2},{7,3},{8,12},{9,13},{10,6},{11,7},{1... | collective-permute-start | bytes 1179656 | tf_op jit(solution)/shard_map/ppermute | solution.py:30
  49.3 7.3 %collective-permute-start.15 = (bf16[48,4096]{1,0:T(8,128)(2,1)S(1)}, bf16[48,4096]{1,0:T(8,128)(2,1)S(1)}, u32[]{:S(2)}, u32[]{:S(2)}) collective-permute-start(bf16[48,4096]{1,0:T(8,128)(2,1)S(1)} %broadcast_select_fusion.5), channel_id=1, source_target_pairs={{0,1},{1,0},{2,3},{3,2},{4,5},{5,4},{6,7},{7,6},{8,9},{9,8},{10,11... | collective-permute-start | bytes 1179656 | tf_op jit(solution)/shard_map/ppermute | solution.py:30
  49.7 15.3 %collective-permute-start.11 = (bf16[48,4096]{1,0:T(8,128)(2,1)S(1)}, bf16[48,4096]{1,0:T(8,128)(2,1)S(1)}, u32[]{:S(2)}, u32[]{:S(2)}) collective-permute-start(bf16[48,4096]{1,0:T(8,128)(2,1)S(1)} %slice.29), channel_id=1, source_target_pairs={{0,2},{1,3},{2,0},{3,1},{4,6},{5,7},{6,4},{7,5},{8,10},{9,11},{10,... | collective-permute-start | bytes 1179656 | tf_op jit(solution)/shard_map/ppermute | solution.py:30
  50.9 14.1 %collective-permute-start.12 = (bf16[48,4096]{1,0:T(8,128)(2,1)S(1)}, bf16[48,4096]{1,0:T(8,128)(2,1)S(1)}, u32[]{:S(2)}, u32[]{:S(2)}) collective-permute-start(bf16[48,4096]{1,0:T(8,128)(2,1)S(1)} %collective-permute-done.4.refs_0_), channel_id=1, source_target_pairs={{0,4},{1,5},{4,8},{5,9},{6,2},{7,3},{8,12},{9,13},{10,6},{11,7},{1... | collective-permute-start | bytes 1179656 | tf_op jit(solution)/shard_map/ppermute | solution.py:30
  56.6 8.4 %collective-permute-start.16 = (bf16[48,4096]{1,0:T(8,128)(2,1)S(1)}, bf16[48,4096]{1,0:T(8,128)(2,1)S(1)}, u32[]{:S(2)}, u32[]{:S(2)}) collective-permute-start(bf16[48,4096]{1,0:T(8,128)(2,1)S(1)} %broadcast_select_fusion.4), channel_id=1, source_target_pairs={{0,1},{1,0},{2,3},{3,2},{4,5},{5,4},{6,7},{7,6},{8,9},{9,8},{10,11... | collective-permute-start | bytes 1179656 | tf_op jit(solution)/shard_map/ppermute | solution.py:30
  58.0 15.4 %collective-permute-start.17 = (bf16[48,4096]{1,0:T(8,128)(2,1)S(1)}, bf16[48,4096]{1,0:T(8,128)(2,1)S(1)}, u32[]{:S(2)}, u32[]{:S(2)}) collective-permute-start(bf16[48,4096]{1,0:T(8,128)(2,1)S(1)} %slice.31), channel_id=1, source_target_pairs={{0,2},{1,3},{2,0},{3,1},{4,6},{5,7},{6,4},{7,5},{8,10},{9,11},{10,... | collective-permute-start | bytes 1179656 | tf_op jit(solution)/shard_map/ppermute | solution.py:30
  59.6 13.9 %collective-permute-start.18 = (bf16[48,4096]{1,0:T(8,128)(2,1)S(1)}, bf16[48,4096]{1,0:T(8,128)(2,1)S(1)}, u32[]{:S(2)}, u32[]{:S(2)}) collective-permute-start(bf16[48,4096]{1,0:T(8,128)(2,1)S(1)} %collective-permute-done.13.refs_0_), channel_id=1, source_target_pairs={{0,4},{1,5},{4,8},{5,9},{6,2},{7,3},{8,12},{9,13},{10,6},{11,7},{1... | collective-permute-start | bytes 1179656 | tf_op jit(solution)/shard_map/ppermute | solution.py:30
  65.1 12.7 %copy-start.10 = (bf16[384,384]{1,0:T(8,128)(2,1)S(1)}, bf16[384,384]{1,0:T(8,128)(2,1)}, u32[]{:S(2)}) copy-start(bf16[384,384]{1,0:T(8,128)(2,1)} %copy-done.9) | copy-start | bytes 884740
  65.1 15.5 %copy-start.8 = (bf16[384,384]{1,0:T(8,128)(2,1)S(1)}, bf16[384,384]{1,0:T(8,128)(2,1)}, u32[]{:S(2)}) copy-start(bf16[384,384]{1,0:T(8,128)(2,1)} %copy-done.7) | copy-start | bytes 884740
  65.1 8.4 %collective-permute-start.19 = (bf16[48,4096]{1,0:T(8,128)(2,1)S(1)}, bf16[48,4096]{1,0:T(8,128)(2,1)S(1)}, u32[]{:S(2)}, u32[]{:S(2)}) collective-permute-start(bf16[48,4096]{1,0:T(8,128)(2,1)S(1)} %broadcast_select_fusion.3), channel_id=1, source_target_pairs={{0,1},{1,0},{2,3},{3,2},{4,5},{5,4},{6,7},{7,6},{8,9},{9,8},{10,11... | collective-permute-start | bytes 1179656 | tf_op jit(solution)/shard_map/ppermute | solution.py:30
  66.5 18.0 %collective-permute-start.20 = (bf16[48,4096]{1,0:T(8,128)(2,1)S(1)}, bf16[48,4096]{1,0:T(8,128)(2,1)S(1)}, u32[]{:S(2)}, u32[]{:S(2)}) collective-permute-start(bf16[48,4096]{1,0:T(8,128)(2,1)S(1)} %collective-permute-done.11.refs_0_), channel_id=1, source_target_pairs={{0,4},{1,5},{4,8},{5,9},{6,2},{7,3},{8,12},{9,13},{10,6},{11,7},{1... | collective-permute-start | bytes 1179656 | tf_op jit(solution)/shard_map/ppermute | solution.py:30
  73.5 12.1 %collective-permute-start.22 = (bf16[48,4096]{1,0:T(8,128)(2,1)S(1)}, bf16[48,4096]{1,0:T(8,128)(2,1)S(1)}, u32[]{:S(2)}, u32[]{:S(2)}) collective-permute-start(bf16[48,4096]{1,0:T(8,128)(2,1)S(1)} %broadcast_select_fusion.2), channel_id=1, source_target_pairs={{0,1},{1,0},{2,3},{3,2},{4,5},{5,4},{6,7},{7,6},{8,9},{9,8},{10,11... | collective-permute-start | bytes 1179656 | tf_op jit(solution)/shard_map/ppermute | solution.py:30
  74.6 15.5 %collective-permute-start.21 = (bf16[48,4096]{1,0:T(8,128)(2,1)S(1)}, bf16[48,4096]{1,0:T(8,128)(2,1)S(1)}, u32[]{:S(2)}, u32[]{:S(2)}) collective-permute-start(bf16[48,4096]{1,0:T(8,128)(2,1)S(1)} %collective-permute-done.17.refs_1_), channel_id=1, source_target_pairs={{0,4},{1,5},{4,8},{5,9},{6,2},{7,3},{8,12},{9,13},{10,6},{11,7},{1... | collective-permute-start | bytes 1179656 | tf_op jit(solution)/shard_map/ppermute | solution.py:30
  77.8 13.4 %collective-permute-start.25 = (bf16[384,384]{1,0:T(8,128)(2,1)S(1)}, bf16[384,384]{1,0:T(8,128)(2,1)S(1)}, u32[]{:S(2)}, u32[]{:S(2)}) collective-permute-start(bf16[384,384]{1,0:T(8,128)(2,1)S(1)} %copy-done.10), channel_id=1, source_target_pairs={{0,1},{1,2},{2,3},{3,4},{4,5},{5,6},{6,7},{7,8},{8,9},{9,10},{10,1... | collective-permute-start | bytes 884744 | tf_op jit(solution)/shard_map/ppermute | solution.py:30
  80.6 12.1 %collective-permute-start.26 = (bf16[384,384]{1,0:T(8,128)(2,1)S(1)}, bf16[384,384]{1,0:T(8,128)(2,1)S(1)}, u32[]{:S(2)}, u32[]{:S(2)}) collective-permute-start(bf16[384,384]{1,0:T(8,128)(2,1)S(1)} %copy-done.8), channel_id=1, source_target_pairs={{0,2},{1,3},{2,4},{3,5},{4,6},{5,7},{6,8},{7,9},{8,10},{9,11},{10,... | collective-permute-start | bytes 884744 | tf_op jit(solution)/shard_map/ppermute | solution.py:30
  85.6 7.1 %slice-start = ((s8[6291456]{0:T(1024)(128)(4,1)}), s8[4194304]{0:T(1024)(128)(4,1)S(1)}, s32[]{:S(2)}) async-start(s8[6291456]{0:T(1024)(128)(4,1)} %bitcast.5), calls=%async_computation | async-start | bytes 8388608
  85.6 7.1 %slice-start.1 = ((s8[6291456]{0:T(1024)(128)(4,1)}), s8[2097152]{0:T(1024)(128)(4,1)S(1)}, s32[]{:S(2)}) async-start(s8[6291456]{0:T(1024)(128)(4,1)} %bitcast.5), calls=%async_computation.1 | async-start | bytes 4194304
  85.6 7.0 %copy-start.2 = (bf16[384,384]{1,0:T(8,128)(2,1)S(1)}, bf16[384,384]{1,0:T(8,128)(2,1)}, u32[]{:S(2)}) copy-start(bf16[384,384]{1,0:T(8,128)(2,1)} %copy-done.1) | copy-start | bytes 884740
  85.7 7.0 %copy-start.4 = (bf16[384,384]{1,0:T(8,128)(2,1)S(1)}, bf16[384,384]{1,0:T(8,128)(2,1)}, u32[]{:S(2)}) copy-start(bf16[384,384]{1,0:T(8,128)(2,1)} %copy-done.3) | copy-start | bytes 884740
  90.2 7.3 %collective-permute-start.24 = (bf16[48,4096]{1,0:T(8,128)(2,1)S(1)}, bf16[48,4096]{1,0:T(8,128)(2,1)S(1)}, u32[]{:S(2)}, u32[]{:S(2)}) collective-permute-start(bf16[48,4096]{1,0:T(8,128)(2,1)S(1)} %broadcast_select_fusion), channel_id=1, source_target_pairs={{0,1},{1,0},{2,3},{3,2},{4,5},{5,4},{6,7},{7,6},{8,9},{9,8},{10,11... | collective-permute-start | bytes 1179656 | tf_op jit(solution)/shard_map/ppermute | solution.py:30
  91.1 6.4 %collective-permute-start.23 = (bf16[48,4096]{1,0:T(8,128)(2,1)S(1)}, bf16[48,4096]{1,0:T(8,128)(2,1)S(1)}, u32[]{:S(2)}, u32[]{:S(2)}) collective-permute-start(bf16[48,4096]{1,0:T(8,128)(2,1)S(1)} %broadcast_select_fusion.1), channel_id=1, source_target_pairs={{0,1},{1,0},{2,3},{3,2},{4,5},{5,4},{6,7},{7,6},{8,9},{9,8},{10,11... | collective-permute-start | bytes 1179656 | tf_op jit(solution)/shard_map/ppermute | solution.py:30
